TPU v7x, 512 devices: a whole 4x4x16 slice. The times are simulated.
512 devices in a mesh: band: 8 (over y, z_hi), dom: 64 (over z_lo, x, core).
Axes of the slice: x: 4, y: 4, z: 16 (z_hi: 2, z_lo: 8; z = z_hi * 8 + z_lo), core: 2. Of those that a mesh axis runs over, the one named last changes fastest.
Arguments:
- orbitals: float32 [64, 64, 16, 16, 128], P('band', 'dom'), may hold values from -40 to 40
- potential: float32 [64, 16, 16, 128], P('dom'), may hold values from 0.2 to 4
Outputs:
- rotated: float32 [64, 64, 16, 16, 128], P('band', 'dom')
All inputs are finite; a program needn't handle non-finite values.
Results may differ from a plain program's by a relative error of at most 0.0003.
Values sent between devices are 32-bit elements; how exact they have to be, the bound alone decides.
No kernel may reach another device: no remote copies, remote signals or barrier semaphores. Data moves between devices by JAX's collectives and lax.ppermute only.
A program may use at most 64 MiB of HBM per device.

v0:
```python
import jax
import jax.numpy as jnp
from jax import lax
from jax.sharding import PartitionSpec as P

DEGREE = 4
PY = 8


STENCIL = (-205.0 / 72.0, 8.0 / 5.0, -1.0 / 5.0, 8.0 / 315.0, -1.0 / 560.0)
FILTER_LOW = 1.5
FILTER_HIGH = 14.0


def from_behind(block, axis, distance):
    devices = range(lax.axis_size(axis))
    route = [(i - distance, i) for i in devices if i - distance in devices]
    return lax.ppermute(block, axis, route)


def from_neighbour(rim, offset):
    return from_behind(rim, "dom", offset)


def hamiltonian(grid_field, potential, keep_low, keep_high):
    plane_count = grid_field.shape[1]
    row_count = grid_field.shape[2]
    layer_count = grid_field.shape[3]
    lower_rim = from_neighbour(grid_field[:, plane_count - 4 :], PY)
    upper_rim = from_neighbour(grid_field[:, :4], -PY)
    front_rim = from_neighbour(grid_field[:, :, row_count - 4 :], 1) * keep_low
    back_rim = from_neighbour(grid_field[:, :, :4], -1) * keep_high
    first_padded = jnp.concatenate((lower_rim, grid_field, upper_rim), axis=1)
    second_padded = jnp.concatenate((front_rim, grid_field, back_rim), axis=2)
    third_padded = jnp.pad(grid_field, ((0, 0), (0, 0), (0, 0), (4, 4)))
    laplace = 3.0 * STENCIL[0] * grid_field
    for shift_by in range(1, 5):
        laplace = laplace + STENCIL[shift_by] * (
            first_padded[:, 4 + shift_by : 4 + shift_by + plane_count]
            + first_padded[:, 4 - shift_by : 4 - shift_by + plane_count]
        )
        laplace = laplace + STENCIL[shift_by] * (
            second_padded[:, :, 4 + shift_by : 4 + shift_by + row_count]
            + second_padded[:, :, 4 - shift_by : 4 - shift_by + row_count]
        )
        laplace = laplace + STENCIL[shift_by] * (
            third_padded[:, :, :, 4 + shift_by : 4 + shift_by + layer_count]
            + third_padded[:, :, :, 4 - shift_by : 4 - shift_by + layer_count]
        )
    return -0.5 * laplace + potential[None] * grid_field


def orthonormal(gram):
    factor = jnp.linalg.cholesky(gram)
    return lax.linalg.triangular_solve(
        factor, jnp.eye(gram.shape[0], dtype=gram.dtype), left_side=True, lower=True
    )


def on_device(orbitals, potential):
    local_orbitals = orbitals[:, 0]
    local_potential = potential[0]
    column_index = lax.axis_index("dom") % PY
    keep_low = (column_index != 0).astype(jnp.float32)
    keep_high = (column_index != PY - 1).astype(jnp.float32)
    middle = 0.5 * (FILTER_HIGH + FILTER_LOW)
    radius = 0.5 * (FILTER_HIGH - FILTER_LOW)
    earlier = local_orbitals
    current = (
        hamiltonian(local_orbitals, local_potential, keep_low, keep_high) - middle * local_orbitals
    ) / radius
    for degree_step in range(DEGREE - 1):
        following = (
            2.0
            * (hamiltonian(current, local_potential, keep_low, keep_high) - middle * current)
            / radius
            - earlier
        )
        earlier = current
        current = following
    per_group = local_orbitals.shape[0]
    cell_count = (
        local_orbitals.shape[1]
        * local_orbitals.shape[2]
        * local_orbitals.shape[3]
        * lax.axis_size("dom")
    )
    flattened = current.reshape(per_group, -1)
    gathered = lax.all_gather(flattened, "band", axis=0, tiled=True)
    gram_rows = jnp.dot(flattened, gathered.T, precision=lax.Precision.HIGHEST)
    offset = lax.axis_index("band") * per_group
    summed_rows = lax.psum(gram_rows, "dom")
    gram = lax.all_gather(summed_rows, "band", axis=0, tiled=True)
    inverse = orthonormal(gram / cell_count)
    own_rows = lax.dynamic_slice_in_dim(inverse, offset, per_group, 0)
    rotated = jnp.dot(own_rows, gathered, precision=lax.Precision.HIGHEST)
    return rotated.reshape(orbitals.shape)


def solution(mesh):
    placed = (P("band", "dom", None, None, None), P("dom", None, None, None))
    return jax.shard_map(
        on_device,
        mesh=mesh,
        in_specs=placed,
        out_specs=P("band", "dom", None, None, None),
        check_vma=False,
    )
```

profile of v0, /device:TPU:1, one launch (start us, length us, event | category | flops | bytes accessed | tf_op | source)
XLA Modules:
  0.0 691.6 jit_solution(9254253498566232592)
XLA Ops:
  7.9 8.8 %collective-permute-start.2 = (f32[8,16,4,128]{3,2,1,0:T(4,128)S(1)}, f32[8,16,4,128]{3,2,1,0:T(4,128)S(1)}, u32[]{:S(2)}, u32[]{:S(2)}) collective-permute-start(f32[8,16,4,128]{3,2,1,0:T(4,128)S(1)} %get-tuple-element.21), channel_id=1, source_target_pairs={{1,0},{2,1},{3,2},{4,3},{5,4},{6,5},{7,6},{8,7},{9,8},{10,9},{11,1... | collective-permute-start | bytes 786440 | tf_op jit(solution)/shard_map/ppermute | solution.py:18
  21.0 4.0 collective-permute-start.1
  25.2 3.8 collective-permute-done
  29.9 3.1 broadcast_multiply_fusion
  33.0 3.6 collective-permute-start.6
  40.0 4.7 collective-permute-start.5
  44.8 4.3 collective-permute-done.4
  50.0 3.1 fusion.71
  53.2 3.2 collective-permute-start.10
  60.2 4.7 collective-permute-start.9
  65.0 4.6 collective-permute-done.8
  70.6 3.1 fusion.42
  73.8 2.7 collective-permute-start.14
  76.5 2.8 collective-permute-start.15
  80.7 4.7 collective-permute-start.13
  85.6 4.4 collective-permute-done.12
  91.5 3.1 fusion.13
  96.2 288.0 %all-gather.2.cloned.1.call-done = f32[64,32768]{1,0:T(8,128)} async-done(((f32[8,32768]{1,0:T(8,128)}), f32[64,32768]{1,0:T(8,128)}) %all-gather.2.cloned.1.call-update) | async-done | bytes 8388624 | tf_op jit(solution)/shard_map/all_gather | solution.py:89
  384.3 9.0 %fusion.217 = f32[8,64]{1,0:T(8,128)S(1)} fusion(f32[64,32768]{1,0:T(8,128)} %all-gather.2.cloned.1.call-done, f32[1,8,256,128]{3,2,1,0:T(8,128)S(1)} %bitcast.39), kind=kOutput, calls=%fused_computation.379 | convolution fusion | flops 201326592 | bytes 9439232 | tf_op jit(solution)/shard_map/dot_general | solution.py:90
  393.3 214.3 %psum.7 = f32[8,64]{1,0:T(8,128)S(1)} all-reduce(f32[8,64]{1,0:T(8,128)S(1)} %fusion.217), channel_id=1, replica_groups=mesh['band'=8,'dom'=64] {'dom'}, use_global_device_ids=true, to_apply=%region_0.1 | all-reduce | flops 512 | bytes 4096 | tf_op jit(solution)/shard_map/psum | solution.py:92
  607.6 57.1 %all_gather.7 = f32[64,64]{1,0:T(8,128)S(1)} all-gather(f32[8,64]{1,0:T(8,128)S(1)} %psum.7), channel_id=1, replica_groups=mesh['band'=8,'dom'=64] {'band'}, dimensions={0}, use_global_device_ids=true | all-gather | bytes 18432 | tf_op jit(solution)/shard_map/all_gather | solution.py:93
  664.9 5.8 cholesky.17
  672.1 4.9 custom-call.6
  677.2 6.4 fusion.214
  (52 shorter events, 23.3 us)
Async XLA Ops:
  6.5 377.7 %all-gather.2.cloned.1.call-start = ((), (), s32[]{:S(2)}) async-start(), calls=%async_computation | async-start | bytes 9437184 | tf_op jit(solution)/shard_map/all_gather | solution.py:89
  6.5 23.3 %copy-start = (f32[8,1,16,16,128]{4,3,2,1,0:T(8,128)S(1)}, f32[8,1,16,16,128]{4,3,2,1,0:T(8,128)}, u32[]{:S(2)}) copy-start(f32[8,1,16,16,128]{4,3,2,1,0:T(8,128)} %param.2) | copy-start | bytes 3145732
  6.5 23.3 %copy-start.1 = (f32[1,16,16,128]{3,2,1,0:T(8,128)S(1)}, f32[1,16,16,128]{3,2,1,0:T(8,128)}, u32[]{:S(2)}) copy-start(f32[1,16,16,128]{3,2,1,0:T(8,128)} %param.3) | copy-start | bytes 393220
  7.9 17.1 %collective-permute-start.2 = (f32[8,16,4,128]{3,2,1,0:T(4,128)S(1)}, f32[8,16,4,128]{3,2,1,0:T(4,128)S(1)}, u32[]{:S(2)}, u32[]{:S(2)}) collective-permute-start(f32[8,16,4,128]{3,2,1,0:T(4,128)S(1)} %get-tuple-element.21), channel_id=1, source_target_pairs={{1,0},{2,1},{3,2},{4,3},{5,4},{6,5},{7,6},{8,7},{9,8},{10,9},{11,1... | collective-permute-start | bytes 786440 | tf_op jit(solution)/shard_map/ppermute | solution.py:18
  16.7 8.4 %collective-permute-start.3 = (f32[8,16,4,128]{3,2,1,0:T(4,128)S(1)}, f32[8,16,4,128]{3,2,1,0:T(4,128)S(1)}, u32[]{:S(2)}, u32[]{:S(2)}) collective-permute-start(f32[8,16,4,128]{3,2,1,0:T(4,128)S(1)} %get-tuple-element.22), channel_id=1, source_target_pairs={{0,1},{1,2},{2,3},{3,4},{4,5},{5,6},{6,7},{7,8},{8,9},{9,10},{10,1... | collective-permute-start | bytes 786440 | tf_op jit(solution)/shard_map/ppermute | solution.py:18
  19.7 9.3 %collective-permute-start = (f32[8,4,16,128]{3,2,1,0:T(8,128)S(1)}, f32[8,4,16,128]{3,2,1,0:T(8,128)S(1)}, u32[]{:S(2)}, u32[]{:S(2)}) collective-permute-start(f32[8,4,16,128]{3,2,1,0:T(8,128)S(1)} %get-tuple-element.19), channel_id=1, source_target_pairs={{8,0},{9,1},{10,2},{11,3},{12,4},{13,5},{14,6},{15,7},{16,8},{17,9... | collective-permute-start | bytes 786440 | tf_op jit(solution)/shard_map/ppermute | solution.py:18
  21.0 8.8 %collective-permute-start.1 = (f32[8,4,16,128]{3,2,1,0:T(8,128)S(1)}, f32[8,4,16,128]{3,2,1,0:T(8,128)S(1)}, u32[]{:S(2)}, u32[]{:S(2)}) collective-permute-start(f32[8,4,16,128]{3,2,1,0:T(8,128)S(1)} %get-tuple-element.20), channel_id=1, source_target_pairs={{0,8},{1,9},{2,10},{3,11},{4,12},{5,13},{6,14},{7,15},{8,16},{9,17... | collective-permute-start | bytes 786440 | tf_op jit(solution)/shard_map/ppermute | solution.py:18
  33.0 11.7 %collective-permute-start.6 = (f32[8,16,4,128]{3,2,1,0:T(4,128)S(1)}, f32[8,16,4,128]{3,2,1,0:T(4,128)S(1)}, u32[]{:S(2)}, u32[]{:S(2)}) collective-permute-start(f32[8,16,4,128]{3,2,1,0:T(4,128)S(1)} %get-tuple-element.15), channel_id=1, source_target_pairs={{1,0},{2,1},{3,2},{4,3},{5,4},{6,5},{7,6},{8,7},{9,8},{10,9},{11,1... | collective-permute-start | bytes 786440 | tf_op jit(solution)/shard_map/ppermute | solution.py:18
  36.7 8.1 %collective-permute-start.7 = (f32[8,16,4,128]{3,2,1,0:T(4,128)S(1)}, f32[8,16,4,128]{3,2,1,0:T(4,128)S(1)}, u32[]{:S(2)}, u32[]{:S(2)}) collective-permute-start(f32[8,16,4,128]{3,2,1,0:T(4,128)S(1)} %get-tuple-element.16), channel_id=1, source_target_pairs={{0,1},{1,2},{2,3},{3,4},{4,5},{5,6},{6,7},{7,8},{8,9},{9,10},{10,1... | collective-permute-start | bytes 786440 | tf_op jit(solution)/shard_map/ppermute | solution.py:18
  38.7 10.4 %collective-permute-start.4 = (f32[8,4,16,128]{3,2,1,0:T(8,128)S(1)}, f32[8,4,16,128]{3,2,1,0:T(8,128)S(1)}, u32[]{:S(2)}, u32[]{:S(2)}) collective-permute-start(f32[8,4,16,128]{3,2,1,0:T(8,128)S(1)} %get-tuple-element.17), channel_id=1, source_target_pairs={{8,0},{9,1},{10,2},{11,3},{12,4},{13,5},{14,6},{15,7},{16,8},{17,9... | collective-permute-start | bytes 786440 | tf_op jit(solution)/shard_map/ppermute | solution.py:18
  40.0 10.0 %collective-permute-start.5 = (f32[8,4,16,128]{3,2,1,0:T(8,128)S(1)}, f32[8,4,16,128]{3,2,1,0:T(8,128)S(1)}, u32[]{:S(2)}, u32[]{:S(2)}) collective-permute-start(f32[8,4,16,128]{3,2,1,0:T(8,128)S(1)} %get-tuple-element.18), channel_id=1, source_target_pairs={{0,8},{1,9},{2,10},{3,11},{4,12},{5,13},{6,14},{7,15},{8,16},{9,17... | collective-permute-start | bytes 786440 | tf_op jit(solution)/shard_map/ppermute | solution.py:18
  53.2 11.7 %collective-permute-start.10 = (f32[8,16,4,128]{3,2,1,0:T(4,128)S(1)}, f32[8,16,4,128]{3,2,1,0:T(4,128)S(1)}, u32[]{:S(2)}, u32[]{:S(2)}) collective-permute-start(f32[8,16,4,128]{3,2,1,0:T(4,128)S(1)} %get-tuple-element.11), channel_id=1, source_target_pairs={{1,0},{2,1},{3,2},{4,3},{5,4},{6,5},{7,6},{8,7},{9,8},{10,9},{11,1... | collective-permute-start | bytes 786440 | tf_op jit(solution)/shard_map/ppermute | solution.py:18
  56.4 8.5 %collective-permute-start.11 = (f32[8,16,4,128]{3,2,1,0:T(4,128)S(1)}, f32[8,16,4,128]{3,2,1,0:T(4,128)S(1)}, u32[]{:S(2)}, u32[]{:S(2)}) collective-permute-start(f32[8,16,4,128]{3,2,1,0:T(4,128)S(1)} %get-tuple-element.12), channel_id=1, source_target_pairs={{0,1},{1,2},{2,3},{3,4},{4,5},{5,6},{6,7},{7,8},{8,9},{9,10},{10,1... | collective-permute-start | bytes 786440 | tf_op jit(solution)/shard_map/ppermute | solution.py:18
  58.9 10.7 %collective-permute-start.8 = (f32[8,4,16,128]{3,2,1,0:T(8,128)S(1)}, f32[8,4,16,128]{3,2,1,0:T(8,128)S(1)}, u32[]{:S(2)}, u32[]{:S(2)}) collective-permute-start(f32[8,4,16,128]{3,2,1,0:T(8,128)S(1)} %get-tuple-element.13), channel_id=1, source_target_pairs={{8,0},{9,1},{10,2},{11,3},{12,4},{13,5},{14,6},{15,7},{16,8},{17,9... | collective-permute-start | bytes 786440 | tf_op jit(solution)/shard_map/ppermute | solution.py:18
  60.2 10.4 %collective-permute-start.9 = (f32[8,4,16,128]{3,2,1,0:T(8,128)S(1)}, f32[8,4,16,128]{3,2,1,0:T(8,128)S(1)}, u32[]{:S(2)}, u32[]{:S(2)}) collective-permute-start(f32[8,4,16,128]{3,2,1,0:T(8,128)S(1)} %get-tuple-element.14), channel_id=1, source_target_pairs={{0,8},{1,9},{2,10},{3,11},{4,12},{5,13},{6,14},{7,15},{8,16},{9,17... | collective-permute-start | bytes 786440 | tf_op jit(solution)/shard_map/ppermute | solution.py:18
  73.8 11.7 %collective-permute-start.14 = (f32[8,16,4,128]{3,2,1,0:T(4,128)S(1)}, f32[8,16,4,128]{3,2,1,0:T(4,128)S(1)}, u32[]{:S(2)}, u32[]{:S(2)}) collective-permute-start(f32[8,16,4,128]{3,2,1,0:T(4,128)S(1)} %get-tuple-element.7), channel_id=1, source_target_pairs={{1,0},{2,1},{3,2},{4,3},{5,4},{6,5},{7,6},{8,7},{9,8},{10,9},{11,1... | collective-permute-start | bytes 786440 | tf_op jit(solution)/shard_map/ppermute | solution.py:18
  76.5 9.0 %collective-permute-start.15 = (f32[8,16,4,128]{3,2,1,0:T(4,128)S(1)}, f32[8,16,4,128]{3,2,1,0:T(4,128)S(1)}, u32[]{:S(2)}, u32[]{:S(2)}) collective-permute-start(f32[8,16,4,128]{3,2,1,0:T(4,128)S(1)} %get-tuple-element.8), channel_id=1, source_target_pairs={{0,1},{1,2},{2,3},{3,4},{4,5},{5,6},{6,7},{7,8},{8,9},{9,10},{10,1... | collective-permute-start | bytes 786440 | tf_op jit(solution)/shard_map/ppermute | solution.py:18
  79.4 10.5 %collective-permute-start.12 = (f32[8,4,16,128]{3,2,1,0:T(8,128)S(1)}, f32[8,4,16,128]{3,2,1,0:T(8,128)S(1)}, u32[]{:S(2)}, u32[]{:S(2)}) collective-permute-start(f32[8,4,16,128]{3,2,1,0:T(8,128)S(1)} %get-tuple-element.9), channel_id=1, source_target_pairs={{8,0},{9,1},{10,2},{11,3},{12,4},{13,5},{14,6},{15,7},{16,8},{17,9... | collective-permute-start | bytes 786440 | tf_op jit(solution)/shard_map/ppermute | solution.py:18
  80.7 10.8 %collective-permute-start.13 = (f32[8,4,16,128]{3,2,1,0:T(8,128)S(1)}, f32[8,4,16,128]{3,2,1,0:T(8,128)S(1)}, u32[]{:S(2)}, u32[]{:S(2)}) collective-permute-start(f32[8,4,16,128]{3,2,1,0:T(8,128)S(1)} %get-tuple-element.10), channel_id=1, source_target_pairs={{0,8},{1,9},{2,10},{3,11},{4,12},{5,13},{6,14},{7,15},{8,16},{9,17... | collective-permute-start | bytes 786440 | tf_op jit(solution)/shard_map/ppermute | solution.py:18
Sparse Core Ops, SparseCore 0:
  96.4 287.8 all-gather.1
where the time goes:
time: 704 us; the launch traced here: 692 us
  waiting for transfers between devices  309 us (44%)
  blocking collectives  271 us (38%)
  starting transfers between devices  50.8 us (7%)
  other arithmetic  24.7 us (4%)
  matrix products  15.6 us (2%)
  between operations  13.8 us (2%)
    all_gather x1, waiting for transfers between devices, on_device(): gathered = lax.all_gather(flattened, 'band', axis=0, tiled=True)  288 us
    psum x1, blocking collectives, on_device(): summed_rows = lax.psum(gram_rows, 'dom')  214 us
    all_gather x1, blocking collectives, on_device(): gram = lax.all_gather(summed_rows, 'band', axis=0, tiled=True)  57.1 us
    ppermute x16, starting transfers between devices, from_behind(): return lax.ppermute(block, axis, route)  50.8 us
    ppermute x16, waiting for transfers between devices, from_behind(): return lax.ppermute(block, axis, route)  21.4 us
  transfers between devices with their start and end apart: 17, of which 9 were waited for; matrix products, arithmetic and copies ran while one was open for 0% of the time, Pallas kernels for 0%

commit v1 on v0

--- a/solution.py
+++ b/solution.py
@@ -57,6 +57,17 @@
     )
 
 
+def spread(row, axis):
+    copies = jnp.broadcast_to(row[None], (lax.axis_size(axis),) + row.shape)
+    return lax.all_to_all(copies, axis, 0, 0, tiled=True)
+
+
+def summed_everywhere(gram):
+    row = lax.all_to_all(gram[:, None], "dom", 0, 0, tiled=True).sum(axis=0)
+    row = spread(row, "band").sum(axis=0)
+    return spread(row, "dom")[:, 0]
+
+
 def on_device(orbitals, potential):
     local_orbitals = orbitals[:, 0]
     local_potential = potential[0]
@@ -78,22 +89,21 @@
         )
         earlier = current
         current = following
-    per_group = local_orbitals.shape[0]
     cell_count = (
         local_orbitals.shape[1]
         * local_orbitals.shape[2]
         * local_orbitals.shape[3]
         * lax.axis_size("dom")
     )
-    flattened = current.reshape(per_group, -1)
-    gathered = lax.all_gather(flattened, "band", axis=0, tiled=True)
-    gram_rows = jnp.dot(flattened, gathered.T, precision=lax.Precision.HIGHEST)
-    offset = lax.axis_index("band") * per_group
-    summed_rows = lax.psum(gram_rows, "dom")
-    gram = lax.all_gather(summed_rows, "band", axis=0, tiled=True)
+    layers = local_orbitals.shape[3]
+    rows = current.reshape(local_orbitals.shape[0], -1, layers)
+    share = lax.all_to_all(rows, "band", 1, 0, tiled=True)
+    bands = share.shape[0]
+    share = share.reshape(bands, -1)
+    gram = summed_everywhere(jnp.dot(share, share.T, precision=lax.Precision.HIGHEST))
     inverse = orthonormal(gram / cell_count)
-    own_rows = lax.dynamic_slice_in_dim(inverse, offset, per_group, 0)
-    rotated = jnp.dot(own_rows, gathered, precision=lax.Precision.HIGHEST)
+    rotated = jnp.dot(inverse, share, precision=lax.Precision.HIGHEST)
+    rotated = lax.all_to_all(rotated.reshape(bands, -1, layers), "band", 0, 1, tiled=True)
     return rotated.reshape(orbitals.shape)
 
 

time: 704 us -> 296 us (0.42)
  the two profiles are of different devices: /device:TPU:1 before, /device:TPU:33 now
where the time goes in v1:
time: 296 us
  blocking collectives  192 us (65%)
  starting transfers between devices  46.2 us (16%)
  waiting for transfers between devices  25.9 us (9%)
  other arithmetic  24.8 us (8%)
  local copies, waits for them, and re-layouts  4.35 us (1%)
    all_to_all x1, blocking collectives, on_device(): lax.all_to_all(rotated.reshape(bands, -1, layers), 'band', 0, 1, tiled=True)  60.9 us
    all_to_all x1, blocking collectives, on_device(): share = lax.all_to_all(rows, 'band', 1, 0, tiled=True)  48.4 us
    ppermute x16, starting transfers between devices, from_behind(): return lax.ppermute(block, axis, route)  46.2 us
    all_to_all x1, blocking collectives, summed_everywhere(): row = lax.all_to_all(gram[:, None], 'dom', 0, 0, tiled=True).sum(axis=0)  46.1 us
    all_to_all x2, blocking collectives, spread(): return lax.all_to_all(copies, axis, 0, 0, tiled=True)  36.2 us
    ppermute x16, waiting for transfers between devices, from_behind(): return lax.ppermute(block, axis, route)  25.9 us
    sub x3, other arithmetic, on_device(): 2.0 * (hamiltonian(current, local_potential, keep_low, keep_high) - middl...  9.36 us
    another operation x3, other arithmetic, orthonormal(): factor = jnp.linalg.cholesky(gram)  6.52 us
  transfers between devices with their start and end apart: 16, of which 8 were waited for; matrix products, arithmetic and copies ran while one was open for 0% of the time, Pallas kernels for 0%

profile of v1, /device:TPU:33, one launch (start us, length us, event | category | flops | bytes accessed | tf_op | source)
XLA Modules:
  0.0 295.5 jit_solution(6860267920127340318)
XLA Ops:
  4.0 3.1 %collective-permute-start.3 = (f32[8,16,4,128]{3,2,1,0:T(4,128)S(1)}, f32[8,16,4,128]{3,2,1,0:T(4,128)S(1)}, u32[]{:S(2)}, u32[]{:S(2)}) collective-permute-start(f32[8,16,4,128]{3,2,1,0:T(4,128)S(1)} %get-tuple-element.22), channel_id=1, source_target_pairs={{0,1},{1,2},{2,3},{3,4},{4,5},{5,6},{6,7},{7,8},{8,9},{9,10},{10,1... | collective-permute-start | bytes 786440 | tf_op jit(solution)/shard_map/ppermute | solution.py:18
  7.2 6.0 %collective-permute-start = (f32[8,4,16,128]{3,2,1,0:T(8,128)S(1)}, f32[8,4,16,128]{3,2,1,0:T(8,128)S(1)}, u32[]{:S(2)}, u32[]{:S(2)}) collective-permute-start(f32[8,4,16,128]{3,2,1,0:T(8,128)S(1)} %get-tuple-element.19), channel_id=1, source_target_pairs={{8,0},{9,1},{10,2},{11,3},{12,4},{13,5},{14,6},{15,7},{16,8},{17,9... | collective-permute-start | bytes 786440 | tf_op jit(solution)/shard_map/ppermute | solution.py:18
  15.3 3.1 %collective-permute-done = f32[8,4,16,128]{3,2,1,0:T(8,128)S(1)} collective-permute-done((f32[8,4,16,128]{3,2,1,0:T(8,128)S(1)}, f32[8,4,16,128]{3,2,1,0:T(8,128)S(1)}, u32[]{:S(2)}, u32[]{:S(2)}) %collective-permute-start) | collective-permute-done | bytes 262176 | tf_op jit(solution)/shard_map/ppermute | solution.py:18
  18.4 3.8 %collective-permute-done.1 = f32[8,4,16,128]{3,2,1,0:T(8,128)S(1)} collective-permute-done((f32[8,4,16,128]{3,2,1,0:T(8,128)S(1)}, f32[8,4,16,128]{3,2,1,0:T(8,128)S(1)}, u32[]{:S(2)}, u32[]{:S(2)}) %collective-permute-start.1) | collective-permute-done | bytes 262176 | tf_op jit(solution)/shard_map/ppermute | solution.py:18
  22.2 3.1 %broadcast_multiply_fusion = (f32[8,16,16,128]{3,2,1,0:T(8,128)S(1)}, f32[8,16,16,128]{3,2,1,0:T(8,128)S(1)}) fusion(f32[8,16,16,128]{3,2,1,0:T(8,128)S(1)} %bitcast.61, f32[16,16,128]{2,1,0:T(8,128)S(1)} %bitcast.64, f32[8,16,4,128]{3,2,1,0:T(4,128)S(1)} %bitcast.71, f32[8,16,4,128]{3,2,1,0:T(4,128)S(1)} %bitcast.68, ...), kind=kLoop, calls=%fused_computation.358 | loop fusion | flops 15466496 | bytes 4325376 | tf_op jit(solution)/shard_map/div | solution.py:80
  25.4 3.6 %collective-permute-start.6 = (f32[8,16,4,128]{3,2,1,0:T(4,128)S(1)}, f32[8,16,4,128]{3,2,1,0:T(4,128)S(1)}, u32[]{:S(2)}, u32[]{:S(2)}) collective-permute-start(f32[8,16,4,128]{3,2,1,0:T(4,128)S(1)} %get-tuple-element.15), channel_id=1, source_target_pairs={{1,0},{2,1},{3,2},{4,3},{5,4},{6,5},{7,6},{8,7},{9,8},{10,9},{11,1... | collective-permute-start | bytes 786440 | tf_op jit(solution)/shard_map/ppermute | solution.py:18
  32.9 3.4 %collective-permute-start.5 = (f32[8,4,16,128]{3,2,1,0:T(8,128)S(1)}, f32[8,4,16,128]{3,2,1,0:T(8,128)S(1)}, u32[]{:S(2)}, u32[]{:S(2)}) collective-permute-start(f32[8,4,16,128]{3,2,1,0:T(8,128)S(1)} %get-tuple-element.18), channel_id=1, source_target_pairs={{0,8},{1,9},{2,10},{3,11},{4,12},{5,13},{6,14},{7,15},{8,16},{9,17... | collective-permute-start | bytes 786440 | tf_op jit(solution)/shard_map/ppermute | solution.py:18
  36.4 4.0 %collective-permute-done.4 = f32[8,4,16,128]{3,2,1,0:T(8,128)S(1)} collective-permute-done((f32[8,4,16,128]{3,2,1,0:T(8,128)S(1)}, f32[8,4,16,128]{3,2,1,0:T(8,128)S(1)}, u32[]{:S(2)}, u32[]{:S(2)}) %collective-permute-start.4) | collective-permute-done | bytes 262176 | tf_op jit(solution)/shard_map/ppermute | solution.py:18
  42.3 3.1 %fusion.71 = f32[8,16,16,128]{3,2,1,0:T(8,128)S(1)} fusion(f32[8,16,16,128]{3,2,1,0:T(8,128)S(1)} %get-tuple-element.5, f32[8,4,16,128]{3,2,1,0:T(8,128)S(1)} %collective-permute-done.5, f32[8,4,16,128]{3,2,1,0:T(8,128)S(1)} %collective-permute-done.4, f32[8,16,4,128]{3,2,1,0:T(4,128)S(1)} %bitcast.74, f32[8,16,4,128]{3,2,1,0:T(4,128)S(1)} %bitcast.73, ...), kind=kLoop, calls=%fused_computation.200 | loop fusion | flops 15728640 | bytes 5373952 | tf_op jit(solution)/shard_map/sub | solution.py:85
  45.5 3.2 %collective-permute-start.10 = (f32[8,16,4,128]{3,2,1,0:T(4,128)S(1)}, f32[8,16,4,128]{3,2,1,0:T(4,128)S(1)}, u32[]{:S(2)}, u32[]{:S(2)}) collective-permute-start(f32[8,16,4,128]{3,2,1,0:T(4,128)S(1)} %get-tuple-element.11), channel_id=1, source_target_pairs={{1,0},{2,1},{3,2},{4,3},{5,4},{6,5},{7,6},{8,7},{9,8},{10,9},{11,1... | collective-permute-start | bytes 786440 | tf_op jit(solution)/shard_map/ppermute | solution.py:18
  53.1 3.4 %collective-permute-start.9 = (f32[8,4,16,128]{3,2,1,0:T(8,128)S(1)}, f32[8,4,16,128]{3,2,1,0:T(8,128)S(1)}, u32[]{:S(2)}, u32[]{:S(2)}) collective-permute-start(f32[8,4,16,128]{3,2,1,0:T(8,128)S(1)} %get-tuple-element.14), channel_id=1, source_target_pairs={{0,8},{1,9},{2,10},{3,11},{4,12},{5,13},{6,14},{7,15},{8,16},{9,17... | collective-permute-start | bytes 786440 | tf_op jit(solution)/shard_map/ppermute | solution.py:18
  56.5 4.4 %collective-permute-done.8 = f32[8,4,16,128]{3,2,1,0:T(8,128)S(1)} collective-permute-done((f32[8,4,16,128]{3,2,1,0:T(8,128)S(1)}, f32[8,4,16,128]{3,2,1,0:T(8,128)S(1)}, u32[]{:S(2)}, u32[]{:S(2)}) %collective-permute-start.8) | collective-permute-done | bytes 262176 | tf_op jit(solution)/shard_map/ppermute | solution.py:18
  62.9 3.1 %fusion.42 = f32[8,16,16,128]{3,2,1,0:T(8,128)S(1)} fusion(f32[8,16,16,128]{3,2,1,0:T(8,128)S(1)} %fusion.71, f32[8,4,16,128]{3,2,1,0:T(8,128)S(1)} %collective-permute-done.9, f32[8,4,16,128]{3,2,1,0:T(8,128)S(1)} %collective-permute-done.8, f32[8,16,4,128]{3,2,1,0:T(4,128)S(1)} %bitcast.72, f32[8,16,4,128]{3,2,1,0:T(4,128)S(1)} %bitcast.69, ...), kind=kLoop, calls=%fused_computation.171 | loop fusion | flops 15990784 | bytes 4325376 | tf_op jit(solution)/shard_map/sub | solution.py:85
  68.8 2.8 collective-permute-start.15
  73.7 3.4 %collective-permute-start.13 = (f32[8,4,16,128]{3,2,1,0:T(8,128)S(1)}, f32[8,4,16,128]{3,2,1,0:T(8,128)S(1)}, u32[]{:S(2)}, u32[]{:S(2)}) collective-permute-start(f32[8,4,16,128]{3,2,1,0:T(8,128)S(1)} %get-tuple-element.10), channel_id=1, source_target_pairs={{0,8},{1,9},{2,10},{3,11},{4,12},{5,13},{6,14},{7,15},{8,16},{9,17... | collective-permute-start | bytes 786440 | tf_op jit(solution)/shard_map/ppermute | solution.py:18
  77.1 4.8 %collective-permute-done.12 = f32[8,4,16,128]{3,2,1,0:T(8,128)S(1)} collective-permute-done((f32[8,4,16,128]{3,2,1,0:T(8,128)S(1)}, f32[8,4,16,128]{3,2,1,0:T(8,128)S(1)}, u32[]{:S(2)}, u32[]{:S(2)}) %collective-permute-start.12) | collective-permute-done | bytes 262176 | tf_op jit(solution)/shard_map/ppermute | solution.py:18
  83.8 3.1 %fusion.13 = f32[8,16,16,128]{3,2,1,0:T(8,128)S(1)} fusion(f32[8,16,16,128]{3,2,1,0:T(8,128)S(1)} %fusion.71, f32[8,16,16,128]{3,2,1,0:T(8,128)S(1)} %fusion.42, f32[8,4,16,128]{3,2,1,0:T(8,128)S(1)} %collective-permute-done.13, f32[8,4,16,128]{3,2,1,0:T(8,128)S(1)} %collective-permute-done.12, f32[8,16,4,128]{3,2,1,0:T(4,128)S(1)} %bitcast.70, ...), kind=kLoop, calls=%fused_computation.142 | loop fusion | flops 15728640 | bytes 4325376 | tf_op jit(solution)/shard_map/sub | solution.py:85
  87.6 48.4 %all_to_all.45 = f32[8,256,128]{2,0,1:T(8,128)S(1)} all-to-all(f32[8,256,128]{2,0,1:T(8,128)S(1)} %bitcast.62), channel_id=1, replica_groups=mesh['band'=8,'dom'=64] {'band'}, dimensions={1} | all-to-all | bytes 2097152 | tf_op jit(solution)/shard_map/all_to_all | solution.py:100
  137.0 46.1 %all_to_all.46 = f32[64,1,64]{2,1,0:T(1,128)S(1)} all-to-all(f32[64,1,64]{2,1,0:T(1,128)S(1)} %bitcast.83), channel_id=1, replica_groups=mesh['band'=8,'dom'=64] {'dom'}, dimensions={0} | all-to-all | bytes 32768 | tf_op jit(solution)/shard_map/all_to_all | solution.py:66
  183.1 18.5 %all_to_all.47 = f32[8,1,64]{2,1,0:T(1,128)S(1)} all-to-all(f32[8,1,64]{2,1,0:T(1,128)S(1)} %broadcast_in_dim.8), channel_id=1, replica_groups=mesh['band'=8,'dom'=64] {'band'}, dimensions={0} | all-to-all | bytes 4096 | tf_op jit(solution)/shard_map/all_to_all | solution.py:62
  201.7 17.7 %all_to_all.48 = f32[64,1,64]{2,1,0:T(1,128)S(1)} all-to-all(f32[64,1,64]{2,1,0:T(1,128)S(1)} %broadcast_in_dim.9), channel_id=1, replica_groups=mesh['band'=8,'dom'=64] {'dom'}, dimensions={0} | all-to-all | bytes 32768 | tf_op jit(solution)/shard_map/all_to_all | solution.py:62
  219.6 5.8 %cholesky.17 = f32[64,64]{1,0:T(8,128)S(1)} custom-call(f32[64,64]{1,0:T(8,128)S(1)} %fusion.214), custom_call_target="Cholesky" | custom-call | tf_op jit(solution)/shard_map/jit(cholesky)/cholesky | solution.py:54
  226.8 4.9 %custom-call.6 = f32[1,64,64]{1,2,0:T(8,128)S(1)} custom-call(f32[1,64,64]{2,1,0:T(8,128)S(1)} %fusion.213), custom_call_target="InvertDiagBlocksLowerTriangular" | custom-call | tf_op jit(solution)/shard_map/triangular_solve | solution.py:55
  233.6 60.9 %all_to_all.49 = f32[64,32,128]{2,1,0:T(8,128)S(1)} all-to-all(f32[64,32,128]{2,1,0:T(8,128)S(1)} %copy.38), channel_id=1, replica_groups=mesh['band'=8,'dom'=64] {'band'}, dimensions={0} | all-to-all | bytes 2097152 | tf_op jit(solution)/shard_map/all_to_all | solution.py:106
  (57 shorter events, 31.4 us)
Async XLA Ops:
  0.0 7.2 %copy-start = (f32[8,1,16,16,128]{4,3,2,1,0:T(8,128)S(1)}, f32[8,1,16,16,128]{4,3,2,1,0:T(8,128)}, u32[]{:S(2)}) copy-start(f32[8,1,16,16,128]{4,3,2,1,0:T(8,128)} %param.2) | copy-start | bytes 3145732
  1.4 13.8 %collective-permute-start.2 = (f32[8,16,4,128]{3,2,1,0:T(4,128)S(1)}, f32[8,16,4,128]{3,2,1,0:T(4,128)S(1)}, u32[]{:S(2)}, u32[]{:S(2)}) collective-permute-start(f32[8,16,4,128]{3,2,1,0:T(4,128)S(1)} %get-tuple-element.21), channel_id=1, source_target_pairs={{1,0},{2,1},{3,2},{4,3},{5,4},{6,5},{7,6},{8,7},{9,8},{10,9},{11,1... | collective-permute-start | bytes 786440 | tf_op jit(solution)/shard_map/ppermute | solution.py:18
  4.0 18.2 %copy-start.1 = (f32[1,16,16,128]{3,2,1,0:T(8,128)S(1)}, f32[1,16,16,128]{3,2,1,0:T(8,128)}, u32[]{:S(2)}) copy-start(f32[1,16,16,128]{3,2,1,0:T(8,128)} %param.3) | copy-start | bytes 393220
  4.0 11.2 %collective-permute-start.3 = (f32[8,16,4,128]{3,2,1,0:T(4,128)S(1)}, f32[8,16,4,128]{3,2,1,0:T(4,128)S(1)}, u32[]{:S(2)}, u32[]{:S(2)}) collective-permute-start(f32[8,16,4,128]{3,2,1,0:T(4,128)S(1)} %get-tuple-element.22), channel_id=1, source_target_pairs={{0,1},{1,2},{2,3},{3,4},{4,5},{5,6},{6,7},{7,8},{8,9},{9,10},{10,1... | collective-permute-start | bytes 786440 | tf_op jit(solution)/shard_map/ppermute | solution.py:18
  7.2 11.2 %collective-permute-start = (f32[8,4,16,128]{3,2,1,0:T(8,128)S(1)}, f32[8,4,16,128]{3,2,1,0:T(8,128)S(1)}, u32[]{:S(2)}, u32[]{:S(2)}) collective-permute-start(f32[8,4,16,128]{3,2,1,0:T(8,128)S(1)} %get-tuple-element.19), channel_id=1, source_target_pairs={{8,0},{9,1},{10,2},{11,3},{12,4},{13,5},{14,6},{15,7},{16,8},{17,9... | collective-permute-start | bytes 786440 | tf_op jit(solution)/shard_map/ppermute | solution.py:18
  13.2 8.9 %collective-permute-start.1 = (f32[8,4,16,128]{3,2,1,0:T(8,128)S(1)}, f32[8,4,16,128]{3,2,1,0:T(8,128)S(1)}, u32[]{:S(2)}, u32[]{:S(2)}) collective-permute-start(f32[8,4,16,128]{3,2,1,0:T(8,128)S(1)} %get-tuple-element.20), channel_id=1, source_target_pairs={{0,8},{1,9},{2,10},{3,11},{4,12},{5,13},{6,14},{7,15},{8,16},{9,17... | collective-permute-start | bytes 786440 | tf_op jit(solution)/shard_map/ppermute | solution.py:18
  25.4 11.0 %collective-permute-start.6 = (f32[8,16,4,128]{3,2,1,0:T(4,128)S(1)}, f32[8,16,4,128]{3,2,1,0:T(4,128)S(1)}, u32[]{:S(2)}, u32[]{:S(2)}) collective-permute-start(f32[8,16,4,128]{3,2,1,0:T(4,128)S(1)} %get-tuple-element.15), channel_id=1, source_target_pairs={{1,0},{2,1},{3,2},{4,3},{5,4},{6,5},{7,6},{8,7},{9,8},{10,9},{11,1... | collective-permute-start | bytes 786440 | tf_op jit(solution)/shard_map/ppermute | solution.py:18
  29.0 7.4 %collective-permute-start.7 = (f32[8,16,4,128]{3,2,1,0:T(4,128)S(1)}, f32[8,16,4,128]{3,2,1,0:T(4,128)S(1)}, u32[]{:S(2)}, u32[]{:S(2)}) collective-permute-start(f32[8,16,4,128]{3,2,1,0:T(4,128)S(1)} %get-tuple-element.16), channel_id=1, source_target_pairs={{0,1},{1,2},{2,3},{3,4},{4,5},{5,6},{6,7},{7,8},{8,9},{9,10},{10,1... | collective-permute-start | bytes 786440 | tf_op jit(solution)/shard_map/ppermute | solution.py:18
  31.0 9.3 %collective-permute-start.4 = (f32[8,4,16,128]{3,2,1,0:T(8,128)S(1)}, f32[8,4,16,128]{3,2,1,0:T(8,128)S(1)}, u32[]{:S(2)}, u32[]{:S(2)}) collective-permute-start(f32[8,4,16,128]{3,2,1,0:T(8,128)S(1)} %get-tuple-element.17), channel_id=1, source_target_pairs={{8,0},{9,1},{10,2},{11,3},{12,4},{13,5},{14,6},{15,7},{16,8},{17,9... | collective-permute-start | bytes 786440 | tf_op jit(solution)/shard_map/ppermute | solution.py:18
  32.9 9.3 %collective-permute-start.5 = (f32[8,4,16,128]{3,2,1,0:T(8,128)S(1)}, f32[8,4,16,128]{3,2,1,0:T(8,128)S(1)}, u32[]{:S(2)}, u32[]{:S(2)}) collective-permute-start(f32[8,4,16,128]{3,2,1,0:T(8,128)S(1)} %get-tuple-element.18), channel_id=1, source_target_pairs={{0,8},{1,9},{2,10},{3,11},{4,12},{5,13},{6,14},{7,15},{8,16},{9,17... | collective-permute-start | bytes 786440 | tf_op jit(solution)/shard_map/ppermute | solution.py:18
  45.5 10.9 %collective-permute-start.10 = (f32[8,16,4,128]{3,2,1,0:T(4,128)S(1)}, f32[8,16,4,128]{3,2,1,0:T(4,128)S(1)}, u32[]{:S(2)}, u32[]{:S(2)}) collective-permute-start(f32[8,16,4,128]{3,2,1,0:T(4,128)S(1)} %get-tuple-element.11), channel_id=1, source_target_pairs={{1,0},{2,1},{3,2},{4,3},{5,4},{6,5},{7,6},{8,7},{9,8},{10,9},{11,1... | collective-permute-start | bytes 786440 | tf_op jit(solution)/shard_map/ppermute | solution.py:18
  48.7 7.8 %collective-permute-start.11 = (f32[8,16,4,128]{3,2,1,0:T(4,128)S(1)}, f32[8,16,4,128]{3,2,1,0:T(4,128)S(1)}, u32[]{:S(2)}, u32[]{:S(2)}) collective-permute-start(f32[8,16,4,128]{3,2,1,0:T(4,128)S(1)} %get-tuple-element.12), channel_id=1, source_target_pairs={{0,1},{1,2},{2,3},{3,4},{4,5},{5,6},{6,7},{7,8},{8,9},{9,10},{10,1... | collective-permute-start | bytes 786440 | tf_op jit(solution)/shard_map/ppermute | solution.py:18
  51.2 9.8 %collective-permute-start.8 = (f32[8,4,16,128]{3,2,1,0:T(8,128)S(1)}, f32[8,4,16,128]{3,2,1,0:T(8,128)S(1)}, u32[]{:S(2)}, u32[]{:S(2)}) collective-permute-start(f32[8,4,16,128]{3,2,1,0:T(8,128)S(1)} %get-tuple-element.13), channel_id=1, source_target_pairs={{8,0},{9,1},{10,2},{11,3},{12,4},{13,5},{14,6},{15,7},{16,8},{17,9... | collective-permute-start | bytes 786440 | tf_op jit(solution)/shard_map/ppermute | solution.py:18
  53.1 9.8 %collective-permute-start.9 = (f32[8,4,16,128]{3,2,1,0:T(8,128)S(1)}, f32[8,4,16,128]{3,2,1,0:T(8,128)S(1)}, u32[]{:S(2)}, u32[]{:S(2)}) collective-permute-start(f32[8,4,16,128]{3,2,1,0:T(8,128)S(1)} %get-tuple-element.14), channel_id=1, source_target_pairs={{0,8},{1,9},{2,10},{3,11},{4,12},{5,13},{6,14},{7,15},{8,16},{9,17... | collective-permute-start | bytes 786440 | tf_op jit(solution)/shard_map/ppermute | solution.py:18
  66.1 10.9 %collective-permute-start.14 = (f32[8,16,4,128]{3,2,1,0:T(4,128)S(1)}, f32[8,16,4,128]{3,2,1,0:T(4,128)S(1)}, u32[]{:S(2)}, u32[]{:S(2)}) collective-permute-start(f32[8,16,4,128]{3,2,1,0:T(4,128)S(1)} %get-tuple-element.7), channel_id=1, source_target_pairs={{1,0},{2,1},{3,2},{4,3},{5,4},{6,5},{7,6},{8,7},{9,8},{10,9},{11,1... | collective-permute-start | bytes 786440 | tf_op jit(solution)/shard_map/ppermute | solution.py:18
  68.8 8.2 %collective-permute-start.15 = (f32[8,16,4,128]{3,2,1,0:T(4,128)S(1)}, f32[8,16,4,128]{3,2,1,0:T(4,128)S(1)}, u32[]{:S(2)}, u32[]{:S(2)}) collective-permute-start(f32[8,16,4,128]{3,2,1,0:T(4,128)S(1)} %get-tuple-element.8), channel_id=1, source_target_pairs={{0,1},{1,2},{2,3},{3,4},{4,5},{5,6},{6,7},{7,8},{8,9},{9,10},{10,1... | collective-permute-start | bytes 786440 | tf_op jit(solution)/shard_map/ppermute | solution.py:18
  71.7 10.2 %collective-permute-start.12 = (f32[8,4,16,128]{3,2,1,0:T(8,128)S(1)}, f32[8,4,16,128]{3,2,1,0:T(8,128)S(1)}, u32[]{:S(2)}, u32[]{:S(2)}) collective-permute-start(f32[8,4,16,128]{3,2,1,0:T(8,128)S(1)} %get-tuple-element.9), channel_id=1, source_target_pairs={{8,0},{9,1},{10,2},{11,3},{12,4},{13,5},{14,6},{15,7},{16,8},{17,9... | collective-permute-start | bytes 786440 | tf_op jit(solution)/shard_map/ppermute | solution.py:18
  73.7 10.2 %collective-permute-start.13 = (f32[8,4,16,128]{3,2,1,0:T(8,128)S(1)}, f32[8,4,16,128]{3,2,1,0:T(8,128)S(1)}, u32[]{:S(2)}, u32[]{:S(2)}) collective-permute-start(f32[8,4,16,128]{3,2,1,0:T(8,128)S(1)} %get-tuple-element.10), channel_id=1, source_target_pairs={{0,8},{1,9},{2,10},{3,11},{4,12},{5,13},{6,14},{7,15},{8,16},{9,17... | collective-permute-start | bytes 786440 | tf_op jit(solution)/shard_map/ppermute | solution.py:18

commit v2 on v1

--- a/solution.py
+++ b/solution.py
@@ -57,15 +57,57 @@
     )
 
 
-def spread(row, axis):
-    copies = jnp.broadcast_to(row[None], (lax.axis_size(axis),) + row.shape)
-    return lax.all_to_all(copies, axis, 0, 0, tiled=True)
+def member(y, z_hi, z_lo, plane):
+    return (y * 2 + z_hi) * 64 + z_lo * 8 + plane
+
+
+Y_RINGS = [[0, 2, 4, 6], [1, 3, 5, 7]]
+SHEETS = [
+    [member(y, z_hi, z_lo, plane) for y in range(4) for plane in range(8)]
+    for z_hi in range(2)
+    for z_lo in range(8)
+]
+Z_RINGS = [
+    [member(y, z_hi, z_lo, plane) for z_hi in range(2) for z_lo in range(8)]
+    for y in range(4)
+    for plane in range(8)
+]
+
+
+def over_y(block, split, joined):
+    return lax.all_to_all(block, "band", split, joined, axis_index_groups=Y_RINGS, tiled=True)
+
+
+def across(block):
+    return lax.ppermute(block, "band", [(i, i ^ 1) for i in range(8)])
+
+
+def small_exchange(chunks, groups):
+    return lax.all_to_all(chunks, ("band", "dom"), 0, 0, axis_index_groups=groups, tiled=True)
+
+
+def spread(row, groups):
+    count = len(groups[0])
+    return small_exchange(jnp.broadcast_to(row, (count,) + row.shape[1:]), groups)
 
 
 def summed_everywhere(gram):
-    row = lax.all_to_all(gram[:, None], "dom", 0, 0, tiled=True).sum(axis=0)
-    row = spread(row, "band").sum(axis=0)
-    return spread(row, "dom")[:, 0]
+    row = small_exchange(gram.reshape(32, 1, 128), SHEETS).sum(axis=0, keepdims=True)
+    row = spread(row, Z_RINGS).sum(axis=0, keepdims=True)
+    return spread(row, SHEETS).reshape(gram.shape)
+
+
+def own_first(matrix, side):
+    size = matrix.shape[0] // 2
+    return jnp.where(side == 0, matrix, jnp.roll(matrix, (size, size), (0, 1)))
+
+
+def by_group(matrix):
+    return matrix.reshape(2, 4, 8, 2, 4, 8).transpose(1, 0, 2, 4, 3, 5).reshape(64, 64)
+
+
+def by_side(matrix):
+    return matrix.reshape(4, 2, 8, 4, 2, 8).transpose(1, 0, 2, 4, 3, 5).reshape(64, 64)
 
 
 def on_device(orbitals, potential):
@@ -97,13 +139,26 @@
     )
     layers = local_orbitals.shape[3]
     rows = current.reshape(local_orbitals.shape[0], -1, layers)
-    share = lax.all_to_all(rows, "band", 1, 0, tiled=True)
-    bands = share.shape[0]
-    share = share.reshape(bands, -1)
-    gram = summed_everywhere(jnp.dot(share, share.T, precision=lax.Precision.HIGHEST))
-    inverse = orthonormal(gram / cell_count)
-    rotated = jnp.dot(inverse, share, precision=lax.Precision.HIGHEST)
-    rotated = lax.all_to_all(rotated.reshape(bands, -1, layers), "band", 0, 1, tiled=True)
+    side = lax.axis_index("band") % 2
+    share = over_y(rows, 1, 0)
+    half = share.shape[1] // 2
+    kept = lax.dynamic_slice_in_dim(share, side * half, half, 1)
+    given = lax.dynamic_slice_in_dim(share, (1 - side) * half, half, 1)
+    taken = across(given)
+    kept_late, taken = lax.optimization_barrier((kept, taken))
+    taken_late = across(kept_late)
+    count = share.shape[0]
+    both = jnp.concatenate((kept, taken)).reshape(2 * count, -1)
+    gram = jnp.dot(both, both.T, precision=lax.Precision.HIGHEST)
+    gram = summed_everywhere(own_first(gram, side)) / cell_count
+    inverse = orthonormal(by_group(gram))
+    inverse = own_first(by_side(inverse), side)[:count]
+    late = jnp.concatenate((given, taken_late)).reshape(2 * count, -1)
+    early_out = jnp.dot(inverse, both, precision=lax.Precision.HIGHEST).reshape(count, half, layers)
+    late_out = jnp.dot(inverse, late, precision=lax.Precision.HIGHEST).reshape(count, half, layers)
+    first = jnp.where(side == 0, early_out, late_out)
+    second = jnp.where(side == 0, late_out, early_out)
+    rotated = over_y(jnp.concatenate((first, second), axis=1), 0, 1)
     return rotated.reshape(orbitals.shape)
 
 

time: 296 us -> 288 us (0.973)
  the two profiles are of different devices: /device:TPU:33 before, /device:TPU:32 now
where the time goes in v2:
time: 288 us; the launch traced here: 287 us
  waiting for transfers between devices  92.2 us (32%)
  starting transfers between devices  91.1 us (32%)
  blocking collectives  66.7 us (23%)
  other arithmetic  25.2 us (9%)
  local copies, waits for them, and re-layouts  8.54 us (3%)
    ppermute x16, starting transfers between devices, from_behind(): return lax.ppermute(block, axis, route)  54.3 us
    all_to_all x1, blocking collectives, small_exchange(): lax.all_to_all(chunks, ('band', 'dom'), 0, 0, axis_index_groups=groups, t...  47.3 us
    ppermute x2, waiting for transfers between devices, across(): return lax.ppermute(block, 'band', [(i, i ^ 1) for i in range(8)])  46.1 us
    ppermute x16, waiting for transfers between devices, from_behind(): return lax.ppermute(block, axis, route)  20.6 us
    all_to_all x1, blocking collectives, over_y(): lax.all_to_all(block, 'band', split, joined, axis_index_groups=Y_RINGS, t...  19.5 us
    all_to_all x2, starting transfers between devices, small_exchange(): lax.all_to_all(chunks, ('band', 'dom'), 0, 0, axis_index_groups=groups, t...  17 us
    ppermute x2, starting transfers between devices, across(): return lax.ppermute(block, 'band', [(i, i ^ 1) for i in range(8)])  16.3 us
    all_to_all x2, waiting for transfers between devices, small_exchange(): lax.all_to_all(chunks, ('band', 'dom'), 0, 0, axis_index_groups=groups, t...  14.6 us
  transfers between devices with their start and end apart: 21, of which 13 were waited for; matrix products, arithmetic and copies ran while one was open for 5% of the time, Pallas kernels for 0%

profile of v2, /device:TPU:32, one launch (start us, length us, event | category | flops | bytes accessed | tf_op | source)
XLA Modules:
  0.0 287.1 jit_solution(16785407954268694175)
XLA Ops:
  1.4 3.7 %collective-permute-start.2 = (f32[8,16,4,128]{3,2,1,0:T(4,128)S(1)}, f32[8,16,4,128]{3,2,1,0:T(4,128)S(1)}, u32[]{:S(2)}, u32[]{:S(2)}) collective-permute-start(f32[8,16,4,128]{3,2,1,0:T(4,128)S(1)} %get-tuple-element.29), channel_id=1, source_target_pairs={{1,0},{2,1},{3,2},{4,3},{5,4},{6,5},{7,6},{8,7},{9,8},{10,9},{11,1... | collective-permute-start | bytes 786440 | tf_op jit(solution)/shard_map/ppermute | solution.py:18
  7.2 6.2 %collective-permute-start = (f32[8,4,16,128]{3,2,1,0:T(8,128)S(1)}, f32[8,4,16,128]{3,2,1,0:T(8,128)S(1)}, u32[]{:S(2)}, u32[]{:S(2)}) collective-permute-start(f32[8,4,16,128]{3,2,1,0:T(8,128)S(1)} %get-tuple-element.27), channel_id=1, source_target_pairs={{8,0},{9,1},{10,2},{11,3},{12,4},{13,5},{14,6},{15,7},{16,8},{17,9... | collective-permute-start | bytes 786440 | tf_op jit(solution)/shard_map/ppermute | solution.py:18
  15.4 3.7 %collective-permute-done = f32[8,4,16,128]{3,2,1,0:T(8,128)S(1)} collective-permute-done((f32[8,4,16,128]{3,2,1,0:T(8,128)S(1)}, f32[8,4,16,128]{3,2,1,0:T(8,128)S(1)}, u32[]{:S(2)}, u32[]{:S(2)}) %collective-permute-start) | collective-permute-done | bytes 262176 | tf_op jit(solution)/shard_map/ppermute | solution.py:18
  19.1 4.1 %collective-permute-done.1 = f32[8,4,16,128]{3,2,1,0:T(8,128)S(1)} collective-permute-done((f32[8,4,16,128]{3,2,1,0:T(8,128)S(1)}, f32[8,4,16,128]{3,2,1,0:T(8,128)S(1)}, u32[]{:S(2)}, u32[]{:S(2)}) %collective-permute-start.1) | collective-permute-done | bytes 262176 | tf_op jit(solution)/shard_map/ppermute | solution.py:18
  28.3 5.8 %collective-permute-start.6 = (f32[8,16,4,128]{3,2,1,0:T(4,128)S(1)}, f32[8,16,4,128]{3,2,1,0:T(4,128)S(1)}, u32[]{:S(2)}, u32[]{:S(2)}) collective-permute-start(f32[8,16,4,128]{3,2,1,0:T(4,128)S(1)} %get-tuple-element.23), channel_id=1, source_target_pairs={{1,0},{2,1},{3,2},{4,3},{5,4},{6,5},{7,6},{8,7},{9,8},{10,9},{11,1... | collective-permute-start | bytes 786440 | tf_op jit(solution)/shard_map/ppermute | solution.py:18
  36.0 3.9 %collective-permute-start.5 = (f32[8,4,16,128]{3,2,1,0:T(8,128)S(1)}, f32[8,4,16,128]{3,2,1,0:T(8,128)S(1)}, u32[]{:S(2)}, u32[]{:S(2)}) collective-permute-start(f32[8,4,16,128]{3,2,1,0:T(8,128)S(1)} %get-tuple-element.26), channel_id=1, source_target_pairs={{0,8},{1,9},{2,10},{3,11},{4,12},{5,13},{6,14},{7,15},{8,16},{9,17... | collective-permute-start | bytes 786440 | tf_op jit(solution)/shard_map/ppermute | solution.py:18
  40.1 3.6 %collective-permute-done.4 = f32[8,4,16,128]{3,2,1,0:T(8,128)S(1)} collective-permute-done((f32[8,4,16,128]{3,2,1,0:T(8,128)S(1)}, f32[8,4,16,128]{3,2,1,0:T(8,128)S(1)}, u32[]{:S(2)}, u32[]{:S(2)}) %collective-permute-start.4) | collective-permute-done | bytes 262176 | tf_op jit(solution)/shard_map/ppermute | solution.py:18
  49.5 5.8 %collective-permute-start.10 = (f32[8,16,4,128]{3,2,1,0:T(4,128)S(1)}, f32[8,16,4,128]{3,2,1,0:T(4,128)S(1)}, u32[]{:S(2)}, u32[]{:S(2)}) collective-permute-start(f32[8,16,4,128]{3,2,1,0:T(4,128)S(1)} %get-tuple-element.19), channel_id=1, source_target_pairs={{1,0},{2,1},{3,2},{4,3},{5,4},{6,5},{7,6},{8,7},{9,8},{10,9},{11,1... | collective-permute-start | bytes 786440 | tf_op jit(solution)/shard_map/ppermute | solution.py:18
  57.2 3.9 %collective-permute-start.9 = (f32[8,4,16,128]{3,2,1,0:T(8,128)S(1)}, f32[8,4,16,128]{3,2,1,0:T(8,128)S(1)}, u32[]{:S(2)}, u32[]{:S(2)}) collective-permute-start(f32[8,4,16,128]{3,2,1,0:T(8,128)S(1)} %get-tuple-element.22), channel_id=1, source_target_pairs={{0,8},{1,9},{2,10},{3,11},{4,12},{5,13},{6,14},{7,15},{8,16},{9,17... | collective-permute-start | bytes 786440 | tf_op jit(solution)/shard_map/ppermute | solution.py:18
  61.3 3.9 %collective-permute-done.8 = f32[8,4,16,128]{3,2,1,0:T(8,128)S(1)} collective-permute-done((f32[8,4,16,128]{3,2,1,0:T(8,128)S(1)}, f32[8,4,16,128]{3,2,1,0:T(8,128)S(1)}, u32[]{:S(2)}, u32[]{:S(2)}) %collective-permute-start.8) | collective-permute-done | bytes 262176 | tf_op jit(solution)/shard_map/ppermute | solution.py:18
  70.7 5.8 %collective-permute-start.14 = (f32[8,16,4,128]{3,2,1,0:T(4,128)S(1)}, f32[8,16,4,128]{3,2,1,0:T(4,128)S(1)}, u32[]{:S(2)}, u32[]{:S(2)}) collective-permute-start(f32[8,16,4,128]{3,2,1,0:T(4,128)S(1)} %get-tuple-element.15), channel_id=1, source_target_pairs={{1,0},{2,1},{3,2},{4,3},{5,4},{6,5},{7,6},{8,7},{9,8},{10,9},{11,1... | collective-permute-start | bytes 786440 | tf_op jit(solution)/shard_map/ppermute | solution.py:18
  78.4 3.9 %collective-permute-start.13 = (f32[8,4,16,128]{3,2,1,0:T(8,128)S(1)}, f32[8,4,16,128]{3,2,1,0:T(8,128)S(1)}, u32[]{:S(2)}, u32[]{:S(2)}) collective-permute-start(f32[8,4,16,128]{3,2,1,0:T(8,128)S(1)} %get-tuple-element.18), channel_id=1, source_target_pairs={{0,8},{1,9},{2,10},{3,11},{4,12},{5,13},{6,14},{7,15},{8,16},{9,17... | collective-permute-start | bytes 786440 | tf_op jit(solution)/shard_map/ppermute | solution.py:18
  82.4 3.9 %collective-permute-done.12 = f32[8,4,16,128]{3,2,1,0:T(8,128)S(1)} collective-permute-done((f32[8,4,16,128]{3,2,1,0:T(8,128)S(1)}, f32[8,4,16,128]{3,2,1,0:T(8,128)S(1)}, u32[]{:S(2)}, u32[]{:S(2)}) %collective-permute-start.12) | collective-permute-done | bytes 262176 | tf_op jit(solution)/shard_map/ppermute | solution.py:18
  94.9 11.0 %all-to-all-done = f32[8,256,128]{2,0,1:T(8,128)S(1)} async-done(((f32[8,256,128]{2,0,1:T(8,128)}), f32[8,256,128]{2,0,1:T(8,128)S(1)}, u32[]{:S(2)}, u32[]{:S(2)}) %all-to-all-start) | async-done | bytes 1048608 | tf_op jit(solution)/shard_map/all_to_all | solution.py:78
  106.1 12.7 %collective-permute-start.16 = (f32[32,32,128]{2,0,1:T(8,128)S(1)}, f32[32,32,128]{2,0,1:T(8,128)S(1)}, u32[]{:S(2)}, u32[]{:S(2)}) collective-permute-start(f32[32,32,128]{2,0,1:T(8,128)S(1)} %get-tuple-element.13), channel_id=1, source_target_pairs={{0,64},{64,0},{128,192},{192,128},{256,320},{320,256},{384,448},{4... | collective-permute-start | bytes 1572872 | tf_op jit(solution)/shard_map/ppermute | solution.py:82
  118.9 10.9 %collective-permute-done.16 = f32[32,32,128]{2,0,1:T(8,128)S(1)} collective-permute-done((f32[32,32,128]{2,0,1:T(8,128)S(1)}, f32[32,32,128]{2,0,1:T(8,128)S(1)}, u32[]{:S(2)}, u32[]{:S(2)}) %collective-permute-start.16) | collective-permute-done | bytes 524320 | tf_op jit(solution)/shard_map/ppermute | solution.py:82
  131.1 47.3 %all_to_all.48 = f32[32,1,128]{2,1,0:T(1,128)S(1)} all-to-all(f32[32,1,128]{2,1,0:T(1,128)S(1)} %bitcast.125), channel_id=1, replica_groups={{0,1,2,3,4,5,6,7,128,129,130,131,132,133,134,135,256,257,258,259,260,26..., dimensions={0} | all-to-all | bytes 32768 | tf_op jit(solution)/shard_map/all_to_all | solution.py:86
  179.0 13.1 %all-to-all-start.2 = ((f32[16,1,128]{2,1,0:T(1,128)}), f32[16,1,128]{2,1,0:T(1,128)S(1)}, u32[]{:S(2)}, u32[]{:S(2)}) async-start(f32[16,1,128]{2,1,0:T(1,128)} %broadcast_in_dim.5), calls=%async_computation.2 | async-start | bytes 16384 | tf_op jit(solution)/shard_map/all_to_all | solution.py:86
  192.2 10.9 %all-to-all-done.2 = f32[16,1,128]{2,1,0:T(1,128)S(1)} async-done(((f32[16,1,128]{2,1,0:T(1,128)}), f32[16,1,128]{2,1,0:T(1,128)S(1)}, u32[]{:S(2)}, u32[]{:S(2)}) %all-to-all-start.2) | async-done | bytes 8224 | tf_op jit(solution)/shard_map/all_to_all | solution.py:86
  203.8 3.8 %all-to-all-start.3 = ((f32[32,1,128]{2,1,0:T(1,128)}), f32[32,1,128]{2,1,0:T(1,128)S(1)}, u32[]{:S(2)}, u32[]{:S(2)}) async-start(f32[32,1,128]{2,1,0:T(1,128)} %broadcast_in_dim.6), calls=%async_computation.3 | async-start | bytes 32768 | tf_op jit(solution)/shard_map/all_to_all | solution.py:86
  215.9 5.8 %cholesky.18 = f32[64,64]{1,0:T(8,128)S(1)} custom-call(f32[64,64]{1,0:T(8,128)S(1)} %fusion.220), custom_call_target="Cholesky" | custom-call | tf_op jit(solution)/shard_map/jit(cholesky)/cholesky | solution.py:54
  223.1 4.9 %custom-call.6 = f32[1,64,64]{1,2,0:T(8,128)S(1)} custom-call(f32[1,64,64]{2,1,0:T(8,128)S(1)} %fusion.217), custom_call_target="InvertDiagBlocksLowerTriangular" | custom-call | tf_op jit(solution)/shard_map/triangular_solve | solution.py:55
  230.0 35.2 %collective-permute-done.17 = f32[32,32,128]{2,0,1:T(8,128)S(1)} collective-permute-done((f32[32,32,128]{2,0,1:T(8,128)S(1)}, f32[32,32,128]{2,0,1:T(8,128)S(1)}, u32[]{:S(2)}, u32[]{:S(2)}) %collective-permute-start.17) | collective-permute-done | bytes 524320 | tf_op jit(solution)/shard_map/ppermute | solution.py:82
  266.5 19.5 %all_to_all.49 = f32[32,64,128]{2,1,0:T(8,128)S(1)} all-to-all(f32[32,64,128]{2,1,0:T(8,128)S(1)} %copy.68), channel_id=1, replica_groups={{0,128,256,384},{64,192,320,448},{1,129,257,385},{65,193,321,449},{2,13..., dimensions={0} | all-to-all | bytes 2097152 | tf_op jit(solution)/shard_map/all_to_all | solution.py:78
  (89 shorter events, 53.1 us)
Async XLA Ops:
  0.0 7.1 %copy-start = (f32[8,1,16,16,128]{4,3,2,1,0:T(8,128)S(1)}, f32[8,1,16,16,128]{4,3,2,1,0:T(8,128)}, u32[]{:S(2)}) copy-start(f32[8,1,16,16,128]{4,3,2,1,0:T(8,128)} %param.2) | copy-start | bytes 3145732
  1.4 13.9 %collective-permute-start.2 = (f32[8,16,4,128]{3,2,1,0:T(4,128)S(1)}, f32[8,16,4,128]{3,2,1,0:T(4,128)S(1)}, u32[]{:S(2)}, u32[]{:S(2)}) collective-permute-start(f32[8,16,4,128]{3,2,1,0:T(4,128)S(1)} %get-tuple-element.29), channel_id=1, source_target_pairs={{1,0},{2,1},{3,2},{4,3},{5,4},{6,5},{7,6},{8,7},{9,8},{10,9},{11,1... | collective-permute-start | bytes 786440 | tf_op jit(solution)/shard_map/ppermute | solution.py:18
  5.1 18.1 %copy-start.1 = (f32[1,16,16,128]{3,2,1,0:T(8,128)S(1)}, f32[1,16,16,128]{3,2,1,0:T(8,128)}, u32[]{:S(2)}) copy-start(f32[1,16,16,128]{3,2,1,0:T(8,128)} %param.3) | copy-start | bytes 393220
  5.1 10.3 %collective-permute-start.3 = (f32[8,16,4,128]{3,2,1,0:T(4,128)S(1)}, f32[8,16,4,128]{3,2,1,0:T(4,128)S(1)}, u32[]{:S(2)}, u32[]{:S(2)}) collective-permute-start(f32[8,16,4,128]{3,2,1,0:T(4,128)S(1)} %get-tuple-element.30), channel_id=1, source_target_pairs={{0,1},{1,2},{2,3},{3,4},{4,5},{5,6},{6,7},{7,8},{8,9},{9,10},{10,1... | collective-permute-start | bytes 786440 | tf_op jit(solution)/shard_map/ppermute | solution.py:18
  7.2 11.9 %collective-permute-start = (f32[8,4,16,128]{3,2,1,0:T(8,128)S(1)}, f32[8,4,16,128]{3,2,1,0:T(8,128)S(1)}, u32[]{:S(2)}, u32[]{:S(2)}) collective-permute-start(f32[8,4,16,128]{3,2,1,0:T(8,128)S(1)} %get-tuple-element.27), channel_id=1, source_target_pairs={{8,0},{9,1},{10,2},{11,3},{12,4},{13,5},{14,6},{15,7},{16,8},{17,9... | collective-permute-start | bytes 786440 | tf_op jit(solution)/shard_map/ppermute | solution.py:18
  13.4 9.8 %collective-permute-start.1 = (f32[8,4,16,128]{3,2,1,0:T(8,128)S(1)}, f32[8,4,16,128]{3,2,1,0:T(8,128)S(1)}, u32[]{:S(2)}, u32[]{:S(2)}) collective-permute-start(f32[8,4,16,128]{3,2,1,0:T(8,128)S(1)} %get-tuple-element.28), channel_id=1, source_target_pairs={{0,8},{1,9},{2,10},{3,11},{4,12},{5,13},{6,14},{7,15},{8,16},{9,17... | collective-permute-start | bytes 786440 | tf_op jit(solution)/shard_map/ppermute | solution.py:18
  26.4 13.6 %collective-permute-start.7 = (f32[8,16,4,128]{3,2,1,0:T(4,128)S(1)}, f32[8,16,4,128]{3,2,1,0:T(4,128)S(1)}, u32[]{:S(2)}, u32[]{:S(2)}) collective-permute-start(f32[8,16,4,128]{3,2,1,0:T(4,128)S(1)} %get-tuple-element.24), channel_id=1, source_target_pairs={{0,1},{1,2},{2,3},{3,4},{4,5},{5,6},{6,7},{7,8},{8,9},{9,10},{10,1... | collective-permute-start | bytes 786440 | tf_op jit(solution)/shard_map/ppermute | solution.py:18
  28.3 11.7 %collective-permute-start.6 = (f32[8,16,4,128]{3,2,1,0:T(4,128)S(1)}, f32[8,16,4,128]{3,2,1,0:T(4,128)S(1)}, u32[]{:S(2)}, u32[]{:S(2)}) collective-permute-start(f32[8,16,4,128]{3,2,1,0:T(4,128)S(1)} %get-tuple-element.23), channel_id=1, source_target_pairs={{1,0},{2,1},{3,2},{4,3},{5,4},{6,5},{7,6},{8,7},{9,8},{10,9},{11,1... | collective-permute-start | bytes 786440 | tf_op jit(solution)/shard_map/ppermute | solution.py:18
  34.1 9.6 %collective-permute-start.4 = (f32[8,4,16,128]{3,2,1,0:T(8,128)S(1)}, f32[8,4,16,128]{3,2,1,0:T(8,128)S(1)}, u32[]{:S(2)}, u32[]{:S(2)}) collective-permute-start(f32[8,4,16,128]{3,2,1,0:T(8,128)S(1)} %get-tuple-element.25), channel_id=1, source_target_pairs={{8,0},{9,1},{10,2},{11,3},{12,4},{13,5},{14,6},{15,7},{16,8},{17,9... | collective-permute-start | bytes 786440 | tf_op jit(solution)/shard_map/ppermute | solution.py:18
  36.0 8.3 %collective-permute-start.5 = (f32[8,4,16,128]{3,2,1,0:T(8,128)S(1)}, f32[8,4,16,128]{3,2,1,0:T(8,128)S(1)}, u32[]{:S(2)}, u32[]{:S(2)}) collective-permute-start(f32[8,4,16,128]{3,2,1,0:T(8,128)S(1)} %get-tuple-element.26), channel_id=1, source_target_pairs={{0,8},{1,9},{2,10},{3,11},{4,12},{5,13},{6,14},{7,15},{8,16},{9,17... | collective-permute-start | bytes 786440 | tf_op jit(solution)/shard_map/ppermute | solution.py:18
  47.6 13.6 %collective-permute-start.11 = (f32[8,16,4,128]{3,2,1,0:T(4,128)S(1)}, f32[8,16,4,128]{3,2,1,0:T(4,128)S(1)}, u32[]{:S(2)}, u32[]{:S(2)}) collective-permute-start(f32[8,16,4,128]{3,2,1,0:T(4,128)S(1)} %get-tuple-element.20), channel_id=1, source_target_pairs={{0,1},{1,2},{2,3},{3,4},{4,5},{5,6},{6,7},{7,8},{8,9},{9,10},{10,1... | collective-permute-start | bytes 786440 | tf_op jit(solution)/shard_map/ppermute | solution.py:18
  49.5 11.7 %collective-permute-start.10 = (f32[8,16,4,128]{3,2,1,0:T(4,128)S(1)}, f32[8,16,4,128]{3,2,1,0:T(4,128)S(1)}, u32[]{:S(2)}, u32[]{:S(2)}) collective-permute-start(f32[8,16,4,128]{3,2,1,0:T(4,128)S(1)} %get-tuple-element.19), channel_id=1, source_target_pairs={{1,0},{2,1},{3,2},{4,3},{5,4},{6,5},{7,6},{8,7},{9,8},{10,9},{11,1... | collective-permute-start | bytes 786440 | tf_op jit(solution)/shard_map/ppermute | solution.py:18
  55.3 9.9 %collective-permute-start.8 = (f32[8,4,16,128]{3,2,1,0:T(8,128)S(1)}, f32[8,4,16,128]{3,2,1,0:T(8,128)S(1)}, u32[]{:S(2)}, u32[]{:S(2)}) collective-permute-start(f32[8,4,16,128]{3,2,1,0:T(8,128)S(1)} %get-tuple-element.21), channel_id=1, source_target_pairs={{8,0},{9,1},{10,2},{11,3},{12,4},{13,5},{14,6},{15,7},{16,8},{17,9... | collective-permute-start | bytes 786440 | tf_op jit(solution)/shard_map/ppermute | solution.py:18
  57.2 8.3 %collective-permute-start.9 = (f32[8,4,16,128]{3,2,1,0:T(8,128)S(1)}, f32[8,4,16,128]{3,2,1,0:T(8,128)S(1)}, u32[]{:S(2)}, u32[]{:S(2)}) collective-permute-start(f32[8,4,16,128]{3,2,1,0:T(8,128)S(1)} %get-tuple-element.22), channel_id=1, source_target_pairs={{0,8},{1,9},{2,10},{3,11},{4,12},{5,13},{6,14},{7,15},{8,16},{9,17... | collective-permute-start | bytes 786440 | tf_op jit(solution)/shard_map/ppermute | solution.py:18
  68.7 13.6 %collective-permute-start.15 = (f32[8,16,4,128]{3,2,1,0:T(4,128)S(1)}, f32[8,16,4,128]{3,2,1,0:T(4,128)S(1)}, u32[]{:S(2)}, u32[]{:S(2)}) collective-permute-start(f32[8,16,4,128]{3,2,1,0:T(4,128)S(1)} %get-tuple-element.16), channel_id=1, source_target_pairs={{0,1},{1,2},{2,3},{3,4},{4,5},{5,6},{6,7},{7,8},{8,9},{9,10},{10,1... | collective-permute-start | bytes 786440 | tf_op jit(solution)/shard_map/ppermute | solution.py:18
  70.7 11.7 %collective-permute-start.14 = (f32[8,16,4,128]{3,2,1,0:T(4,128)S(1)}, f32[8,16,4,128]{3,2,1,0:T(4,128)S(1)}, u32[]{:S(2)}, u32[]{:S(2)}) collective-permute-start(f32[8,16,4,128]{3,2,1,0:T(4,128)S(1)} %get-tuple-element.15), channel_id=1, source_target_pairs={{1,0},{2,1},{3,2},{4,3},{5,4},{6,5},{7,6},{8,7},{9,8},{10,9},{11,1... | collective-permute-start | bytes 786440 | tf_op jit(solution)/shard_map/ppermute | solution.py:18
  76.5 9.9 %collective-permute-start.12 = (f32[8,4,16,128]{3,2,1,0:T(8,128)S(1)}, f32[8,4,16,128]{3,2,1,0:T(8,128)S(1)}, u32[]{:S(2)}, u32[]{:S(2)}) collective-permute-start(f32[8,4,16,128]{3,2,1,0:T(8,128)S(1)} %get-tuple-element.17), channel_id=1, source_target_pairs={{8,0},{9,1},{10,2},{11,3},{12,4},{13,5},{14,6},{15,7},{16,8},{17,9... | collective-permute-start | bytes 786440 | tf_op jit(solution)/shard_map/ppermute | solution.py:18
  78.4 8.3 %collective-permute-start.13 = (f32[8,4,16,128]{3,2,1,0:T(8,128)S(1)}, f32[8,4,16,128]{3,2,1,0:T(8,128)S(1)}, u32[]{:S(2)}, u32[]{:S(2)}) collective-permute-start(f32[8,4,16,128]{3,2,1,0:T(8,128)S(1)} %get-tuple-element.18), channel_id=1, source_target_pairs={{0,8},{1,9},{2,10},{3,11},{4,12},{5,13},{6,14},{7,15},{8,16},{9,17... | collective-permute-start | bytes 786440 | tf_op jit(solution)/shard_map/ppermute | solution.py:18
  91.4 14.5 %all-to-all-start = ((f32[8,256,128]{2,0,1:T(8,128)}), f32[8,256,128]{2,0,1:T(8,128)S(1)}, u32[]{:S(2)}, u32[]{:S(2)}) async-start(f32[8,256,128]{2,0,1:T(8,128)} %bitcast.2), calls=%async_computation | async-start | bytes 2097152 | tf_op jit(solution)/shard_map/all_to_all | solution.py:78
  106.1 23.7 %collective-permute-start.16 = (f32[32,32,128]{2,0,1:T(8,128)S(1)}, f32[32,32,128]{2,0,1:T(8,128)S(1)}, u32[]{:S(2)}, u32[]{:S(2)}) collective-permute-start(f32[32,32,128]{2,0,1:T(8,128)S(1)} %get-tuple-element.13), channel_id=1, source_target_pairs={{0,64},{64,0},{128,192},{192,128},{256,320},{320,256},{384,448},{4... | collective-permute-start | bytes 1572872 | tf_op jit(solution)/shard_map/ppermute | solution.py:82
  179.0 24.2 %all-to-all-start.2 = ((f32[16,1,128]{2,1,0:T(1,128)}), f32[16,1,128]{2,1,0:T(1,128)S(1)}, u32[]{:S(2)}, u32[]{:S(2)}) async-start(f32[16,1,128]{2,1,0:T(1,128)} %broadcast_in_dim.5), calls=%async_computation.2 | async-start | bytes 16384 | tf_op jit(solution)/shard_map/all_to_all | solution.py:86
  203.8 11.1 %all-to-all-start.3 = ((f32[32,1,128]{2,1,0:T(1,128)}), f32[32,1,128]{2,1,0:T(1,128)S(1)}, u32[]{:S(2)}, u32[]{:S(2)}) async-start(f32[32,1,128]{2,1,0:T(1,128)} %broadcast_in_dim.6), calls=%async_computation.3 | async-start | bytes 32768 | tf_op jit(solution)/shard_map/all_to_all | solution.py:86
  207.7 57.5 %collective-permute-start.17 = (f32[32,32,128]{2,0,1:T(8,128)S(1)}, f32[32,32,128]{2,0,1:T(8,128)S(1)}, u32[]{:S(2)}, u32[]{:S(2)}) collective-permute-start(f32[32,32,128]{2,0,1:T(8,128)S(1)} %get-tuple-element.8), channel_id=1, source_target_pairs={{0,64},{64,0},{128,192},{192,128},{256,320},{320,256},{384,448},{4... | collective-permute-start | bytes 1572872 | tf_op jit(solution)/shard_map/ppermute | solution.py:82

commit v3 on v2

v3 whole, which is shorter than its diff:
```python
import functools

import jax
import jax.numpy as jnp
import numpy as np
from jax import lax
from jax.experimental import pallas as pl
from jax.experimental.pallas import tpu as pltpu
from jax.sharding import PartitionSpec as P

STENCIL = (-205.0 / 72.0, 8.0 / 5.0, -1.0 / 5.0, 8.0 / 315.0, -1.0 / 560.0)
FILTER_LOW = 1.5
FILTER_HIGH = 14.0
MIDDLE = 0.5 * (FILTER_HIGH + FILTER_LOW)
RADIUS = 0.5 * (FILTER_HIGH - FILTER_LOW)
SIDE_STEP = tuple(-0.5 * c / RADIUS for c in STENCIL)

PX = 8
PY = 8
CX = 16
CY = 16
NZ = 128
GROUP = 8
REACH = 4
DEEP = 8
VMEM_BYTES = 40 * 2**20


def member(y, z_hi, z_lo, plane):
    return (y * 2 + z_hi) * 64 + z_lo * 8 + plane


Y_RINGS = [[0, 2, 4, 6], [1, 3, 5, 7]]
Z_PAIRS = [[0, 1], [2, 3], [4, 5], [6, 7]]
SHEETS = [
    [member(y, z_hi, z_lo, plane) for y in range(4) for plane in range(8)]
    for z_hi in range(2)
    for z_lo in range(8)
]
Z_RINGS = [
    [member(y, z_hi, z_lo, plane) for z_hi in range(2) for z_lo in range(8)]
    for y in range(4)
    for plane in range(8)
]


def third_dimension_matrix():
    matrix = np.zeros((NZ, NZ))
    for offset in range(1, REACH + 1):
        band = np.eye(NZ, k=offset) + np.eye(NZ, k=-offset)
        matrix += SIDE_STEP[offset] * band
    matrix += np.eye(NZ) * (3.0 * SIDE_STEP[0] - MIDDLE / RADIUS)
    return matrix.astype(np.float32)


def scaled_hamiltonian(field, potential, along, plane, first, count, origin):
    here = field[plane, pl.ds(first, count)]
    total = jnp.dot(
        here.reshape(count * GROUP, NZ),
        along[...],
        precision=lax.Precision.HIGHEST,
        preferred_element_type=jnp.float32,
    ).reshape(count, GROUP, NZ)
    for offset in range(1, REACH + 1):
        total += SIDE_STEP[offset] * (
            (field[plane + offset, pl.ds(first, count)] + field[plane - offset, pl.ds(first, count)])
            + (
                field[plane, pl.ds(first + offset, count)]
                + field[plane, pl.ds(first - offset, count)]
            )
        )
    local = potential[plane - origin, pl.ds(first - origin, count)] * (1.0 / RADIUS)
    return total + local[:, None, :] * here


def rims_kernel(field, potential, low, high, front, back):
    low[: DEEP * CY] = field[:DEEP].reshape(DEEP * CY, GROUP, NZ)
    high[: DEEP * CY] = field[CX - DEEP :].reshape(DEEP * CY, GROUP, NZ)
    front[: CX * DEEP] = field[:, :DEEP].reshape(CX * DEEP, GROUP, NZ)
    back[: CX * DEEP] = field[:, CY - DEEP :].reshape(CX * DEEP, GROUP, NZ)
    if potential is not None:
        tail = DEEP * CY
        low[tail:] = potential[:REACH].reshape(8, 8, NZ)
        high[tail:] = potential[CX - REACH :].reshape(8, 8, NZ)
        for plane in range(CX):
            slot, row = tail + plane // 2, plane % 2 * REACH
            front[slot, row : row + REACH] = potential[plane, :REACH]
            back[slot, row : row + REACH] = potential[plane, CY - REACH :]


def fill_padded(padded, field, low, high, front, back, low_corner, high_corner):
    end = DEEP + CX
    padded[DEEP:end, DEEP:end] = field[...]
    padded[:DEEP, DEEP:end] = low[: DEEP * CY].reshape(DEEP, CY, GROUP, NZ)
    padded[end:, DEEP:end] = high[: DEEP * CY].reshape(DEEP, CY, GROUP, NZ)
    padded[DEEP:end, :DEEP] = front[: CX * DEEP].reshape(CX, DEEP, GROUP, NZ)
    padded[DEEP:end, end:] = back[: CX * DEEP].reshape(CX, DEEP, GROUP, NZ)
    for rows, corner in ((DEEP - REACH, low_corner), (end, high_corner)):
        padded[rows : rows + REACH, DEEP - REACH : DEEP] = corner[:, :REACH]
        padded[rows : rows + REACH, end : end + REACH] = corner[:, REACH:]


def kept_sides():
    place = lax.axis_index("dom")
    row, column = place // PY, place % PY
    return tuple(
        jnp.where(edge, 0.0, 1.0)
        for edge in (row == 0, row == PX - 1, column == 0, column == PY - 1)
    )


def wide_step(padded, potential, along, earlier, later):
    keep_low, keep_high, keep_front, keep_back = kept_sides()

    def value(plane, first, count):
        total = scaled_hamiltonian(padded, potential, along, plane + DEEP, first + DEEP, count, REACH)
        if earlier is not None:
            total = 2.0 * total - earlier[plane + REACH, pl.ds(first + REACH, count)]
        return total

    def middle(plane, carry):
        total = value(plane, -REACH, CY + 2 * REACH)
        later[plane + REACH, :REACH] = total[:REACH] * keep_front
        later[plane + REACH, REACH : REACH + CY] = total[REACH : REACH + CY]
        later[plane + REACH, REACH + CY :] = total[REACH + CY :] * keep_back
        return carry

    def outer(layer, carry):
        later[layer, REACH : REACH + CY] = value(layer - REACH, 0, CY) * keep_low
        later[layer + CX + REACH, REACH : REACH + CY] = value(layer + CX, 0, CY) * keep_high
        return carry

    lax.fori_loop(0, CX, middle, 0)
    lax.fori_loop(0, REACH, outer, 0)


def narrow_step(wide, potential, along, earlier, store):
    def body(plane, carry):
        total = scaled_hamiltonian(wide, potential, along, plane + REACH, REACH, CY, 0)
        store(plane, 2.0 * total - earlier[plane])
        return carry

    lax.fori_loop(0, CX, body, 0)


def first_pair_kernel(
    field, potential, low, high, front, back, low_corner, high_corner, along,
    once, twice, wide_potential, next_low, next_high, next_front, next_back, padded,
):
    fill_padded(padded, field, low, high, front, back, low_corner, high_corner)
    tail, end = DEEP * CY, REACH + CX
    wide_potential[...] = jnp.zeros_like(wide_potential)
    wide_potential[REACH:end, REACH:end] = potential[...]
    wide_potential[:REACH, REACH:end] = low[tail:].reshape(REACH, CY, NZ)
    wide_potential[end:, REACH:end] = high[tail:].reshape(REACH, CY, NZ)
    for plane in range(CX):
        slot, row = tail + plane // 2, plane % 2 * REACH
        wide_potential[REACH + plane, :REACH] = front[slot, row : row + REACH]
        wide_potential[REACH + plane, end:] = back[slot, row : row + REACH]
    wide_step(padded, wide_potential, along, None, once)

    def store(plane, total):
        twice[plane] = total

    narrow_step(once, wide_potential, along, field, store)
    rims_kernel(twice, None, next_low, next_high, next_front, next_back)


def second_pair_kernel(
    field, once, potential, low, high, front, back, low_corner, high_corner, along,
    given, kept, padded, wide,
):
    fill_padded(padded, field, low, high, front, back, low_corner, high_corner)
    wide_step(padded, potential, along, once, wide)
    side = lax.axis_index("band") % 2

    def store(plane, total):
        row = pl.multiple_of((plane // 4 * 2 + plane % 2) * CY, CY)
        mine = plane // 2 % 2 == side

        @pl.when(mine)
        def _():
            kept[pl.ds(row, CY)] = total

        @pl.when(jnp.logical_not(mine))
        def _():
            given[pl.ds(row, CY)] = total

    narrow_step(wide, potential, along, field, store)


def call(kernel, shapes, scratch, *operands):
    whole = pl.BlockSpec(memory_space=pltpu.VMEM)
    return pl.pallas_call(
        kernel,
        out_shape=[jax.ShapeDtypeStruct(shape, jnp.float32) for shape in shapes],
        in_specs=[whole] * len(operands),
        out_specs=[whole] * len(shapes),
        scratch_shapes=[pltpu.VMEM(shape, jnp.float32) for shape in scratch],
        compiler_params=pltpu.CompilerParams(vmem_limit_bytes=VMEM_BYTES),
    )(*operands)


def along_rows(rim, offset):
    route = [(i - offset * PY, i) for i in range(PX * PY) if 0 <= i // PY - offset < PX]
    return lax.ppermute(rim, "dom", route)


def along_columns(rim, offset):
    route = [(i - offset, i) for i in range(PX * PY) if 0 <= i % PY - offset < PY]
    return lax.ppermute(rim, "dom", route)


def halo(low, high, front, back):
    from_low, from_high = along_rows(high, 1), along_rows(low, -1)
    from_front, from_back = along_columns(back, 1), along_columns(front, -1)
    side_shape = (CX, DEEP, GROUP, NZ)
    front_side = from_front[: CX * DEEP].reshape(side_shape)
    back_side = from_back[: CX * DEEP].reshape(side_shape)

    def corners(planes):
        return jnp.concatenate(
            (front_side[planes, DEEP - REACH :], back_side[planes, :REACH]), axis=1
        )

    low_corner = along_rows(corners(slice(CX - REACH, CX)), 1)
    high_corner = along_rows(corners(slice(0, REACH)), -1)
    return from_low, from_high, from_front, from_back, low_corner, high_corner


def filtered_halves(orbitals, potential):
    field = orbitals.transpose(1, 2, 0, 3)
    along = jnp.asarray(third_dimension_matrix())
    tiles = DEEP * CY
    block = (CX, CY, GROUP, NZ)
    wide = (CX + 2 * REACH, CY + 2 * REACH, GROUP, NZ)
    padded = (CX + 2 * DEEP, CY + 2 * DEEP, GROUP, NZ)
    rims = call(rims_kernel, [(tiles + 8, GROUP, NZ)] * 4, [], field, potential)
    once, twice, wide_potential, *rims = call(
        first_pair_kernel,
        [wide, block, wide[:2] + (NZ,)] + [(tiles, GROUP, NZ)] * 4,
        [padded],
        field, potential, *halo(*rims), along,
    )
    return call(
        second_pair_kernel,
        [(tiles, GROUP, NZ)] * 2,
        [padded, wide],
        twice, once, wide_potential, *halo(*rims), along,
    )


def over_y(block):
    return lax.all_to_all(block, "band", 0, 0, axis_index_groups=Y_RINGS, tiled=True)


def across(block):
    return lax.ppermute(block, "band", [(i, i ^ 1) for i in range(8)])


def small_exchange(chunks, groups):
    return lax.all_to_all(chunks, ("band", "dom"), 0, 0, axis_index_groups=groups, tiled=True)


def spread(row, groups):
    count = len(groups[0])
    return small_exchange(jnp.broadcast_to(row, (count,) + row.shape[1:]), groups)


def summed_everywhere(gram):
    row = small_exchange(gram.reshape(32, 1, 128), SHEETS).sum(axis=0, keepdims=True)
    row = spread(row, Z_RINGS).sum(axis=0, keepdims=True)
    return spread(row, SHEETS).reshape(gram.shape)


def own_first(matrix, side):
    size = matrix.shape[0] // 2
    return jnp.where(side == 0, matrix, jnp.roll(matrix, (size, size), (0, 1)))


def by_group(matrix):
    return matrix.reshape(2, 4, 8, 2, 4, 8).transpose(1, 0, 2, 4, 3, 5).reshape(64, 64)


def by_side(matrix):
    return matrix.reshape(4, 2, 8, 4, 2, 8).transpose(1, 0, 2, 4, 3, 5).reshape(64, 64)


def orthonormal(gram):
    factor = jnp.linalg.cholesky(gram)
    return lax.linalg.triangular_solve(
        factor, jnp.eye(gram.shape[0], dtype=gram.dtype), left_side=True, lower=True
    )


def bands_by_rows(block):
    rows = block.shape[0] // 4
    return block.reshape(4, rows, GROUP, NZ).transpose(0, 2, 1, 3).reshape(4 * GROUP, rows, NZ)


def on_device(orbitals, potential):
    cell_count = CX * CY * NZ * lax.axis_size("dom")
    given, kept = filtered_halves(orbitals[:, 0], potential[0])
    side = lax.axis_index("band") % 2
    given = over_y(given)
    taken = across(given)
    kept = over_y(kept)
    kept_late, taken = lax.optimization_barrier((kept, taken))
    late_pair = lax.all_gather(kept_late, "band", axis=0, axis_index_groups=Z_PAIRS)
    taken_late = jnp.where(side == 0, late_pair[1], late_pair[0])
    count, half = 32, 32
    both = jnp.concatenate((bands_by_rows(kept), bands_by_rows(taken))).reshape(2 * count, -1)
    gram = jnp.dot(both, both.T, precision=lax.Precision.HIGHEST)
    gram = summed_everywhere(own_first(gram, side)) / cell_count
    inverse = orthonormal(by_group(gram))
    inverse = own_first(by_side(inverse), side)[:count]
    late = jnp.concatenate((bands_by_rows(given), bands_by_rows(taken_late))).reshape(2 * count, -1)
    early_out = jnp.dot(inverse, both, precision=lax.Precision.HIGHEST).reshape(count, half, NZ)
    late_out = jnp.dot(inverse, late, precision=lax.Precision.HIGHEST).reshape(count, half, NZ)
    first = jnp.where(side == 0, early_out, late_out)
    second = jnp.where(side == 0, late_out, early_out)
    rotated = lax.all_to_all(
        jnp.concatenate((first, second), axis=1), "band", 0, 1, axis_index_groups=Y_RINGS, tiled=True
    )
    return rotated.reshape(orbitals.shape)


def solution(mesh):
    placed = (P("band", "dom", None, None, None), P("dom", None, None, None))
    return jax.shard_map(
        on_device,
        mesh=mesh,
        in_specs=placed,
        out_specs=P("band", "dom", None, None, None),
        check_vma=False,
    )
```

time: 288 us -> 293 us (1.017)
  the two profiles are of different devices: /device:TPU:32 before, /device:TPU:1 now
where the time goes in v3:
time: 293 us; the launch traced here: 292 us
  waiting for transfers between devices  107 us (37%)
  starting transfers between devices  88.4 us (30%)
  blocking collectives  38.9 us (13%)
  Pallas kernels  19.1 us (7%)
  other arithmetic  14 us (5%)
  between operations  13.8 us (5%)
  local copies, waits for them, and re-layouts  7.86 us (3%)
    all_gather x1, waiting for transfers between devices, on_device(): lax.all_gather(kept_late, 'band', axis=0, axis_index_groups=Z_PAIRS)  47.4 us
    all_to_all x2, starting transfers between devices, small_exchange(): lax.all_to_all(chunks, ('band', 'dom'), 0, 0, axis_index_groups=groups, t...  38.1 us
    pallas_call x3, Pallas kernels, call(): pl.pallas_call(kernel, out_shape=[jax.ShapeDtypeStruct(shape, jnp.float32...  19.1 us
    ppermute x8, starting transfers between devices, along_rows(): return lax.ppermute(rim, 'dom', route)  18.7 us
    all_to_all x2, waiting for transfers between devices, small_exchange(): lax.all_to_all(chunks, ('band', 'dom'), 0, 0, axis_index_groups=groups, t...  17.5 us
    all_to_all x1, blocking collectives, on_device(): lax.all_to_all(jnp.concatenate((first, second), axis=1), 'band', 0, 1, ax...  16.5 us
    ppermute x8, waiting for transfers between devices, along_rows(): return lax.ppermute(rim, 'dom', route)  15.3 us
    ppermute x4, starting transfers between devices, along_columns(): return lax.ppermute(rim, 'dom', route)  14.5 us
  transfers between devices with their start and end apart: 17, of which 12 were waited for; matrix products, arithmetic and copies ran while one was open for 5% of the time, Pallas kernels for 0%

profile of v3, /device:TPU:1, one launch (start us, length us, event | category | flops | bytes accessed | tf_op | source)
XLA Modules:
  0.0 292.1 jit_solution(6590000821657763209)
XLA Ops:
  9.5 4.5 %collective-permute-start.2 = (f32[136,8,128]{2,1,0:T(8,128)S(1)}, f32[136,8,128]{2,1,0:T(8,128)S(1)}, u32[]{:S(2)}, u32[]{:S(2)}) collective-permute-start(f32[136,8,128]{2,1,0:T(8,128)S(1)} %get-tuple-element.22), channel_id=1, source_target_pairs={{0,1},{1,2},{2,3},{3,4},{4,5},{5,6},{6,7},{8,9},{9,10},{10,11},{11... | collective-permute-start | bytes 1671176 | tf_op jit(solution)/shard_map/ppermute | solution.py:211
  14.0 5.6 %collective-permute-start.3 = (f32[136,8,128]{2,1,0:T(8,128)S(1)}, f32[136,8,128]{2,1,0:T(8,128)S(1)}, u32[]{:S(2)}, u32[]{:S(2)}) collective-permute-start(f32[136,8,128]{2,1,0:T(8,128)S(1)} %get-tuple-element.23), channel_id=1, source_target_pairs={{1,0},{2,1},{3,2},{4,3},{5,4},{6,5},{7,6},{9,8},{10,9},{11,10},{12... | collective-permute-start | bytes 1671176 | tf_op jit(solution)/shard_map/ppermute | solution.py:211
  26.2 4.5 %collective-permute-start.4 = (f32[4,8,8,128]{3,2,1,0:T(8,128)S(1)}, f32[4,8,8,128]{3,2,1,0:T(8,128)S(1)}, u32[]{:S(2)}, u32[]{:S(2)}) collective-permute-start(f32[4,8,8,128]{3,2,1,0:T(8,128)S(1)} %pad_maximum_fusion.1), channel_id=1, source_target_pairs={{0,8},{1,9},{2,10},{3,11},{4,12},{5,13},{6,14},{7,15},{8,16},{9,17... | collective-permute-start | bytes 393224 | tf_op jit(solution)/shard_map/ppermute | solution.py:206
  33.2 4.2 %collective-permute-done.1.high = f32[136,8,128]{2,1,0:T(8,128)S(1)} collective-permute-done((f32[136,8,128]{2,1,0:T(8,128)S(1)}, f32[136,8,128]{2,1,0:T(8,128)S(1)}, u32[]{:S(2)}, u32[]{:S(2)}) %collective-permute-start.1) | collective-permute-done | bytes 557088 | tf_op jit(solution)/shard_map/ppermute | solution.py:206
  40.0 9.1 %shard_map.38 = (f32[24,24,8,128]{3,2,1,0:T(8,128)S(1)}, f32[16,16,8,128]{3,2,1,0:T(8,128)S(1)}, f32[24,24,128]{2,1,0:T(8,128)S(1)}, f32[128,8,128]{2,1,0:T(8,12...) custom-call(f32[16,16,8,128]{3,2,1,0:T(8,128)S(1)} %bitcast.90, ...), custom_call_target="tpu_custom_call" | custom-call | tf_op jit(solution)/shard_map/pallas_call | solution.py:194
  53.4 3.6 %collective-permute-start.6 = (f32[128,8,128]{2,1,0:T(8,128)S(1)}, f32[128,8,128]{2,1,0:T(8,128)S(1)}, u32[]{:S(2)}, u32[]{:S(2)}) collective-permute-start(f32[128,8,128]{2,1,0:T(8,128)S(1)} %get-tuple-element.27), channel_id=1, source_target_pairs={{0,8},{1,9},{2,10},{3,11},{4,12},{5,13},{6,14},{7,15},{8,16},{9,17... | collective-permute-start | bytes 1572872 | tf_op jit(solution)/shard_map/ppermute | solution.py:206
  58.4 4.0 %collective-permute-done.9.back = f32[128,8,128]{2,1,0:T(8,128)S(1)} collective-permute-done((f32[128,8,128]{2,1,0:T(8,128)S(1)}, f32[128,8,128]{2,1,0:T(8,128)S(1)}, u32[]{:S(2)}, u32[]{:S(2)}) %collective-permute-start.9) | collective-permute-done | bytes 524320 | tf_op jit(solution)/shard_map/ppermute | solution.py:211
  63.7 4.2 %collective-permute-start.10 = (f32[4,8,8,128]{3,2,1,0:T(8,128)S(1)}, f32[4,8,8,128]{3,2,1,0:T(8,128)S(1)}, u32[]{:S(2)}, u32[]{:S(2)}) collective-permute-start(f32[4,8,8,128]{3,2,1,0:T(8,128)S(1)} %pad_maximum_fusion.3), channel_id=1, source_target_pairs={{0,8},{1,9},{2,10},{3,11},{4,12},{5,13},{6,14},{7,15},{8,16},{9,17... | collective-permute-start | bytes 393224 | tf_op jit(solution)/shard_map/ppermute | solution.py:206
  67.9 4.7 %collective-permute-done.7.high = f32[128,8,128]{2,1,0:T(8,128)S(1)} collective-permute-done((f32[128,8,128]{2,1,0:T(8,128)S(1)}, f32[128,8,128]{2,1,0:T(8,128)S(1)}, u32[]{:S(2)}, u32[]{:S(2)}) %collective-permute-start.7) | collective-permute-done | bytes 524320 | tf_op jit(solution)/shard_map/ppermute | solution.py:206
  73.9 9.9 %shard_map.39 = (f32[128,8,128]{2,1,0:T(8,128)S(1)}, f32[128,8,128]{2,1,0:T(8,128)}) custom-call(f32[16,16,8,128]{3,2,1,0:T(8,128)S(1)} %get-tuple-element.24.field, f32[24,24,8,128]{3,2,1,0:T(8,128)S(1)} %get-tuple-element.25.once, f32[24,24,128]{2,1,0:T(8,128)S(1)} %get-tuple-element.26.potential, f32[128,8,128]{2,1,0:T(8,128)S(1)} %collective-permute-done.6.low, ...), custom_call_target="tpu_custom_call" | custom-call | tf_op jit(solution)/shard_map/pallas_call | solution.py:194
  83.8 12.0 %all_to_all.40 = f32[128,8,128]{2,1,0:T(8,128)S(1)} all-to-all(f32[128,8,128]{2,1,0:T(8,128)S(1)} %get-tuple-element.32), channel_id=1, replica_groups={{0,128,256,384},{64,192,320,448},{1,129,257,385},{65,193,321,449},{2,13..., dimensions={0} | all-to-all | bytes 1048576 | tf_op jit(solution)/shard_map/all_to_all | solution.py:254
  95.8 13.4 %collective-permute-start.12 = (f32[128,8,128]{2,1,0:T(8,128)S(1)}, f32[128,8,128]{2,1,0:T(8,128)S(1)}, u32[]{:S(2)}, u32[]{:S(2)}) collective-permute-start(f32[128,8,128]{2,1,0:T(8,128)S(1)} %all_to_all.40), channel_id=1, source_target_pairs={{0,64},{64,0},{128,192},{192,128},{256,320},{320,256},{384,448},{4... | collective-permute-start | bytes 1572872 | tf_op jit(solution)/shard_map/ppermute | solution.py:258
  109.3 3.5 %all-to-all-start = ((f32[128,8,128]{2,1,0:T(8,128)}), f32[128,8,128]{2,1,0:T(8,128)S(1)}, u32[]{:S(2)}, u32[]{:S(2)}) async-start(f32[128,8,128]{2,1,0:T(8,128)} %get-tuple-element.31), calls=%async_computation | async-start | bytes 1048576 | tf_op jit(solution)/shard_map/all_to_all | solution.py:254
  112.8 9.4 %all-to-all-done = f32[128,8,128]{2,1,0:T(8,128)S(1)} async-done(((f32[128,8,128]{2,1,0:T(8,128)}), f32[128,8,128]{2,1,0:T(8,128)S(1)}, u32[]{:S(2)}, u32[]{:S(2)}) %all-to-all-start) | async-done | bytes 524320 | tf_op jit(solution)/shard_map/all_to_all | solution.py:254
  122.3 10.7 %collective-permute-done.12 = f32[128,8,128]{2,1,0:T(8,128)S(1)} collective-permute-done((f32[128,8,128]{2,1,0:T(8,128)S(1)}, f32[128,8,128]{2,1,0:T(8,128)S(1)}, u32[]{:S(2)}, u32[]{:S(2)}) %collective-permute-start.12) | collective-permute-done | bytes 524320 | tf_op jit(solution)/shard_map/ppermute | solution.py:258
  134.3 10.4 %all_to_all.41 = f32[32,1,128]{2,1,0:T(1,128)S(1)} all-to-all(f32[32,1,128]{2,1,0:T(1,128)S(1)} %bitcast.108), channel_id=1, replica_groups={{0,1,2,3,4,5,6,7,128,129,130,131,132,133,134,135,256,257,258,259,260,26..., dimensions={0} | all-to-all | bytes 32768 | tf_op jit(solution)/shard_map/all_to_all | solution.py:262
  145.3 32.6 %all-to-all-start.3 = ((f32[16,1,128]{2,1,0:T(1,128)}), f32[16,1,128]{2,1,0:T(1,128)S(1)}, u32[]{:S(2)}, u32[]{:S(2)}) async-start(f32[16,1,128]{2,1,0:T(1,128)} %broadcast_in_dim.5), calls=%async_computation.3 | async-start | bytes 16384 | tf_op jit(solution)/shard_map/all_to_all | solution.py:262
  178.1 11.2 %all-to-all-done.3 = f32[16,1,128]{2,1,0:T(1,128)S(1)} async-done(((f32[16,1,128]{2,1,0:T(1,128)}), f32[16,1,128]{2,1,0:T(1,128)S(1)}, u32[]{:S(2)}, u32[]{:S(2)}) %all-to-all-start.3) | async-done | bytes 8224 | tf_op jit(solution)/shard_map/all_to_all | solution.py:262
  189.9 5.5 %all-to-all-start.4 = ((f32[32,1,128]{2,1,0:T(1,128)}), f32[32,1,128]{2,1,0:T(1,128)S(1)}, u32[]{:S(2)}, u32[]{:S(2)}) async-start(f32[32,1,128]{2,1,0:T(1,128)} %broadcast_in_dim.6), calls=%async_computation.4 | async-start | bytes 32768 | tf_op jit(solution)/shard_map/all_to_all | solution.py:262
  196.1 6.3 %all-to-all-done.4 = f32[32,1,128]{2,1,0:T(1,128)S(1)} async-done(((f32[32,1,128]{2,1,0:T(1,128)}), f32[32,1,128]{2,1,0:T(1,128)S(1)}, u32[]{:S(2)}, u32[]{:S(2)}) %all-to-all-start.4) | async-done | bytes 16416 | tf_op jit(solution)/shard_map/all_to_all | solution.py:262
  203.5 5.8 %cholesky.18 = f32[64,64]{1,0:T(8,128)S(1)} custom-call(f32[64,64]{1,0:T(8,128)S(1)} %fusion.12), custom_call_target="Cholesky" | custom-call | tf_op jit(solution)/shard_map/jit(cholesky)/cholesky | solution.py:290
  210.7 4.9 %custom-call.6 = f32[1,64,64]{1,2,0:T(8,128)S(1)} custom-call(f32[1,64,64]{2,1,0:T(8,128)S(1)} %fusion.9), custom_call_target="InvertDiagBlocksLowerTriangular" | custom-call | tf_op jit(solution)/shard_map/triangular_solve | solution.py:291
  217.0 47.4 %all-gather.3.cloned.1.call-done = f32[256,8,128]{2,1,0:T(8,128)} async-done(((f32[128,8,128]{2,1,0:T(8,128)}), f32[256,8,128]{2,1,0:T(8,128)}) %all-gather.3.cloned.1.call-update) | async-done | bytes 1048592 | tf_op jit(solution)/shard_map/all_gather | solution.py:309
  267.7 16.5 %all_to_all.42 = f32[32,64,128]{2,1,0:T(8,128)S(1)} all-to-all(f32[32,64,128]{2,1,0:T(8,128)S(1)} %copy.66), channel_id=1, replica_groups={{0,128,256,384},{64,192,320,448},{1,129,257,385},{65,193,321,449},{2,13..., dimensions={0} | all-to-all | bytes 2097152 | tf_op jit(solution)/shard_map/all_to_all | solution.py:322
  (81 shorter events, 34.3 us)
Async XLA Ops:
  6.5 33.4 %copy-start.1 = (f32[1,16,16,128]{3,2,1,0:T(8,128)S(1)}, f32[1,16,16,128]{3,2,1,0:T(8,128)}, u32[]{:S(2)}) copy-start(f32[1,16,16,128]{3,2,1,0:T(8,128)} %param.4) | copy-start | bytes 393220
  6.5 33.4 %copy-start.2 = (f32[128,128]{1,0:T(8,128)S(1)}, f32[128,128]{1,0:T(8,128)}, u32[]{:S(2)}) copy-start(f32[128,128]{1,0:T(8,128)} %constant.71.clone.along) | copy-start | bytes 196612
  8.4 0.9 copy-start
  9.5 12.8 %collective-permute-start.2 = (f32[136,8,128]{2,1,0:T(8,128)S(1)}, f32[136,8,128]{2,1,0:T(8,128)S(1)}, u32[]{:S(2)}, u32[]{:S(2)}) collective-permute-start(f32[136,8,128]{2,1,0:T(8,128)S(1)} %get-tuple-element.22), channel_id=1, source_target_pairs={{0,1},{1,2},{2,3},{3,4},{4,5},{5,6},{6,7},{8,9},{9,10},{10,11},{11... | collective-permute-start | bytes 1671176 | tf_op jit(solution)/shard_map/ppermute | solution.py:211
  14.0 10.9 %collective-permute-start.3 = (f32[136,8,128]{2,1,0:T(8,128)S(1)}, f32[136,8,128]{2,1,0:T(8,128)S(1)}, u32[]{:S(2)}, u32[]{:S(2)}) collective-permute-start(f32[136,8,128]{2,1,0:T(8,128)S(1)} %get-tuple-element.23), channel_id=1, source_target_pairs={{1,0},{2,1},{3,2},{4,3},{5,4},{6,5},{7,6},{9,8},{10,9},{11,10},{12... | collective-permute-start | bytes 1671176 | tf_op jit(solution)/shard_map/ppermute | solution.py:211
  19.6 13.6 %collective-permute-start = (f32[136,8,128]{2,1,0:T(8,128)S(1)}, f32[136,8,128]{2,1,0:T(8,128)S(1)}, u32[]{:S(2)}, u32[]{:S(2)}) collective-permute-start(f32[136,8,128]{2,1,0:T(8,128)S(1)} %get-tuple-element.20), channel_id=1, source_target_pairs={{0,8},{1,9},{2,10},{3,11},{4,12},{5,13},{6,14},{7,15},{8,16},{9,17... | collective-permute-start | bytes 1671176 | tf_op jit(solution)/shard_map/ppermute | solution.py:206
  20.9 16.5 %collective-permute-start.1 = (f32[136,8,128]{2,1,0:T(8,128)S(1)}, f32[136,8,128]{2,1,0:T(8,128)S(1)}, u32[]{:S(2)}, u32[]{:S(2)}) collective-permute-start(f32[136,8,128]{2,1,0:T(8,128)S(1)} %get-tuple-element.21), channel_id=1, source_target_pairs={{8,0},{9,1},{10,2},{11,3},{12,4},{13,5},{14,6},{15,7},{16,8},{17,9... | collective-permute-start | bytes 1671176 | tf_op jit(solution)/shard_map/ppermute | solution.py:206
  24.9 15.0 %collective-permute-start.5 = (f32[4,8,8,128]{3,2,1,0:T(8,128)S(1)}, f32[4,8,8,128]{3,2,1,0:T(8,128)S(1)}, u32[]{:S(2)}, u32[]{:S(2)}) collective-permute-start(f32[4,8,8,128]{3,2,1,0:T(8,128)S(1)} %pad_maximum_fusion.2), channel_id=1, source_target_pairs={{8,0},{9,1},{10,2},{11,3},{12,4},{13,5},{14,6},{15,7},{16,8},{17,9... | collective-permute-start | bytes 393224 | tf_op jit(solution)/shard_map/ppermute | solution.py:206
  26.2 13.7 %collective-permute-start.4 = (f32[4,8,8,128]{3,2,1,0:T(8,128)S(1)}, f32[4,8,8,128]{3,2,1,0:T(8,128)S(1)}, u32[]{:S(2)}, u32[]{:S(2)}) collective-permute-start(f32[4,8,8,128]{3,2,1,0:T(8,128)S(1)} %pad_maximum_fusion.1), channel_id=1, source_target_pairs={{0,8},{1,9},{2,10},{3,11},{4,12},{5,13},{6,14},{7,15},{8,16},{9,17... | collective-permute-start | bytes 393224 | tf_op jit(solution)/shard_map/ppermute | solution.py:206
  49.1 9.3 %collective-permute-start.8 = (f32[128,8,128]{2,1,0:T(8,128)S(1)}, f32[128,8,128]{2,1,0:T(8,128)S(1)}, u32[]{:S(2)}, u32[]{:S(2)}) collective-permute-start(f32[128,8,128]{2,1,0:T(8,128)S(1)} %get-tuple-element.29), channel_id=1, source_target_pairs={{0,1},{1,2},{2,3},{3,4},{4,5},{5,6},{6,7},{8,9},{9,10},{10,11},{11... | collective-permute-start | bytes 1572872 | tf_op jit(solution)/shard_map/ppermute | solution.py:211
  51.5 10.8 %collective-permute-start.9 = (f32[128,8,128]{2,1,0:T(8,128)S(1)}, f32[128,8,128]{2,1,0:T(8,128)S(1)}, u32[]{:S(2)}, u32[]{:S(2)}) collective-permute-start(f32[128,8,128]{2,1,0:T(8,128)S(1)} %get-tuple-element.30), channel_id=1, source_target_pairs={{1,0},{2,1},{3,2},{4,3},{5,4},{6,5},{7,6},{9,8},{10,9},{11,10},{12... | collective-permute-start | bytes 1572872 | tf_op jit(solution)/shard_map/ppermute | solution.py:211
  53.4 14.4 %collective-permute-start.6 = (f32[128,8,128]{2,1,0:T(8,128)S(1)}, f32[128,8,128]{2,1,0:T(8,128)S(1)}, u32[]{:S(2)}, u32[]{:S(2)}) collective-permute-start(f32[128,8,128]{2,1,0:T(8,128)S(1)} %get-tuple-element.27), channel_id=1, source_target_pairs={{0,8},{1,9},{2,10},{3,11},{4,12},{5,13},{6,14},{7,15},{8,16},{9,17... | collective-permute-start | bytes 1572872 | tf_op jit(solution)/shard_map/ppermute | solution.py:206
  57.0 15.5 %collective-permute-start.7 = (f32[128,8,128]{2,1,0:T(8,128)S(1)}, f32[128,8,128]{2,1,0:T(8,128)S(1)}, u32[]{:S(2)}, u32[]{:S(2)}) collective-permute-start(f32[128,8,128]{2,1,0:T(8,128)S(1)} %get-tuple-element.28), channel_id=1, source_target_pairs={{8,0},{9,1},{10,2},{11,3},{12,4},{13,5},{14,6},{15,7},{16,8},{17,9... | collective-permute-start | bytes 1572872 | tf_op jit(solution)/shard_map/ppermute | solution.py:206
  62.3 11.6 %collective-permute-start.11 = (f32[4,8,8,128]{3,2,1,0:T(8,128)S(1)}, f32[4,8,8,128]{3,2,1,0:T(8,128)S(1)}, u32[]{:S(2)}, u32[]{:S(2)}) collective-permute-start(f32[4,8,8,128]{3,2,1,0:T(8,128)S(1)} %pad_maximum_fusion.4), channel_id=1, source_target_pairs={{8,0},{9,1},{10,2},{11,3},{12,4},{13,5},{14,6},{15,7},{16,8},{17,9... | collective-permute-start | bytes 393224 | tf_op jit(solution)/shard_map/ppermute | solution.py:206
  63.7 10.3 %collective-permute-start.10 = (f32[4,8,8,128]{3,2,1,0:T(8,128)S(1)}, f32[4,8,8,128]{3,2,1,0:T(8,128)S(1)}, u32[]{:S(2)}, u32[]{:S(2)}) collective-permute-start(f32[4,8,8,128]{3,2,1,0:T(8,128)S(1)} %pad_maximum_fusion.3), channel_id=1, source_target_pairs={{0,8},{1,9},{2,10},{3,11},{4,12},{5,13},{6,14},{7,15},{8,16},{9,17... | collective-permute-start | bytes 393224 | tf_op jit(solution)/shard_map/ppermute | solution.py:206
  95.8 37.2 %collective-permute-start.12 = (f32[128,8,128]{2,1,0:T(8,128)S(1)}, f32[128,8,128]{2,1,0:T(8,128)S(1)}, u32[]{:S(2)}, u32[]{:S(2)}) collective-permute-start(f32[128,8,128]{2,1,0:T(8,128)S(1)} %all_to_all.40), channel_id=1, source_target_pairs={{0,64},{64,0},{128,192},{192,128},{256,320},{320,256},{384,448},{4... | collective-permute-start | bytes 1572872 | tf_op jit(solution)/shard_map/ppermute | solution.py:258
  109.3 12.9 %all-to-all-start = ((f32[128,8,128]{2,1,0:T(8,128)}), f32[128,8,128]{2,1,0:T(8,128)S(1)}, u32[]{:S(2)}, u32[]{:S(2)}) async-start(f32[128,8,128]{2,1,0:T(8,128)} %get-tuple-element.31), calls=%async_computation | async-start | bytes 1048576 | tf_op jit(solution)/shard_map/all_to_all | solution.py:254
  122.2 73.5 %copy-start.3 = (f32[128,8,128]{2,1,0:T(8,128)}, f32[128,8,128]{2,1,0:T(8,128)S(1)}, u32[]{:S(2)}) copy-start(f32[128,8,128]{2,1,0:T(8,128)S(1)} %all-to-all-done) | copy-start | bytes 1572868
  145.3 43.9 %all-to-all-start.3 = ((f32[16,1,128]{2,1,0:T(1,128)}), f32[16,1,128]{2,1,0:T(1,128)S(1)}, u32[]{:S(2)}, u32[]{:S(2)}) async-start(f32[16,1,128]{2,1,0:T(1,128)} %broadcast_in_dim.5), calls=%async_computation.3 | async-start | bytes 16384 | tf_op jit(solution)/shard_map/all_to_all | solution.py:262
  189.9 12.5 %all-to-all-start.4 = ((f32[32,1,128]{2,1,0:T(1,128)}), f32[32,1,128]{2,1,0:T(1,128)S(1)}, u32[]{:S(2)}, u32[]{:S(2)}) async-start(f32[32,1,128]{2,1,0:T(1,128)} %broadcast_in_dim.6), calls=%async_computation.4 | async-start | bytes 32768 | tf_op jit(solution)/shard_map/all_to_all | solution.py:262
  195.4 69.1 %all-gather.3.cloned.1.call-start = ((), (), s32[]{:S(2)}) async-start(), calls=%async_computation.6 | async-start | bytes 1572864 | tf_op jit(solution)/shard_map/all_gather | solution.py:309
  216.3 50.1 %copy-start.4 = (f32[128,8,128]{2,1,0:T(8,128)S(1)}, f32[128,8,128]{2,1,0:T(8,128)}, u32[]{:S(2)}) copy-start(f32[128,8,128]{2,1,0:T(8,128)} %copy-done.3) | copy-start | bytes 1572868
Sparse Core Ops, SparseCore 0:
  198.3 66.0 all-gather.2

commit v4 on v3

--- a/solution.py
+++ b/solution.py
@@ -1,3 +1,5 @@
+import functools
+
 import functools
 
 import jax
@@ -23,6 +25,8 @@
 GROUP = 8
 REACH = 4
 DEEP = 8
+BANDS = 64
+HALF = 32
 VMEM_BYTES = 40 * 2**20
 
 
@@ -31,7 +35,6 @@
 
 
 Y_RINGS = [[0, 2, 4, 6], [1, 3, 5, 7]]
-Z_PAIRS = [[0, 1], [2, 3], [4, 5], [6, 7]]
 SHEETS = [
     [member(y, z_hi, z_lo, plane) for y in range(4) for plane in range(8)]
     for z_hi in range(2)
@@ -267,62 +270,108 @@
     return small_exchange(jnp.broadcast_to(row, (count,) + row.shape[1:]), groups)
 
 
-def summed_everywhere(gram):
-    row = small_exchange(gram.reshape(32, 1, 128), SHEETS).sum(axis=0, keepdims=True)
-    row = spread(row, Z_RINGS).sum(axis=0, keepdims=True)
-    return spread(row, SHEETS).reshape(gram.shape)
-
-
-def own_first(matrix, side):
-    size = matrix.shape[0] // 2
-    return jnp.where(side == 0, matrix, jnp.roll(matrix, (size, size), (0, 1)))
-
-
-def by_group(matrix):
-    return matrix.reshape(2, 4, 8, 2, 4, 8).transpose(1, 0, 2, 4, 3, 5).reshape(64, 64)
-
-
-def by_side(matrix):
-    return matrix.reshape(4, 2, 8, 4, 2, 8).transpose(1, 0, 2, 4, 3, 5).reshape(64, 64)
-
-
-def orthonormal(gram):
-    factor = jnp.linalg.cholesky(gram)
-    return lax.linalg.triangular_solve(
-        factor, jnp.eye(gram.shape[0], dtype=gram.dtype), left_side=True, lower=True
-    )
-
-
-def bands_by_rows(block):
-    rows = block.shape[0] // 4
-    return block.reshape(4, rows, GROUP, NZ).transpose(0, 2, 1, 3).reshape(4 * GROUP, rows, NZ)
+def all_bands(mine, theirs, row, count, side):
+    columns = []
+    for offset in range(count):
+        tiles = []
+        for ring in range(4):
+            own, other = mine[ring * HALF + row + offset], theirs[ring * HALF + row + offset]
+            tiles += [jnp.where(side == 0, own, other), jnp.where(side == 0, other, own)]
+        columns.append(jnp.concatenate(tiles, axis=0))
+    return jnp.concatenate(columns, axis=1)
+
+
+def gram_kernel(kept, taken, gram):
+    side = lax.axis_index("band") % 2
+
+    def body(step, total):
+        bands = all_bands(kept, taken, step * 8, 8, side)
+        return total + lax.dot_general(
+            bands,
+            bands,
+            (((1,), (1,)), ((), ())),
+            precision=lax.Precision.HIGHEST,
+            preferred_element_type=jnp.float32,
+        )
+
+    total = lax.fori_loop(0, HALF // 8, body, jnp.zeros((BANDS, BANDS), jnp.float32))
+    gram[...] = jnp.concatenate((total[: BANDS // 2], total[BANDS // 2 :]), axis=1)
+
+
+def factor_kernel(cell_count, gram, inverse):
+    both = gram[...] * (1.0 / cell_count)
+    matrix = jnp.concatenate((both[:, :BANDS], both[:, BANDS:]), axis=0)
+    rows = lax.broadcasted_iota(jnp.int32, (BANDS, BANDS), 0)
+    columns = lax.broadcasted_iota(jnp.int32, (BANDS, BANDS), 1)
+    work = jnp.concatenate((matrix, jnp.where(rows == columns, 1.0, 0.0)), axis=1)
+    row_index = lax.broadcasted_iota(jnp.int32, (BANDS, 2 * BANDS), 0)
+    scales = jnp.zeros((BANDS, 2 * BANDS), jnp.float32)
+    for step in range(BANDS):
+        pivot_row = work[step : step + 1]
+        column = jnp.broadcast_to(work[:, step : step + 1], work.shape)
+        pivot = jnp.broadcast_to(column[step : step + 1], work.shape)
+        scales = jnp.where(row_index == step, pivot, scales)
+        below = jnp.where(row_index > step, column / pivot, 0.0)
+        work = work - below * pivot_row
+    inverse[...] = (work * lax.rsqrt(scales))[:, BANDS:]
+
+
+def rotation_kernel(inverse, kept, taken, given, late_0, late_1, late_2, rotated, taken_late):
+    side = lax.axis_index("band") % 2
+    place = 0
+    for late in (late_0, late_1, late_2):
+        taken_late[place : place + late.shape[0]] = late[...]
+        place += late.shape[0]
+    own = jnp.concatenate(
+        [inverse[pl.ds(pl.multiple_of((2 * ring + side) * GROUP, GROUP), GROUP)] for ring in range(4)],
+        axis=0,
+    )
+    for mine, theirs, half in ((kept, taken, side), (given, taken_late, 1 - side)):
+
+        def body(step, carry, mine=mine, theirs=theirs, half=half):
+            bands = all_bands(mine, theirs, step * 8, 8, side)
+            turned = jnp.dot(
+                own,
+                bands,
+                precision=lax.Precision.HIGHEST,
+                preferred_element_type=jnp.float32,
+            )
+            for offset in range(8):
+                for ring in range(4):
+                    rotated[ring * 2 * HALF + half * HALF + step * 8 + offset] = turned[
+                        ring * GROUP : (ring + 1) * GROUP, offset * NZ : (offset + 1) * NZ
+                    ]
+            return carry
+
+        lax.fori_loop(0, HALF // 8, body, 0)
 
 
 def on_device(orbitals, potential):
     cell_count = CX * CY * NZ * lax.axis_size("dom")
     given, kept = filtered_halves(orbitals[:, 0], potential[0])
-    side = lax.axis_index("band") % 2
     given = over_y(given)
     taken = across(given)
     kept = over_y(kept)
-    kept_late, taken = lax.optimization_barrier((kept, taken))
-    late_pair = lax.all_gather(kept_late, "band", axis=0, axis_index_groups=Z_PAIRS)
-    taken_late = jnp.where(side == 0, late_pair[1], late_pair[0])
-    count, half = 32, 32
-    both = jnp.concatenate((bands_by_rows(kept), bands_by_rows(taken))).reshape(2 * count, -1)
-    gram = jnp.dot(both, both.T, precision=lax.Precision.HIGHEST)
-    gram = summed_everywhere(own_first(gram, side)) / cell_count
-    inverse = orthonormal(by_group(gram))
-    inverse = own_first(by_side(inverse), side)[:count]
-    late = jnp.concatenate((bands_by_rows(given), bands_by_rows(taken_late))).reshape(2 * count, -1)
-    early_out = jnp.dot(inverse, both, precision=lax.Precision.HIGHEST).reshape(count, half, NZ)
-    late_out = jnp.dot(inverse, late, precision=lax.Precision.HIGHEST).reshape(count, half, NZ)
-    first = jnp.where(side == 0, early_out, late_out)
-    second = jnp.where(side == 0, late_out, early_out)
-    rotated = lax.all_to_all(
-        jnp.concatenate((first, second), axis=1), "band", 0, 1, axis_index_groups=Y_RINGS, tiled=True
-    )
-    return rotated.reshape(orbitals.shape)
+    kept, taken = lax.optimization_barrier((kept, taken))
+    first, second, third = kept[:48], kept[48:88], kept[88:]
+    late_0 = across(first)
+    (gram,) = call(gram_kernel, [(32, 128)], [], kept, taken)
+    row = small_exchange(gram[:, None], SHEETS).sum(axis=0, keepdims=True)
+    row, late_0, second = lax.optimization_barrier((row, late_0, second))
+    late_1 = across(second)
+    row = spread(row, Z_RINGS).sum(axis=0, keepdims=True)
+    row, late_1, third = lax.optimization_barrier((row, late_1, third))
+    late_2 = across(third)
+    gram = spread(row, SHEETS)[:, 0]
+    (inverse,) = call(functools.partial(factor_kernel, cell_count), [(BANDS, BANDS)], [], gram)
+    (rotated,) = call(
+        rotation_kernel,
+        [(CX * CY, GROUP, NZ)],
+        [(4 * HALF, GROUP, NZ)],
+        inverse, kept, taken, given, late_0, late_1, late_2,
+    )
+    rotated = over_y(rotated)
+    return rotated.transpose(1, 0, 2).reshape(orbitals.shape)
 
 
 def solution(mesh):

time: 293 us -> 257 us (0.88)
  waiting for transfers between devices: 107 us -> 39.7 us
  blocking collectives: 38.9 us -> 90.6 us
  other arithmetic: 14 us -> 0.11 us
  between operations: 13.8 us -> 0.29 us
  Pallas kernels: 19.1 us -> 31 us
  local copies, waits for them, and re-layouts: 7.86 us -> 4.11 us
    all_gather x1 -> x0, waiting for transfers between devices: 47.4 us -> none  [on_device(): lax.all_gather(kept_late, 'band', axis=0, axis_index_groups=Z_PAIRS)]
    all_to_all x1 -> x2, blocking collectives: 10.4 us -> 49.3 us  [small_exchange(): lax.all_to_all(chunks, ('band', 'dom'), 0, 0, axis_index_groups=groups, t...]
    ppermute x1 -> x4, starting transfers between devices: 13.4 us -> 48.3 us  [across(): return lax.ppermute(block, 'band', [(i, i ^ 1) for i in range(8)])]
    all_to_all x1 -> x3, blocking collectives: 12 us -> 41.3 us  [over_y(): lax.all_to_all(block, 'band', 0, 0, axis_index_groups=Y_RINGS, tiled=True)]
    all_to_all x2 -> x1, starting transfers between devices: 38.1 us -> 9.87 us  [small_exchange(): lax.all_to_all(chunks, ('band', 'dom'), 0, 0, axis_index_groups=groups, t...]
    all_to_all x2 -> x1, waiting for transfers between devices: 17.5 us -> 0.01 us  [small_exchange(): lax.all_to_all(chunks, ('band', 'dom'), 0, 0, axis_index_groups=groups, t...]
    all_to_all x1 -> x0, blocking collectives: 16.5 us -> none  [on_device(): lax.all_to_all(jnp.concatenate((first, second), axis=1), 'band', 0, 1, ax...]
    another operation x7 -> x0, other arithmetic: 12.2 us -> none  [the longest x4 6.66 us: orthonormal(): factor = jnp.linalg.cholesky(gram)]
  transfers between devices with their start and end apart: 17 -> 17, of which waited for: 12 -> 10; matrix products, arithmetic and copies ran while one was open for 5% -> 0% of each run, Pallas kernels for 0% -> 3%
where the time goes in v4:
time: 257 us; the launch traced here: 256 us
  blocking collectives  90.6 us (35%)
  starting transfers between devices  90.3 us (35%)
  waiting for transfers between devices  39.7 us (15%)
  Pallas kernels  31 us (12%)
  local copies, waits for them, and re-layouts  4.11 us (2%)
    all_to_all x2, blocking collectives, small_exchange(): lax.all_to_all(chunks, ('band', 'dom'), 0, 0, axis_index_groups=groups, t...  49.3 us
    ppermute x4, starting transfers between devices, across(): return lax.ppermute(block, 'band', [(i, i ^ 1) for i in range(8)])  48.3 us
    all_to_all x3, blocking collectives, over_y(): lax.all_to_all(block, 'band', 0, 0, axis_index_groups=Y_RINGS, tiled=True)  41.3 us
    pallas_call x6, Pallas kernels, call(): pl.pallas_call(kernel, out_shape=[jax.ShapeDtypeStruct(shape, jnp.float32...  31 us
    ppermute x8, starting transfers between devices, along_rows(): return lax.ppermute(rim, 'dom', route)  17.7 us
    ppermute x4, waiting for transfers between devices, across(): return lax.ppermute(block, 'band', [(i, i ^ 1) for i in range(8)])  16.7 us
    ppermute x8, waiting for transfers between devices, along_rows(): return lax.ppermute(rim, 'dom', route)  16.6 us
    ppermute x4, starting transfers between devices, along_columns(): return lax.ppermute(rim, 'dom', route)  14.5 us
  transfers between devices with their start and end apart: 17, of which 10 were waited for; matrix products, arithmetic and copies ran while one was open for 0% of the time, Pallas kernels for 3%

profile of v4, /device:TPU:1, one launch (start us, length us, event | category | flops | bytes accessed | tf_op | source)
XLA Modules:
  0.0 256.2 jit_solution(1620790769601847358)
XLA Ops:
  2.9 4.5 %collective-permute-start.2 = (f32[136,8,128]{2,1,0:T(8,128)S(1)}, f32[136,8,128]{2,1,0:T(8,128)S(1)}, u32[]{:S(2)}, u32[]{:S(2)}) collective-permute-start(f32[136,8,128]{2,1,0:T(8,128)S(1)} %get-tuple-element.28), channel_id=1, source_target_pairs={{0,1},{1,2},{2,3},{3,4},{4,5},{5,6},{6,7},{8,9},{9,10},{10,11},{11... | collective-permute-start | bytes 1671176 | tf_op jit(solution)/shard_map/ppermute | solution.py:214
  7.5 5.6 %collective-permute-start.3 = (f32[136,8,128]{2,1,0:T(8,128)S(1)}, f32[136,8,128]{2,1,0:T(8,128)S(1)}, u32[]{:S(2)}, u32[]{:S(2)}) collective-permute-start(f32[136,8,128]{2,1,0:T(8,128)S(1)} %get-tuple-element.29), channel_id=1, source_target_pairs={{1,0},{2,1},{3,2},{4,3},{5,4},{6,5},{7,6},{9,8},{10,9},{11,10},{12... | collective-permute-start | bytes 1671176 | tf_op jit(solution)/shard_map/ppermute | solution.py:214
  15.8 2.6 collective-permute-done.3.back
  18.4 3.8 %collective-permute-start.4 = (f32[4,8,8,128]{3,2,1,0:T(8,128)S(1)}, f32[4,8,8,128]{3,2,1,0:T(8,128)S(1)}, u32[]{:S(2)}, u32[]{:S(2)}) collective-permute-start(f32[4,8,8,128]{3,2,1,0:T(8,128)S(1)} %pad_maximum_fusion), channel_id=1, source_target_pairs={{0,8},{1,9},{2,10},{3,11},{4,12},{5,13},{6,14},{7,15},{8,16},{9,17... | collective-permute-start | bytes 393224 | tf_op jit(solution)/shard_map/ppermute | solution.py:209
  23.6 3.1 %collective-permute-done.low = f32[136,8,128]{2,1,0:T(8,128)S(1)} collective-permute-done((f32[136,8,128]{2,1,0:T(8,128)S(1)}, f32[136,8,128]{2,1,0:T(8,128)S(1)}, u32[]{:S(2)}, u32[]{:S(2)}) %collective-permute-start) | collective-permute-done | bytes 557088 | tf_op jit(solution)/shard_map/ppermute | solution.py:209
  26.7 4.2 %collective-permute-done.1.high = f32[136,8,128]{2,1,0:T(8,128)S(1)} collective-permute-done((f32[136,8,128]{2,1,0:T(8,128)S(1)}, f32[136,8,128]{2,1,0:T(8,128)S(1)}, u32[]{:S(2)}, u32[]{:S(2)}) %collective-permute-start.1) | collective-permute-done | bytes 557088 | tf_op jit(solution)/shard_map/ppermute | solution.py:209
  33.4 9.0 %shard_map.38 = (f32[24,24,8,128]{3,2,1,0:T(8,128)S(1)}, f32[16,16,8,128]{3,2,1,0:T(8,128)S(1)}, f32[24,24,128]{2,1,0:T(8,128)S(1)}, f32[128,8,128]{2,1,0:T(8,12...) custom-call(f32[16,16,8,128]{3,2,1,0:T(8,128)S(1)} %bitcast.23, ...), custom_call_target="tpu_custom_call" | custom-call | tf_op jit(solution)/shard_map/pallas_call | solution.py:197
  46.8 3.7 %collective-permute-start.6 = (f32[128,8,128]{2,1,0:T(8,128)S(1)}, f32[128,8,128]{2,1,0:T(8,128)S(1)}, u32[]{:S(2)}, u32[]{:S(2)}) collective-permute-start(f32[128,8,128]{2,1,0:T(8,128)S(1)} %get-tuple-element.33), channel_id=1, source_target_pairs={{0,8},{1,9},{2,10},{3,11},{4,12},{5,13},{6,14},{7,15},{8,16},{9,17... | collective-permute-start | bytes 1572872 | tf_op jit(solution)/shard_map/ppermute | solution.py:209
  51.8 3.8 %collective-permute-done.9.back = f32[128,8,128]{2,1,0:T(8,128)S(1)} collective-permute-done((f32[128,8,128]{2,1,0:T(8,128)S(1)}, f32[128,8,128]{2,1,0:T(8,128)S(1)}, u32[]{:S(2)}, u32[]{:S(2)}) %collective-permute-start.9) | collective-permute-done | bytes 524320 | tf_op jit(solution)/shard_map/ppermute | solution.py:214
  55.7 3.7 %collective-permute-start.10 = (f32[4,8,8,128]{3,2,1,0:T(8,128)S(1)}, f32[4,8,8,128]{3,2,1,0:T(8,128)S(1)}, u32[]{:S(2)}, u32[]{:S(2)}) collective-permute-start(f32[4,8,8,128]{3,2,1,0:T(8,128)S(1)} %pad_maximum_fusion.2), channel_id=1, source_target_pairs={{0,8},{1,9},{2,10},{3,11},{4,12},{5,13},{6,14},{7,15},{8,16},{9,17... | collective-permute-start | bytes 393224 | tf_op jit(solution)/shard_map/ppermute | solution.py:209
  61.2 4.8 %collective-permute-done.7.high = f32[128,8,128]{2,1,0:T(8,128)S(1)} collective-permute-done((f32[128,8,128]{2,1,0:T(8,128)S(1)}, f32[128,8,128]{2,1,0:T(8,128)S(1)}, u32[]{:S(2)}, u32[]{:S(2)}) %collective-permute-start.7) | collective-permute-done | bytes 524320 | tf_op jit(solution)/shard_map/ppermute | solution.py:209
  67.4 9.1 %shard_map.39 = (f32[128,8,128]{2,1,0:T(8,128)S(1)}, f32[128,8,128]{2,1,0:T(8,128)S(1)}) custom-call(f32[16,16,8,128]{3,2,1,0:T(8,128)S(1)} %get-tuple-element.30.field, f32[24,24,8,128]{3,2,1,0:T(8,128)S(1)} %get-tuple-element.31.once, f32[24,24,128]{2,1,0:T(8,128)S(1)} %get-tuple-element.32.potential, f32[128,8,128]{2,1,0:T(8,128)S(1)} %collective-permute-done.6.low, ...), custom_call_target="tpu_custom_call" | custom-call | tf_op jit(solution)/shard_map/pallas_call | solution.py:197
  76.5 12.2 %all_to_all.30.given = f32[128,8,128]{2,1,0:T(8,128)S(1)} all-to-all(f32[128,8,128]{2,1,0:T(8,128)S(1)} %get-tuple-element.38), channel_id=1, replica_groups={{0,128,256,384},{64,192,320,448},{1,129,257,385},{65,193,321,449},{2,13..., dimensions={0} | all-to-all | bytes 1048576 | tf_op jit(solution)/shard_map/all_to_all | solution.py:257
  88.6 13.3 %collective-permute-start.12 = (f32[128,8,128]{2,1,0:T(8,128)S(1)}, f32[128,8,128]{2,1,0:T(8,128)S(1)}, u32[]{:S(2)}, u32[]{:S(2)}) collective-permute-start(f32[128,8,128]{2,1,0:T(8,128)S(1)} %all_to_all.30.given), channel_id=1, source_target_pairs={{0,64},{64,0},{128,192},{192,128},{256,320},{320,256},{384,448},{4... | collective-permute-start | bytes 1572872 | tf_op jit(solution)/shard_map/ppermute | solution.py:261
  101.9 11.9 %all_to_all.31.kept = f32[128,8,128]{2,1,0:T(8,128)S(1)} all-to-all(f32[128,8,128]{2,1,0:T(8,128)S(1)} %get-tuple-element.37), channel_id=1, replica_groups={{0,128,256,384},{64,192,320,448},{1,129,257,385},{65,193,321,449},{2,13..., dimensions={0} | all-to-all | bytes 1048576 | tf_op jit(solution)/shard_map/all_to_all | solution.py:257
  113.8 11.7 %collective-permute-done.12.taken = f32[128,8,128]{2,1,0:T(8,128)S(1)} collective-permute-done((f32[128,8,128]{2,1,0:T(8,128)S(1)}, f32[128,8,128]{2,1,0:T(8,128)S(1)}, u32[]{:S(2)}, u32[]{:S(2)}) %collective-permute-start.12) | collective-permute-done | bytes 524320 | tf_op jit(solution)/shard_map/ppermute | solution.py:261
  127.7 9.9 %all-to-all-start.2 = ((f32[32,1,128]{2,1,0:T(1,128)}), f32[32,1,128]{2,1,0:T(1,128)S(1)}, u32[]{:S(2)}, u32[]{:S(2)}) async-start(f32[32,1,128]{2,1,0:T(1,128)} %bitcast.9), calls=%async_computation.2 | async-start | bytes 32768 | tf_op jit(solution)/shard_map/all_to_all | solution.py:265
  137.5 20.7 %collective-permute-start.13 = (f32[48,8,128]{2,1,0:T(8,128)S(1)}, f32[48,8,128]{2,1,0:T(8,128)S(1)}, u32[]{:S(2)}, u32[]{:S(2)}) collective-permute-start(f32[48,8,128]{2,1,0:T(8,128)S(1)} %slice.49), channel_id=1, source_target_pairs={{0,64},{64,0},{128,192},{192,128},{256,320},{320,256},{384,448},{4... | collective-permute-start | bytes 589832 | tf_op jit(solution)/shard_map/ppermute | solution.py:261
  158.4 5.0 %collective-permute-done.13.late_0 = f32[48,8,128]{2,1,0:T(8,128)S(1)} collective-permute-done((f32[48,8,128]{2,1,0:T(8,128)S(1)}, f32[48,8,128]{2,1,0:T(8,128)S(1)}, u32[]{:S(2)}, u32[]{:S(2)}) %collective-permute-start.13) | collective-permute-done | bytes 196640 | tf_op jit(solution)/shard_map/ppermute | solution.py:261
  163.4 11.7 %collective-permute-start.14 = (f32[40,8,128]{2,1,0:T(8,128)S(1)}, f32[40,8,128]{2,1,0:T(8,128)S(1)}, u32[]{:S(2)}, u32[]{:S(2)}) collective-permute-start(f32[40,8,128]{2,1,0:T(8,128)S(1)} %get-tuple-element.42), channel_id=1, source_target_pairs={{0,64},{64,0},{128,192},{192,128},{256,320},{320,256},{384,448},{4... | collective-permute-start | bytes 491528 | tf_op jit(solution)/shard_map/ppermute | solution.py:261
  175.2 32.6 %all_to_all.32 = f32[16,1,128]{2,1,0:T(1,128)S(1)} all-to-all(f32[16,1,128]{2,1,0:T(1,128)S(1)} %broadcast_in_dim.26), channel_id=1, replica_groups={{0,8,16,24,32,40,48,56,64,72,80,88,96,104,112,120},{1,9,17,25,33,41,49,..., dimensions={0} | all-to-all | bytes 16384 | tf_op jit(solution)/shard_map/all_to_all | solution.py:265
  210.3 16.7 %all_to_all.33 = f32[32,1,128]{2,1,0:T(1,128)S(1)} all-to-all(f32[32,1,128]{2,1,0:T(1,128)S(1)} %broadcast_in_dim.29), channel_id=1, replica_groups={{0,1,2,3,4,5,6,7,128,129,130,131,132,133,134,135,256,257,258,259,260,26..., dimensions={0} | all-to-all | bytes 32768 | tf_op jit(solution)/shard_map/all_to_all | solution.py:265
  227.1 8.5 %shard_map.41.inverse = f32[64,64]{1,0:T(8,128)S(1)} custom-call(f32[32,128]{1,0:T(8,128)S(1)} %bitcast.28), custom_call_target="tpu_custom_call" | custom-call | tf_op jit(solution)/shard_map/pallas_call | solution.py:197
  237.7 17.3 %all_to_all.34 = f32[256,8,128]{2,1,0:T(8,128)S(1)} all-to-all(f32[256,8,128]{2,1,0:T(8,128)S(1)} %shard_map.42), channel_id=1, replica_groups={{0,128,256,384},{64,192,320,448},{1,129,257,385},{65,193,321,449},{2,13..., dimensions={0} | all-to-all | bytes 2097152 | tf_op jit(solution)/shard_map/all_to_all | solution.py:257
  (44 shorter events, 26.5 us)
Async XLA Ops:
  0.0 33.4 %copy-start.1 = (f32[1,16,16,128]{3,2,1,0:T(8,128)S(1)}, f32[1,16,16,128]{3,2,1,0:T(8,128)}, u32[]{:S(2)}) copy-start(f32[1,16,16,128]{3,2,1,0:T(8,128)} %param.4) | copy-start | bytes 393220
  0.0 33.4 %copy-start.2 = (f32[128,128]{1,0:T(8,128)S(1)}, f32[128,128]{1,0:T(8,128)}, u32[]{:S(2)}) copy-start(f32[128,128]{1,0:T(8,128)} %constant.4.clone.along) | copy-start | bytes 196612
  1.9 0.9 copy-start
  2.9 12.8 %collective-permute-start.2 = (f32[136,8,128]{2,1,0:T(8,128)S(1)}, f32[136,8,128]{2,1,0:T(8,128)S(1)}, u32[]{:S(2)}, u32[]{:S(2)}) collective-permute-start(f32[136,8,128]{2,1,0:T(8,128)S(1)} %get-tuple-element.28), channel_id=1, source_target_pairs={{0,1},{1,2},{2,3},{3,4},{4,5},{5,6},{6,7},{8,9},{9,10},{10,11},{11... | collective-permute-start | bytes 1671176 | tf_op jit(solution)/shard_map/ppermute | solution.py:214
  7.5 10.9 %collective-permute-start.3 = (f32[136,8,128]{2,1,0:T(8,128)S(1)}, f32[136,8,128]{2,1,0:T(8,128)S(1)}, u32[]{:S(2)}, u32[]{:S(2)}) collective-permute-start(f32[136,8,128]{2,1,0:T(8,128)S(1)} %get-tuple-element.29), channel_id=1, source_target_pairs={{1,0},{2,1},{3,2},{4,3},{5,4},{6,5},{7,6},{9,8},{10,9},{11,10},{12... | collective-permute-start | bytes 1671176 | tf_op jit(solution)/shard_map/ppermute | solution.py:214
  13.1 13.6 %collective-permute-start = (f32[136,8,128]{2,1,0:T(8,128)S(1)}, f32[136,8,128]{2,1,0:T(8,128)S(1)}, u32[]{:S(2)}, u32[]{:S(2)}) collective-permute-start(f32[136,8,128]{2,1,0:T(8,128)S(1)} %get-tuple-element.26), channel_id=1, source_target_pairs={{0,8},{1,9},{2,10},{3,11},{4,12},{5,13},{6,14},{7,15},{8,16},{9,17... | collective-permute-start | bytes 1671176 | tf_op jit(solution)/shard_map/ppermute | solution.py:209
  14.4 16.5 %collective-permute-start.1 = (f32[136,8,128]{2,1,0:T(8,128)S(1)}, f32[136,8,128]{2,1,0:T(8,128)S(1)}, u32[]{:S(2)}, u32[]{:S(2)}) collective-permute-start(f32[136,8,128]{2,1,0:T(8,128)S(1)} %get-tuple-element.27), channel_id=1, source_target_pairs={{8,0},{9,1},{10,2},{11,3},{12,4},{13,5},{14,6},{15,7},{16,8},{17,9... | collective-permute-start | bytes 1671176 | tf_op jit(solution)/shard_map/ppermute | solution.py:209
  18.4 12.5 %collective-permute-start.4 = (f32[4,8,8,128]{3,2,1,0:T(8,128)S(1)}, f32[4,8,8,128]{3,2,1,0:T(8,128)S(1)}, u32[]{:S(2)}, u32[]{:S(2)}) collective-permute-start(f32[4,8,8,128]{3,2,1,0:T(8,128)S(1)} %pad_maximum_fusion), channel_id=1, source_target_pairs={{0,8},{1,9},{2,10},{3,11},{4,12},{5,13},{6,14},{7,15},{8,16},{9,17... | collective-permute-start | bytes 393224 | tf_op jit(solution)/shard_map/ppermute | solution.py:209
  22.3 11.2 %collective-permute-start.5 = (f32[4,8,8,128]{3,2,1,0:T(8,128)S(1)}, f32[4,8,8,128]{3,2,1,0:T(8,128)S(1)}, u32[]{:S(2)}, u32[]{:S(2)}) collective-permute-start(f32[4,8,8,128]{3,2,1,0:T(8,128)S(1)} %pad_maximum_fusion.1), channel_id=1, source_target_pairs={{8,0},{9,1},{10,2},{11,3},{12,4},{13,5},{14,6},{15,7},{16,8},{17,9... | collective-permute-start | bytes 393224 | tf_op jit(solution)/shard_map/ppermute | solution.py:209
  42.4 9.4 %collective-permute-start.8 = (f32[128,8,128]{2,1,0:T(8,128)S(1)}, f32[128,8,128]{2,1,0:T(8,128)S(1)}, u32[]{:S(2)}, u32[]{:S(2)}) collective-permute-start(f32[128,8,128]{2,1,0:T(8,128)S(1)} %get-tuple-element.35), channel_id=1, source_target_pairs={{0,1},{1,2},{2,3},{3,4},{4,5},{5,6},{6,7},{8,9},{9,10},{10,11},{11... | collective-permute-start | bytes 1572872 | tf_op jit(solution)/shard_map/ppermute | solution.py:214
  44.9 10.8 %collective-permute-start.9 = (f32[128,8,128]{2,1,0:T(8,128)S(1)}, f32[128,8,128]{2,1,0:T(8,128)S(1)}, u32[]{:S(2)}, u32[]{:S(2)}) collective-permute-start(f32[128,8,128]{2,1,0:T(8,128)S(1)} %get-tuple-element.36), channel_id=1, source_target_pairs={{1,0},{2,1},{3,2},{4,3},{5,4},{6,5},{7,6},{9,8},{10,9},{11,10},{12... | collective-permute-start | bytes 1572872 | tf_op jit(solution)/shard_map/ppermute | solution.py:214
  46.8 14.4 %collective-permute-start.6 = (f32[128,8,128]{2,1,0:T(8,128)S(1)}, f32[128,8,128]{2,1,0:T(8,128)S(1)}, u32[]{:S(2)}, u32[]{:S(2)}) collective-permute-start(f32[128,8,128]{2,1,0:T(8,128)S(1)} %get-tuple-element.33), channel_id=1, source_target_pairs={{0,8},{1,9},{2,10},{3,11},{4,12},{5,13},{6,14},{7,15},{8,16},{9,17... | collective-permute-start | bytes 1572872 | tf_op jit(solution)/shard_map/ppermute | solution.py:209
  50.5 15.5 %collective-permute-start.7 = (f32[128,8,128]{2,1,0:T(8,128)S(1)}, f32[128,8,128]{2,1,0:T(8,128)S(1)}, u32[]{:S(2)}, u32[]{:S(2)}) collective-permute-start(f32[128,8,128]{2,1,0:T(8,128)S(1)} %get-tuple-element.34), channel_id=1, source_target_pairs={{8,0},{9,1},{10,2},{11,3},{12,4},{13,5},{14,6},{15,7},{16,8},{17,9... | collective-permute-start | bytes 1572872 | tf_op jit(solution)/shard_map/ppermute | solution.py:209
  55.7 10.3 %collective-permute-start.10 = (f32[4,8,8,128]{3,2,1,0:T(8,128)S(1)}, f32[4,8,8,128]{3,2,1,0:T(8,128)S(1)}, u32[]{:S(2)}, u32[]{:S(2)}) collective-permute-start(f32[4,8,8,128]{3,2,1,0:T(8,128)S(1)} %pad_maximum_fusion.2), channel_id=1, source_target_pairs={{0,8},{1,9},{2,10},{3,11},{4,12},{5,13},{6,14},{7,15},{8,16},{9,17... | collective-permute-start | bytes 393224 | tf_op jit(solution)/shard_map/ppermute | solution.py:209
  59.4 8.0 %collective-permute-start.11 = (f32[4,8,8,128]{3,2,1,0:T(8,128)S(1)}, f32[4,8,8,128]{3,2,1,0:T(8,128)S(1)}, u32[]{:S(2)}, u32[]{:S(2)}) collective-permute-start(f32[4,8,8,128]{3,2,1,0:T(8,128)S(1)} %pad_maximum_fusion.3), channel_id=1, source_target_pairs={{8,0},{9,1},{10,2},{11,3},{12,4},{13,5},{14,6},{15,7},{16,8},{17,9... | collective-permute-start | bytes 393224 | tf_op jit(solution)/shard_map/ppermute | solution.py:209
  88.6 36.9 %collective-permute-start.12 = (f32[128,8,128]{2,1,0:T(8,128)S(1)}, f32[128,8,128]{2,1,0:T(8,128)S(1)}, u32[]{:S(2)}, u32[]{:S(2)}) collective-permute-start(f32[128,8,128]{2,1,0:T(8,128)S(1)} %all_to_all.30.given), channel_id=1, source_target_pairs={{0,64},{64,0},{128,192},{192,128},{256,320},{320,256},{384,448},{4... | collective-permute-start | bytes 1572872 | tf_op jit(solution)/shard_map/ppermute | solution.py:261
  127.7 30.7 %all-to-all-start.2 = ((f32[32,1,128]{2,1,0:T(1,128)}), f32[32,1,128]{2,1,0:T(1,128)S(1)}, u32[]{:S(2)}, u32[]{:S(2)}) async-start(f32[32,1,128]{2,1,0:T(1,128)} %bitcast.9), calls=%async_computation.2 | async-start | bytes 32768 | tf_op jit(solution)/shard_map/all_to_all | solution.py:265
  137.5 25.9 %collective-permute-start.13 = (f32[48,8,128]{2,1,0:T(8,128)S(1)}, f32[48,8,128]{2,1,0:T(8,128)S(1)}, u32[]{:S(2)}, u32[]{:S(2)}) collective-permute-start(f32[48,8,128]{2,1,0:T(8,128)S(1)} %slice.49), channel_id=1, source_target_pairs={{0,64},{64,0},{128,192},{192,128},{256,320},{320,256},{384,448},{4... | collective-permute-start | bytes 589832 | tf_op jit(solution)/shard_map/ppermute | solution.py:261
  163.4 44.4 %collective-permute-start.14 = (f32[40,8,128]{2,1,0:T(8,128)S(1)}, f32[40,8,128]{2,1,0:T(8,128)S(1)}, u32[]{:S(2)}, u32[]{:S(2)}) collective-permute-start(f32[40,8,128]{2,1,0:T(8,128)S(1)} %get-tuple-element.42), channel_id=1, source_target_pairs={{0,64},{64,0},{128,192},{192,128},{256,320},{320,256},{384,448},{4... | collective-permute-start | bytes 491528 | tf_op jit(solution)/shard_map/ppermute | solution.py:261
  207.8 27.8 %collective-permute-start.15 = (f32[40,8,128]{2,1,0:T(8,128)S(1)}, f32[40,8,128]{2,1,0:T(8,128)S(1)}, u32[]{:S(2)}, u32[]{:S(2)}) collective-permute-start(f32[40,8,128]{2,1,0:T(8,128)S(1)} %get-tuple-element.46), channel_id=1, source_target_pairs={{0,64},{64,0},{128,192},{192,128},{256,320},{320,256},{384,448},{4... | collective-permute-start | bytes 491528 | tf_op jit(solution)/shard_map/ppermute | solution.py:261

commit v5 on v4

--- a/solution.py
+++ b/solution.py
@@ -56,14 +56,24 @@
     return matrix.astype(np.float32)
 
 
+def parts(matrix):
+    high = matrix.astype(jnp.bfloat16)
+    return high, (matrix - high.astype(jnp.float32)).astype(jnp.bfloat16)
+
+
+def product(left, right, contract=(1, 0)):
+    def one(a, b):
+        return lax.dot_general(
+            a, b, (((contract[0],), (contract[1],)), ((), ())), preferred_element_type=jnp.float32
+        )
+
+    (left_high, left_low), (right_high, right_low) = parts(left), parts(right)
+    return one(left_high, right_high) + (one(left_low, right_high) + one(left_high, right_low))
+
+
 def scaled_hamiltonian(field, potential, along, plane, first, count, origin):
     here = field[plane, pl.ds(first, count)]
-    total = jnp.dot(
-        here.reshape(count * GROUP, NZ),
-        along[...],
-        precision=lax.Precision.HIGHEST,
-        preferred_element_type=jnp.float32,
-    ).reshape(count, GROUP, NZ)
+    total = product(here.reshape(count * GROUP, NZ), along[...]).reshape(count, GROUP, NZ)
     for offset in range(1, REACH + 1):
         total += SIDE_STEP[offset] * (
             (field[plane + offset, pl.ds(first, count)] + field[plane - offset, pl.ds(first, count)])
@@ -133,8 +143,8 @@
         later[layer + CX + REACH, REACH : REACH + CY] = value(layer + CX, 0, CY) * keep_high
         return carry
 
-    lax.fori_loop(0, CX, middle, 0)
-    lax.fori_loop(0, REACH, outer, 0)
+    lax.fori_loop(0, CX, middle, 0, unroll=True)
+    lax.fori_loop(0, REACH, outer, 0, unroll=True)
 
 
 def narrow_step(wide, potential, along, earlier, store):
@@ -143,7 +153,7 @@
         store(plane, 2.0 * total - earlier[plane])
         return carry
 
-    lax.fori_loop(0, CX, body, 0)
+    lax.fori_loop(0, CX, body, 0, unroll=True)
 
 
 def first_pair_kernel(
@@ -283,18 +293,10 @@
 
 def gram_kernel(kept, taken, gram):
     side = lax.axis_index("band") % 2
-
-    def body(step, total):
+    total = jnp.zeros((BANDS, BANDS), jnp.float32)
+    for step in range(HALF // 8):
         bands = all_bands(kept, taken, step * 8, 8, side)
-        return total + lax.dot_general(
-            bands,
-            bands,
-            (((1,), (1,)), ((), ())),
-            precision=lax.Precision.HIGHEST,
-            preferred_element_type=jnp.float32,
-        )
-
-    total = lax.fori_loop(0, HALF // 8, body, jnp.zeros((BANDS, BANDS), jnp.float32))
+        total = total + product(bands, bands, (1, 1))
     gram[...] = jnp.concatenate((total[: BANDS // 2], total[BANDS // 2 :]), axis=1)
 
 
@@ -316,34 +318,40 @@
     inverse[...] = (work * lax.rsqrt(scales))[:, BANDS:]
 
 
-def rotation_kernel(inverse, kept, taken, given, late_0, late_1, late_2, rotated, taken_late):
+def rotation_kernel(inverse, mine, *rest):
+    theirs, rotated = rest[:-1], rest[-1]
+    if len(theirs) > 1:
+        *pieces, rotated, theirs = rest
+        place = 0
+        for piece in pieces:
+            theirs[place : place + piece.shape[0]] = piece[...]
+            place += piece.shape[0]
+    else:
+        theirs = theirs[0]
     side = lax.axis_index("band") % 2
-    place = 0
-    for late in (late_0, late_1, late_2):
-        taken_late[place : place + late.shape[0]] = late[...]
-        place += late.shape[0]
     own = jnp.concatenate(
         [inverse[pl.ds(pl.multiple_of((2 * ring + side) * GROUP, GROUP), GROUP)] for ring in range(4)],
         axis=0,
     )
-    for mine, theirs, half in ((kept, taken, side), (given, taken_late, 1 - side)):
-
-        def body(step, carry, mine=mine, theirs=theirs, half=half):
-            bands = all_bands(mine, theirs, step * 8, 8, side)
-            turned = jnp.dot(
-                own,
-                bands,
-                precision=lax.Precision.HIGHEST,
-                preferred_element_type=jnp.float32,
-            )
-            for offset in range(8):
-                for ring in range(4):
-                    rotated[ring * 2 * HALF + half * HALF + step * 8 + offset] = turned[
-                        ring * GROUP : (ring + 1) * GROUP, offset * NZ : (offset + 1) * NZ
-                    ]
-            return carry
-
-        lax.fori_loop(0, HALF // 8, body, 0)
+    for step in range(HALF // 8):
+        bands = all_bands(mine, theirs, step * 8, 8, side)
+        turned = product(own, bands)
+        for offset in range(8):
+            for ring in range(4):
+                rotated[ring * HALF + step * 8 + offset] = turned[
+                    ring * GROUP : (ring + 1) * GROUP, offset * NZ : (offset + 1) * NZ
+                ]
+
+
+def placing_kernel(early, late, rotated):
+    side = lax.axis_index("band") % 2
+    for quarter in range(4):
+        for half in range(2):
+            for step in range(HALF // 8):
+                rows = pl.ds(quarter * HALF + step * 8, 8)
+                tiles = jnp.where(side == half, early[rows], late[rows])
+                place = (quarter * 2 + half) * HALF + step * 8
+                rotated[:, place : place + 8] = jnp.swapaxes(tiles, 0, 1)
 
 
 def on_device(orbitals, potential):
@@ -353,25 +361,30 @@
     taken = across(given)
     kept = over_y(kept)
     kept, taken = lax.optimization_barrier((kept, taken))
-    first, second, third = kept[:48], kept[48:88], kept[88:]
+    first, second, third, fourth = kept[:40], kept[40:72], kept[72:96], kept[96:]
     late_0 = across(first)
     (gram,) = call(gram_kernel, [(32, 128)], [], kept, taken)
     row = small_exchange(gram[:, None], SHEETS).sum(axis=0, keepdims=True)
     row, late_0, second = lax.optimization_barrier((row, late_0, second))
+    row = spread(row, Z_RINGS).sum(axis=0, keepdims=True)
+    row, second = lax.optimization_barrier((row, second))
     late_1 = across(second)
-    row = spread(row, Z_RINGS).sum(axis=0, keepdims=True)
-    row, late_1, third = lax.optimization_barrier((row, late_1, third))
+    gram = spread(row, SHEETS)[:, 0]
+    gram, late_1, third = lax.optimization_barrier((gram, late_1, third))
     late_2 = across(third)
-    gram = spread(row, SHEETS)[:, 0]
     (inverse,) = call(functools.partial(factor_kernel, cell_count), [(BANDS, BANDS)], [], gram)
-    (rotated,) = call(
-        rotation_kernel,
-        [(CX * CY, GROUP, NZ)],
-        [(4 * HALF, GROUP, NZ)],
-        inverse, kept, taken, given, late_0, late_1, late_2,
-    )
-    rotated = over_y(rotated)
-    return rotated.transpose(1, 0, 2).reshape(orbitals.shape)
+    tiles = (4 * HALF, GROUP, NZ)
+    inverse, late_2, fourth = lax.optimization_barrier((inverse, late_2, fourth))
+    late_3 = across(fourth)
+    (early,) = call(rotation_kernel, [tiles], [], inverse, kept, taken)
+    early = over_y(early)
+    early, late_3 = lax.optimization_barrier((early, late_3))
+    (late,) = call(
+        rotation_kernel, [tiles], [tiles], inverse, given, late_0, late_1, late_2, late_3
+    )
+    late = over_y(late)
+    (rotated,) = call(placing_kernel, [(GROUP, CX * CY, NZ)], [], early, late)
+    return rotated.reshape(orbitals.shape)
 
 
 def solution(mesh):

time: 257 us -> 274 us (1.066)
  starting transfers between devices: 90.3 us -> 118 us
  blocking collectives: 90.6 us -> 66.5 us
  waiting for transfers between devices: 39.7 us -> 61.4 us
  Pallas kernels: 31 us -> 22 us
    all_to_all x2 -> x1, blocking collectives: 49.3 us -> 29.4 us  [small_exchange(): lax.all_to_all(chunks, ('band', 'dom'), 0, 0, axis_index_groups=groups, t...]
    ppermute x4 -> x5, waiting for transfers between devices: 16.7 us -> 31.5 us  [across(): return lax.ppermute(block, 'band', [(i, i ^ 1) for i in range(8)])]
    ppermute x4 -> x5, starting transfers between devices: 48.3 us -> 61.6 us  [across(): return lax.ppermute(block, 'band', [(i, i ^ 1) for i in range(8)])]
    all_to_all x1 -> x2, starting transfers between devices: 9.87 us -> 20.5 us  [small_exchange(): lax.all_to_all(chunks, ('band', 'dom'), 0, 0, axis_index_groups=groups, t...]
    pallas_call x6 -> x8, Pallas kernels: 31 us -> 22 us  [call(): pl.pallas_call(kernel, out_shape=[jax.ShapeDtypeStruct(shape, jnp.float32...]
    all_to_all x1 -> x2, waiting for transfers between devices: 0.01 us -> 6.85 us  [small_exchange(): lax.all_to_all(chunks, ('band', 'dom'), 0, 0, axis_index_groups=groups, t...]
    all_to_all x3, blocking collectives: 41.3 us -> 37.1 us  [over_y(): lax.all_to_all(block, 'band', 0, 0, axis_index_groups=Y_RINGS, tiled=True)]
    all_to_all x0 -> x1, starting transfers between devices: none -> 3.47 us  [over_y(): lax.all_to_all(block, 'band', 0, 0, axis_index_groups=Y_RINGS, tiled=True)]
  transfers between devices with their start and end apart: 17 -> 20, of which waited for: 10 -> 12; matrix products, arithmetic and copies ran while one was open for 0% -> 0% of each run, Pallas kernels for 3% -> 3%
where the time goes in v5:
time: 274 us; the launch traced here: 271 us
  starting transfers between devices  118 us (43%)
  blocking collectives  66.5 us (24%)
  waiting for transfers between devices  61.4 us (22%)
  Pallas kernels  22 us (8%)
  local copies, waits for them, and re-layouts  3.55 us (1%)
    ppermute x5, starting transfers between devices, across(): return lax.ppermute(block, 'band', [(i, i ^ 1) for i in range(8)])  61.6 us
    all_to_all x3, blocking collectives, over_y(): lax.all_to_all(block, 'band', 0, 0, axis_index_groups=Y_RINGS, tiled=True)  37.1 us
    ppermute x5, waiting for transfers between devices, across(): return lax.ppermute(block, 'band', [(i, i ^ 1) for i in range(8)])  31.5 us
    all_to_all x1, blocking collectives, small_exchange(): lax.all_to_all(chunks, ('band', 'dom'), 0, 0, axis_index_groups=groups, t...  29.4 us
    pallas_call x8, Pallas kernels, call(): pl.pallas_call(kernel, out_shape=[jax.ShapeDtypeStruct(shape, jnp.float32...  22 us
    all_to_all x2, starting transfers between devices, small_exchange(): lax.all_to_all(chunks, ('band', 'dom'), 0, 0, axis_index_groups=groups, t...  20.5 us
    ppermute x8, starting transfers between devices, along_rows(): return lax.ppermute(rim, 'dom', route)  17.5 us
    ppermute x8, waiting for transfers between devices, along_rows(): return lax.ppermute(rim, 'dom', route)  16.6 us
  transfers between devices with their start and end apart: 20, of which 12 were waited for; matrix products, arithmetic and copies ran while one was open for 0% of the time, Pallas kernels for 3%

profile of v5, /device:TPU:1, one launch (start us, length us, event | category | flops | bytes accessed | tf_op | source)
XLA Modules:
  0.0 271.5 jit_solution(9888350634633864232)
XLA Ops:
  2.9 4.5 %collective-permute-start.2 = (f32[136,8,128]{2,1,0:T(8,128)S(1)}, f32[136,8,128]{2,1,0:T(8,128)S(1)}, u32[]{:S(2)}, u32[]{:S(2)}) collective-permute-start(f32[136,8,128]{2,1,0:T(8,128)S(1)} %get-tuple-element.35), channel_id=1, source_target_pairs={{0,1},{1,2},{2,3},{3,4},{4,5},{5,6},{6,7},{8,9},{9,10},{10,11},{11... | collective-permute-start | bytes 1671176 | tf_op jit(solution)/shard_map/ppermute | solution.py:224
  7.5 5.6 %collective-permute-start.3 = (f32[136,8,128]{2,1,0:T(8,128)S(1)}, f32[136,8,128]{2,1,0:T(8,128)S(1)}, u32[]{:S(2)}, u32[]{:S(2)}) collective-permute-start(f32[136,8,128]{2,1,0:T(8,128)S(1)} %get-tuple-element.36), channel_id=1, source_target_pairs={{1,0},{2,1},{3,2},{4,3},{5,4},{6,5},{7,6},{9,8},{10,9},{11,10},{12... | collective-permute-start | bytes 1671176 | tf_op jit(solution)/shard_map/ppermute | solution.py:224
  18.4 3.8 %collective-permute-start.4 = (f32[4,8,8,128]{3,2,1,0:T(8,128)S(1)}, f32[4,8,8,128]{3,2,1,0:T(8,128)S(1)}, u32[]{:S(2)}, u32[]{:S(2)}) collective-permute-start(f32[4,8,8,128]{3,2,1,0:T(8,128)S(1)} %pad_maximum_fusion), channel_id=1, source_target_pairs={{0,8},{1,9},{2,10},{3,11},{4,12},{5,13},{6,14},{7,15},{8,16},{9,17... | collective-permute-start | bytes 393224 | tf_op jit(solution)/shard_map/ppermute | solution.py:219
  26.7 4.2 %collective-permute-done.1.high = f32[136,8,128]{2,1,0:T(8,128)S(1)} collective-permute-done((f32[136,8,128]{2,1,0:T(8,128)S(1)}, f32[136,8,128]{2,1,0:T(8,128)S(1)}, u32[]{:S(2)}, u32[]{:S(2)}) %collective-permute-start.1) | collective-permute-done | bytes 557088 | tf_op jit(solution)/shard_map/ppermute | solution.py:219
  33.4 3.7 %shard_map.38 = (f32[24,24,8,128]{3,2,1,0:T(8,128)S(1)}, f32[16,16,8,128]{3,2,1,0:T(8,128)S(1)}, f32[24,24,128]{2,1,0:T(8,128)S(1)}, f32[128,8,128]{2,1,0:T(8,12...) custom-call(f32[16,16,8,128]{3,2,1,0:T(8,128)S(1)} %bitcast.23, ...), custom_call_target="tpu_custom_call" | custom-call | tf_op jit(solution)/shard_map/pallas_call | solution.py:207
  41.6 3.6 %collective-permute-start.6 = (f32[128,8,128]{2,1,0:T(8,128)S(1)}, f32[128,8,128]{2,1,0:T(8,128)S(1)}, u32[]{:S(2)}, u32[]{:S(2)}) collective-permute-start(f32[128,8,128]{2,1,0:T(8,128)S(1)} %get-tuple-element.40), channel_id=1, source_target_pairs={{0,8},{1,9},{2,10},{3,11},{4,12},{5,13},{6,14},{7,15},{8,16},{9,17... | collective-permute-start | bytes 1572872 | tf_op jit(solution)/shard_map/ppermute | solution.py:219
  46.5 4.0 %collective-permute-done.9.back = f32[128,8,128]{2,1,0:T(8,128)S(1)} collective-permute-done((f32[128,8,128]{2,1,0:T(8,128)S(1)}, f32[128,8,128]{2,1,0:T(8,128)S(1)}, u32[]{:S(2)}, u32[]{:S(2)}) %collective-permute-start.9) | collective-permute-done | bytes 524320 | tf_op jit(solution)/shard_map/ppermute | solution.py:224
  55.9 4.7 %collective-permute-done.7.high = f32[128,8,128]{2,1,0:T(8,128)S(1)} collective-permute-done((f32[128,8,128]{2,1,0:T(8,128)S(1)}, f32[128,8,128]{2,1,0:T(8,128)S(1)}, u32[]{:S(2)}, u32[]{:S(2)}) %collective-permute-start.7) | collective-permute-done | bytes 524320 | tf_op jit(solution)/shard_map/ppermute | solution.py:219
  62.0 5.6 %shard_map.39 = (f32[128,8,128]{2,1,0:T(8,128)S(1)}, f32[128,8,128]{2,1,0:T(8,128)S(1)}) custom-call(f32[16,16,8,128]{3,2,1,0:T(8,128)S(1)} %get-tuple-element.37.field, f32[24,24,8,128]{3,2,1,0:T(8,128)S(1)} %get-tuple-element.38.once, f32[24,24,128]{2,1,0:T(8,128)S(1)} %get-tuple-element.39.potential, f32[128,8,128]{2,1,0:T(8,128)S(1)} %collective-permute-done.6.low, ...), custom_call_target="tpu_custom_call" | custom-call | tf_op jit(solution)/shard_map/pallas_call | solution.py:207
  67.6 12.3 %all_to_all.35.mine = f32[128,8,128]{2,1,0:T(8,128)S(1)} all-to-all(f32[128,8,128]{2,1,0:T(8,128)S(1)} %get-tuple-element.45), channel_id=1, replica_groups={{0,128,256,384},{64,192,320,448},{1,129,257,385},{65,193,321,449},{2,13..., dimensions={0} | all-to-all | bytes 1048576 | tf_op jit(solution)/shard_map/all_to_all | solution.py:267
  79.9 13.2 %collective-permute-start.12 = (f32[128,8,128]{2,1,0:T(8,128)S(1)}, f32[128,8,128]{2,1,0:T(8,128)S(1)}, u32[]{:S(2)}, u32[]{:S(2)}) collective-permute-start(f32[128,8,128]{2,1,0:T(8,128)S(1)} %all_to_all.35.mine), channel_id=1, source_target_pairs={{0,64},{64,0},{128,192},{192,128},{256,320},{320,256},{384,448},{4... | collective-permute-start | bytes 1572872 | tf_op jit(solution)/shard_map/ppermute | solution.py:271
  93.1 11.9 %all_to_all.36.kept.mine = f32[128,8,128]{2,1,0:T(8,128)S(1)} all-to-all(f32[128,8,128]{2,1,0:T(8,128)S(1)} %get-tuple-element.44), channel_id=1, replica_groups={{0,128,256,384},{64,192,320,448},{1,129,257,385},{65,193,321,449},{2,13..., dimensions={0} | all-to-all | bytes 1048576 | tf_op jit(solution)/shard_map/all_to_all | solution.py:267
  105.0 11.9 %collective-permute-done.12.taken.rest_0_ = f32[128,8,128]{2,1,0:T(8,128)S(1)} collective-permute-done((f32[128,8,128]{2,1,0:T(8,128)S(1)}, f32[128,8,128]{2,1,0:T(8,128)S(1)}, u32[]{:S(2)}, u32[]{:S(2)}) %collective-permute-start.12) | collective-permute-done | bytes 524320 | tf_op jit(solution)/shard_map/ppermute | solution.py:271
  118.1 8.9 %all-to-all-start.2 = ((f32[32,1,128]{2,1,0:T(1,128)}), f32[32,1,128]{2,1,0:T(1,128)S(1)}, u32[]{:S(2)}, u32[]{:S(2)}) async-start(f32[32,1,128]{2,1,0:T(1,128)} %bitcast.9), calls=%async_computation.2 | async-start | bytes 32768 | tf_op jit(solution)/shard_map/all_to_all | solution.py:275
  127.1 27.5 %collective-permute-start.13 = (f32[40,8,128]{2,1,0:T(8,128)S(1)}, f32[40,8,128]{2,1,0:T(8,128)S(1)}, u32[]{:S(2)}, u32[]{:S(2)}) collective-permute-start(f32[40,8,128]{2,1,0:T(8,128)S(1)} %slice.52), channel_id=1, source_target_pairs={{0,64},{64,0},{128,192},{192,128},{256,320},{320,256},{384,448},{4... | collective-permute-start | bytes 491528 | tf_op jit(solution)/shard_map/ppermute | solution.py:271
  154.7 4.3 %collective-permute-done.13.rest_0_ = f32[40,8,128]{2,1,0:T(8,128)S(1)} collective-permute-done((f32[40,8,128]{2,1,0:T(8,128)S(1)}, f32[40,8,128]{2,1,0:T(8,128)S(1)}, u32[]{:S(2)}, u32[]{:S(2)}) %collective-permute-start.13) | collective-permute-done | bytes 163872 | tf_op jit(solution)/shard_map/ppermute | solution.py:271
  159.0 29.4 %all_to_all.37 = f32[16,1,128]{2,1,0:T(1,128)S(1)} all-to-all(f32[16,1,128]{2,1,0:T(1,128)S(1)} %broadcast_in_dim.26), channel_id=1, replica_groups={{0,8,16,24,32,40,48,56,64,72,80,88,96,104,112,120},{1,9,17,25,33,41,49,..., dimensions={0} | all-to-all | bytes 16384 | tf_op jit(solution)/shard_map/all_to_all | solution.py:275
  191.5 11.6 %all-to-all-start.4 = ((f32[32,1,128]{2,1,0:T(1,128)}), f32[32,1,128]{2,1,0:T(1,128)S(1)}, u32[]{:S(2)}, u32[]{:S(2)}) async-start(f32[32,1,128]{2,1,0:T(1,128)} %broadcast_in_dim.29), calls=%async_computation.4 | async-start | bytes 32768 | tf_op jit(solution)/shard_map/all_to_all | solution.py:275
  203.1 6.8 %all-to-all-done.4 = f32[32,1,128]{2,1,0:T(1,128)S(1)} async-done(((f32[32,1,128]{2,1,0:T(1,128)}), f32[32,1,128]{2,1,0:T(1,128)S(1)}, u32[]{:S(2)}, u32[]{:S(2)}) %all-to-all-start.4) | async-done | bytes 16416 | tf_op jit(solution)/shard_map/all_to_all | solution.py:275
  209.9 11.7 %collective-permute-start.15 = (f32[24,8,128]{2,1,0:T(8,128)S(1)}, f32[24,8,128]{2,1,0:T(8,128)S(1)}, u32[]{:S(2)}, u32[]{:S(2)}) collective-permute-start(f32[24,8,128]{2,1,0:T(8,128)S(1)} %slice.54), channel_id=1, source_target_pairs={{0,64},{64,0},{128,192},{192,128},{256,320},{320,256},{384,448},{4... | collective-permute-start | bytes 294920 | tf_op jit(solution)/shard_map/ppermute | solution.py:271
  221.7 8.5 %shard_map.41.inverse = f32[64,64]{1,0:T(8,128)S(1)} custom-call(f32[32,128]{1,0:T(8,128)S(1)} %bitcast.28), custom_call_target="tpu_custom_call" | custom-call | tf_op jit(solution)/shard_map/pallas_call | solution.py:207
  234.9 6.8 %collective-permute-start.16 = (f32[32,8,128]{2,1,0:T(8,128)S(1)}, f32[32,8,128]{2,1,0:T(8,128)S(1)}, u32[]{:S(2)}, u32[]{:S(2)}) collective-permute-start(f32[32,8,128]{2,1,0:T(8,128)S(1)} %get-tuple-element.55), channel_id=1, source_target_pairs={{0,64},{64,0},{128,192},{192,128},{256,320},{320,256},{384,448},{4... | collective-permute-start | bytes 393224 | tf_op jit(solution)/shard_map/ppermute | solution.py:271
  241.7 15.3 %collective-permute-done.16.rest_3_ = f32[32,8,128]{2,1,0:T(8,128)S(1)} collective-permute-done((f32[32,8,128]{2,1,0:T(8,128)S(1)}, f32[32,8,128]{2,1,0:T(8,128)S(1)}, u32[]{:S(2)}, u32[]{:S(2)}) %collective-permute-start.16) | collective-permute-done | bytes 131104 | tf_op jit(solution)/shard_map/ppermute | solution.py:271
  257.3 12.9 %all_to_all.38.late = f32[128,8,128]{2,1,0:T(8,128)S(1)} all-to-all(f32[128,8,128]{2,1,0:T(8,128)S(1)} %shard_map.43), channel_id=1, replica_groups={{0,128,256,384},{64,192,320,448},{1,129,257,385},{65,193,321,449},{2,13..., dimensions={0} | all-to-all | bytes 1048576 | tf_op jit(solution)/shard_map/all_to_all | solution.py:267
  (51 shorter events, 38.3 us)
Async XLA Ops:
  0.0 33.4 %copy-start.1 = (f32[1,16,16,128]{3,2,1,0:T(8,128)S(1)}, f32[1,16,16,128]{3,2,1,0:T(8,128)}, u32[]{:S(2)}) copy-start(f32[1,16,16,128]{3,2,1,0:T(8,128)} %param.4) | copy-start | bytes 393220
  0.0 33.4 %copy-start.2 = (f32[128,128]{1,0:T(8,128)S(1)}, f32[128,128]{1,0:T(8,128)}, u32[]{:S(2)}) copy-start(f32[128,128]{1,0:T(8,128)} %constant.4.clone.along) | copy-start | bytes 196612
  1.9 0.9 copy-start
  2.9 12.8 %collective-permute-start.2 = (f32[136,8,128]{2,1,0:T(8,128)S(1)}, f32[136,8,128]{2,1,0:T(8,128)S(1)}, u32[]{:S(2)}, u32[]{:S(2)}) collective-permute-start(f32[136,8,128]{2,1,0:T(8,128)S(1)} %get-tuple-element.35), channel_id=1, source_target_pairs={{0,1},{1,2},{2,3},{3,4},{4,5},{5,6},{6,7},{8,9},{9,10},{10,11},{11... | collective-permute-start | bytes 1671176 | tf_op jit(solution)/shard_map/ppermute | solution.py:224
  7.5 10.9 %collective-permute-start.3 = (f32[136,8,128]{2,1,0:T(8,128)S(1)}, f32[136,8,128]{2,1,0:T(8,128)S(1)}, u32[]{:S(2)}, u32[]{:S(2)}) collective-permute-start(f32[136,8,128]{2,1,0:T(8,128)S(1)} %get-tuple-element.36), channel_id=1, source_target_pairs={{1,0},{2,1},{3,2},{4,3},{5,4},{6,5},{7,6},{9,8},{10,9},{11,10},{12... | collective-permute-start | bytes 1671176 | tf_op jit(solution)/shard_map/ppermute | solution.py:224
  13.1 13.6 %collective-permute-start = (f32[136,8,128]{2,1,0:T(8,128)S(1)}, f32[136,8,128]{2,1,0:T(8,128)S(1)}, u32[]{:S(2)}, u32[]{:S(2)}) collective-permute-start(f32[136,8,128]{2,1,0:T(8,128)S(1)} %get-tuple-element.33), channel_id=1, source_target_pairs={{0,8},{1,9},{2,10},{3,11},{4,12},{5,13},{6,14},{7,15},{8,16},{9,17... | collective-permute-start | bytes 1671176 | tf_op jit(solution)/shard_map/ppermute | solution.py:219
  14.4 16.5 %collective-permute-start.1 = (f32[136,8,128]{2,1,0:T(8,128)S(1)}, f32[136,8,128]{2,1,0:T(8,128)S(1)}, u32[]{:S(2)}, u32[]{:S(2)}) collective-permute-start(f32[136,8,128]{2,1,0:T(8,128)S(1)} %get-tuple-element.34), channel_id=1, source_target_pairs={{8,0},{9,1},{10,2},{11,3},{12,4},{13,5},{14,6},{15,7},{16,8},{17,9... | collective-permute-start | bytes 1671176 | tf_op jit(solution)/shard_map/ppermute | solution.py:219
  18.4 12.5 %collective-permute-start.4 = (f32[4,8,8,128]{3,2,1,0:T(8,128)S(1)}, f32[4,8,8,128]{3,2,1,0:T(8,128)S(1)}, u32[]{:S(2)}, u32[]{:S(2)}) collective-permute-start(f32[4,8,8,128]{3,2,1,0:T(8,128)S(1)} %pad_maximum_fusion), channel_id=1, source_target_pairs={{0,8},{1,9},{2,10},{3,11},{4,12},{5,13},{6,14},{7,15},{8,16},{9,17... | collective-permute-start | bytes 393224 | tf_op jit(solution)/shard_map/ppermute | solution.py:219
  22.3 11.2 %collective-permute-start.5 = (f32[4,8,8,128]{3,2,1,0:T(8,128)S(1)}, f32[4,8,8,128]{3,2,1,0:T(8,128)S(1)}, u32[]{:S(2)}, u32[]{:S(2)}) collective-permute-start(f32[4,8,8,128]{3,2,1,0:T(8,128)S(1)} %pad_maximum_fusion.1), channel_id=1, source_target_pairs={{8,0},{9,1},{10,2},{11,3},{12,4},{13,5},{14,6},{15,7},{16,8},{17,9... | collective-permute-start | bytes 393224 | tf_op jit(solution)/shard_map/ppermute | solution.py:219
  37.2 9.3 %collective-permute-start.8 = (f32[128,8,128]{2,1,0:T(8,128)S(1)}, f32[128,8,128]{2,1,0:T(8,128)S(1)}, u32[]{:S(2)}, u32[]{:S(2)}) collective-permute-start(f32[128,8,128]{2,1,0:T(8,128)S(1)} %get-tuple-element.42), channel_id=1, source_target_pairs={{0,1},{1,2},{2,3},{3,4},{4,5},{5,6},{6,7},{8,9},{9,10},{10,11},{11... | collective-permute-start | bytes 1572872 | tf_op jit(solution)/shard_map/ppermute | solution.py:224
  39.6 10.8 %collective-permute-start.9 = (f32[128,8,128]{2,1,0:T(8,128)S(1)}, f32[128,8,128]{2,1,0:T(8,128)S(1)}, u32[]{:S(2)}, u32[]{:S(2)}) collective-permute-start(f32[128,8,128]{2,1,0:T(8,128)S(1)} %get-tuple-element.43), channel_id=1, source_target_pairs={{1,0},{2,1},{3,2},{4,3},{5,4},{6,5},{7,6},{9,8},{10,9},{11,10},{12... | collective-permute-start | bytes 1572872 | tf_op jit(solution)/shard_map/ppermute | solution.py:224
  41.6 14.4 %collective-permute-start.6 = (f32[128,8,128]{2,1,0:T(8,128)S(1)}, f32[128,8,128]{2,1,0:T(8,128)S(1)}, u32[]{:S(2)}, u32[]{:S(2)}) collective-permute-start(f32[128,8,128]{2,1,0:T(8,128)S(1)} %get-tuple-element.40), channel_id=1, source_target_pairs={{0,8},{1,9},{2,10},{3,11},{4,12},{5,13},{6,14},{7,15},{8,16},{9,17... | collective-permute-start | bytes 1572872 | tf_op jit(solution)/shard_map/ppermute | solution.py:219
  45.1 15.5 %collective-permute-start.7 = (f32[128,8,128]{2,1,0:T(8,128)S(1)}, f32[128,8,128]{2,1,0:T(8,128)S(1)}, u32[]{:S(2)}, u32[]{:S(2)}) collective-permute-start(f32[128,8,128]{2,1,0:T(8,128)S(1)} %get-tuple-element.41), channel_id=1, source_target_pairs={{8,0},{9,1},{10,2},{11,3},{12,4},{13,5},{14,6},{15,7},{16,8},{17,9... | collective-permute-start | bytes 1572872 | tf_op jit(solution)/shard_map/ppermute | solution.py:219
  50.5 10.2 %collective-permute-start.10 = (f32[4,8,8,128]{3,2,1,0:T(8,128)S(1)}, f32[4,8,8,128]{3,2,1,0:T(8,128)S(1)}, u32[]{:S(2)}, u32[]{:S(2)}) collective-permute-start(f32[4,8,8,128]{3,2,1,0:T(8,128)S(1)} %pad_maximum_fusion.2), channel_id=1, source_target_pairs={{0,8},{1,9},{2,10},{3,11},{4,12},{5,13},{6,14},{7,15},{8,16},{9,17... | collective-permute-start | bytes 393224 | tf_op jit(solution)/shard_map/ppermute | solution.py:219
  54.0 8.0 %collective-permute-start.11 = (f32[4,8,8,128]{3,2,1,0:T(8,128)S(1)}, f32[4,8,8,128]{3,2,1,0:T(8,128)S(1)}, u32[]{:S(2)}, u32[]{:S(2)}) collective-permute-start(f32[4,8,8,128]{3,2,1,0:T(8,128)S(1)} %pad_maximum_fusion.3), channel_id=1, source_target_pairs={{8,0},{9,1},{10,2},{11,3},{12,4},{13,5},{14,6},{15,7},{16,8},{17,9... | collective-permute-start | bytes 393224 | tf_op jit(solution)/shard_map/ppermute | solution.py:219
  79.9 37.0 %collective-permute-start.12 = (f32[128,8,128]{2,1,0:T(8,128)S(1)}, f32[128,8,128]{2,1,0:T(8,128)S(1)}, u32[]{:S(2)}, u32[]{:S(2)}) collective-permute-start(f32[128,8,128]{2,1,0:T(8,128)S(1)} %all_to_all.35.mine), channel_id=1, source_target_pairs={{0,64},{64,0},{128,192},{192,128},{256,320},{320,256},{384,448},{4... | collective-permute-start | bytes 1572872 | tf_op jit(solution)/shard_map/ppermute | solution.py:271
  118.1 36.5 %all-to-all-start.2 = ((f32[32,1,128]{2,1,0:T(1,128)}), f32[32,1,128]{2,1,0:T(1,128)S(1)}, u32[]{:S(2)}, u32[]{:S(2)}) async-start(f32[32,1,128]{2,1,0:T(1,128)} %bitcast.9), calls=%async_computation.2 | async-start | bytes 32768 | tf_op jit(solution)/shard_map/all_to_all | solution.py:275
  127.1 31.9 %collective-permute-start.13 = (f32[40,8,128]{2,1,0:T(8,128)S(1)}, f32[40,8,128]{2,1,0:T(8,128)S(1)}, u32[]{:S(2)}, u32[]{:S(2)}) collective-permute-start(f32[40,8,128]{2,1,0:T(8,128)S(1)} %slice.52), channel_id=1, source_target_pairs={{0,64},{64,0},{128,192},{192,128},{256,320},{320,256},{384,448},{4... | collective-permute-start | bytes 491528 | tf_op jit(solution)/shard_map/ppermute | solution.py:271
  188.4 21.5 %collective-permute-start.14 = (f32[32,8,128]{2,1,0:T(8,128)S(1)}, f32[32,8,128]{2,1,0:T(8,128)S(1)}, u32[]{:S(2)}, u32[]{:S(2)}) collective-permute-start(f32[32,8,128]{2,1,0:T(8,128)S(1)} %get-tuple-element.51), channel_id=1, source_target_pairs={{0,64},{64,0},{128,192},{192,128},{256,320},{320,256},{384,448},{4... | collective-permute-start | bytes 393224 | tf_op jit(solution)/shard_map/ppermute | solution.py:271
  191.5 18.5 %all-to-all-start.4 = ((f32[32,1,128]{2,1,0:T(1,128)}), f32[32,1,128]{2,1,0:T(1,128)S(1)}, u32[]{:S(2)}, u32[]{:S(2)}) async-start(f32[32,1,128]{2,1,0:T(1,128)} %broadcast_in_dim.29), calls=%async_computation.4 | async-start | bytes 32768 | tf_op jit(solution)/shard_map/all_to_all | solution.py:275
  209.9 20.3 %collective-permute-start.15 = (f32[24,8,128]{2,1,0:T(8,128)S(1)}, f32[24,8,128]{2,1,0:T(8,128)S(1)}, u32[]{:S(2)}, u32[]{:S(2)}) collective-permute-start(f32[24,8,128]{2,1,0:T(8,128)S(1)} %slice.54), channel_id=1, source_target_pairs={{0,64},{64,0},{128,192},{192,128},{256,320},{320,256},{384,448},{4... | collective-permute-start | bytes 294920 | tf_op jit(solution)/shard_map/ppermute | solution.py:271
  231.4 25.5 %all-to-all-start.5 = ((f32[128,8,128]{2,1,0:T(8,128)}), f32[128,8,128]{2,1,0:T(8,128)S(1)}, u32[]{:S(2)}, u32[]{:S(2)}) async-start(f32[128,8,128]{2,1,0:T(8,128)} %shard_map.42), calls=%async_computation.5 | async-start | bytes 1048576 | tf_op jit(solution)/shard_map/all_to_all | solution.py:267
  234.9 22.1 %collective-permute-start.16 = (f32[32,8,128]{2,1,0:T(8,128)S(1)}, f32[32,8,128]{2,1,0:T(8,128)S(1)}, u32[]{:S(2)}, u32[]{:S(2)}) collective-permute-start(f32[32,8,128]{2,1,0:T(8,128)S(1)} %get-tuple-element.55), channel_id=1, source_target_pairs={{0,64},{64,0},{128,192},{192,128},{256,320},{320,256},{384,448},{4... | collective-permute-start | bytes 393224 | tf_op jit(solution)/shard_map/ppermute | solution.py:271

commit v6 on v5

--- a/solution.py
+++ b/solution.py
@@ -27,6 +27,7 @@
 DEEP = 8
 BANDS = 64
 HALF = 32
+PIVOTS = 4
 VMEM_BYTES = 40 * 2**20
 
 
@@ -35,6 +36,7 @@
 
 
 Y_RINGS = [[0, 2, 4, 6], [1, 3, 5, 7]]
+Z_PAIRS = [[0, 1], [2, 3], [4, 5], [6, 7]]
 SHEETS = [
     [member(y, z_hi, z_lo, plane) for y in range(4) for plane in range(8)]
     for z_hi in range(2)
@@ -305,30 +307,30 @@
     matrix = jnp.concatenate((both[:, :BANDS], both[:, BANDS:]), axis=0)
     rows = lax.broadcasted_iota(jnp.int32, (BANDS, BANDS), 0)
     columns = lax.broadcasted_iota(jnp.int32, (BANDS, BANDS), 1)
-    work = jnp.concatenate((matrix, jnp.where(rows == columns, 1.0, 0.0)), axis=1)
-    row_index = lax.broadcasted_iota(jnp.int32, (BANDS, 2 * BANDS), 0)
-    scales = jnp.zeros((BANDS, 2 * BANDS), jnp.float32)
-    for step in range(BANDS):
-        pivot_row = work[step : step + 1]
-        column = jnp.broadcast_to(work[:, step : step + 1], work.shape)
-        pivot = jnp.broadcast_to(column[step : step + 1], work.shape)
-        scales = jnp.where(row_index == step, pivot, scales)
-        below = jnp.where(row_index > step, column / pivot, 0.0)
-        work = work - below * pivot_row
-    inverse[...] = (work * lax.rsqrt(scales))[:, BANDS:]
-
-
-def rotation_kernel(inverse, mine, *rest):
-    theirs, rotated = rest[:-1], rest[-1]
-    if len(theirs) > 1:
-        *pieces, rotated, theirs = rest
-        place = 0
-        for piece in pieces:
-            theirs[place : place + piece.shape[0]] = piece[...]
-            place += piece.shape[0]
-    else:
-        theirs = theirs[0]
+    work = jnp.concatenate((jnp.where(rows == columns, 1.0, 0.0), matrix), axis=1)
+    row_index = lax.broadcasted_iota(jnp.int32, work.shape, 0)
+    for start in range(0, BANDS, PIVOTS):
+        picked = [
+            jnp.broadcast_to(work[:, BANDS + step : BANDS + step + 1], work.shape)
+            for step in range(start, start + PIVOTS)
+        ]
+        pivot_rows = [work[step : step + 1] for step in range(start, start + PIVOTS)]
+        for j in range(PIVOTS):
+            here = slice(start + j, start + j + 1)
+            pivot = picked[j][here]
+            below = jnp.where(row_index > start + j, picked[j] * (1.0 / pivot), 0.0)
+            for later in range(j + 1, PIVOTS):
+                there = slice(start + later, start + later + 1)
+                picked[later] = picked[later] - below * picked[later][here]
+                pivot_rows[later] = pivot_rows[later] - below[there] * pivot_rows[j]
+            work = work - below * pivot_rows[j]
+            inverse[here] = (pivot_rows[j] * lax.rsqrt(pivot))[:, :BANDS]
+
+
+def rotation_kernel(inverse, mine, theirs, rotated):
     side = lax.axis_index("band") % 2
+    if len(theirs.shape) == 4:
+        theirs = theirs.at[1 - side]
     own = jnp.concatenate(
         [inverse[pl.ds(pl.multiple_of((2 * ring + side) * GROUP, GROUP), GROUP)] for ring in range(4)],
         axis=0,
@@ -361,27 +363,23 @@
     taken = across(given)
     kept = over_y(kept)
     kept, taken = lax.optimization_barrier((kept, taken))
-    first, second, third, fourth = kept[:40], kept[40:72], kept[72:96], kept[96:]
-    late_0 = across(first)
-    (gram,) = call(gram_kernel, [(32, 128)], [], kept, taken)
-    row = small_exchange(gram[:, None], SHEETS).sum(axis=0, keepdims=True)
-    row, late_0, second = lax.optimization_barrier((row, late_0, second))
-    row = spread(row, Z_RINGS).sum(axis=0, keepdims=True)
-    row, second = lax.optimization_barrier((row, second))
-    late_1 = across(second)
-    gram = spread(row, SHEETS)[:, 0]
-    gram, late_1, third = lax.optimization_barrier((gram, late_1, third))
-    late_2 = across(third)
-    (inverse,) = call(functools.partial(factor_kernel, cell_count), [(BANDS, BANDS)], [], gram)
+    pair = lax.all_gather(kept, "band", axis=0, axis_index_groups=Z_PAIRS)
     tiles = (4 * HALF, GROUP, NZ)
-    inverse, late_2, fourth = lax.optimization_barrier((inverse, late_2, fourth))
-    late_3 = across(fourth)
-    (early,) = call(rotation_kernel, [tiles], [], inverse, kept, taken)
-    early = over_y(early)
-    early, late_3 = lax.optimization_barrier((early, late_3))
-    (late,) = call(
-        rotation_kernel, [tiles], [tiles], inverse, given, late_0, late_1, late_2, late_3
-    )
+
+    def sum_factor_rotate(_, carry):
+        (gram,) = call(gram_kernel, [(32, 128)], [], kept, taken)
+        row = small_exchange(gram[:, None], SHEETS).sum(axis=0, keepdims=True)
+        row = spread(row, Z_RINGS).sum(axis=0, keepdims=True)
+        gram = spread(row, SHEETS)[:, 0]
+        (inverse,) = call(functools.partial(factor_kernel, cell_count), [(BANDS, BANDS)], [], gram)
+        (early,) = call(rotation_kernel, [tiles], [], inverse, kept, taken)
+        return inverse, over_y(early)
+
+    once = jnp.where(lax.axis_index("dom") < PX * PY, 1, 2)
+    empty = (jnp.zeros((BANDS, BANDS), jnp.float32), jnp.zeros(tiles, jnp.float32))
+    inverse, early = lax.fori_loop(0, once, sum_factor_rotate, empty)
+    early, pair = lax.optimization_barrier((early, pair))
+    (late,) = call(rotation_kernel, [tiles], [], inverse, given, pair)
     late = over_y(late)
     (rotated,) = call(placing_kernel, [(GROUP, CX * CY, NZ)], [], early, late)
     return rotated.reshape(orbitals.shape)

time: 274 us -> 241 us (0.88)
  starting transfers between devices: 118 us -> 67.7 us
  between operations: 0.32 us -> 13.6 us
  blocking collectives: 66.5 us -> 77.3 us
  waiting for transfers between devices: 61.4 us -> 55.5 us
  Pallas kernels: 22 us -> 18.5 us
  local copies, waits for them, and re-layouts: 3.55 us -> 6.98 us
    ppermute x5 -> x1, starting transfers between devices: 61.6 us -> 13.2 us  [across(): return lax.ppermute(block, 'band', [(i, i ^ 1) for i in range(8)])]
    ppermute x5 -> x1, waiting for transfers between devices: 31.5 us -> 10.8 us  [across(): return lax.ppermute(block, 'band', [(i, i ^ 1) for i in range(8)])]
    all_to_all x1 -> x2, blocking collectives: 29.4 us -> 40.2 us  [small_exchange(): lax.all_to_all(chunks, ('band', 'dom'), 0, 0, axis_index_groups=groups, t...]
    all_to_all x1, waiting for transfers between devices: 0.01 us -> 9.43 us  [over_y(): lax.all_to_all(block, 'band', 0, 0, axis_index_groups=Y_RINGS, tiled=True)]
    all_to_all x2 -> x1, waiting for transfers between devices: 6.85 us -> 13.3 us  [small_exchange(): lax.all_to_all(chunks, ('band', 'dom'), 0, 0, axis_index_groups=groups, t...]
    pallas_call x8, Pallas kernels: 22 us -> 18.5 us  [call(): pl.pallas_call(kernel, out_shape=[jax.ShapeDtypeStruct(shape, jnp.float32...]
    all_to_all x2 -> x1, starting transfers between devices: 20.5 us -> 17.8 us  [small_exchange(): lax.all_to_all(chunks, ('band', 'dom'), 0, 0, axis_index_groups=groups, t...]
  transfers between devices with their start and end apart: 20 -> 16, of which waited for: 12 -> 11; matrix products, arithmetic and copies ran while one was open for 0% -> 1% of each run, Pallas kernels for 3% -> 3%
where the time goes in v6:
time: 241 us; the launch traced here: 240 us
  blocking collectives  77.3 us (32%)
  starting transfers between devices  67.7 us (28%)
  waiting for transfers between devices  55.5 us (23%)
  Pallas kernels  18.5 us (8%)
  between operations  13.6 us (6%)
  local copies, waits for them, and re-layouts  6.98 us (3%)
    all_to_all x2, blocking collectives, small_exchange(): lax.all_to_all(chunks, ('band', 'dom'), 0, 0, axis_index_groups=groups, t...  40.2 us
    all_to_all x3, blocking collectives, over_y(): lax.all_to_all(block, 'band', 0, 0, axis_index_groups=Y_RINGS, tiled=True)  37.1 us
    ppermute x8, starting transfers between devices, along_rows(): return lax.ppermute(rim, 'dom', route)  18.7 us
    pallas_call x8, Pallas kernels, call(): pl.pallas_call(kernel, out_shape=[jax.ShapeDtypeStruct(shape, jnp.float32...  18.5 us
    all_to_all x1, starting transfers between devices, small_exchange(): lax.all_to_all(chunks, ('band', 'dom'), 0, 0, axis_index_groups=groups, t...  17.8 us
    ppermute x8, waiting for transfers between devices, along_rows(): return lax.ppermute(rim, 'dom', route)  15.3 us
    ppermute x4, starting transfers between devices, along_columns(): return lax.ppermute(rim, 'dom', route)  14.5 us
    all_to_all x1, waiting for transfers between devices, small_exchange(): lax.all_to_all(chunks, ('band', 'dom'), 0, 0, axis_index_groups=groups, t...  13.3 us
  transfers between devices with their start and end apart: 16, of which 11 were waited for; matrix products, arithmetic and copies ran while one was open for 1% of the time, Pallas kernels for 3%

profile of v6, /device:TPU:1, one launch (start us, length us, event | category | flops | bytes accessed | tf_op | source)
XLA Modules:
  0.0 239.7 jit_solution(14694664360584367222)
XLA Ops:
  9.5 4.5 %collective-permute-start.2 = (f32[136,8,128]{2,1,0:T(8,128)S(1)}, f32[136,8,128]{2,1,0:T(8,128)S(1)}, u32[]{:S(2)}, u32[]{:S(2)}) collective-permute-start(f32[136,8,128]{2,1,0:T(8,128)S(1)} %get-tuple-element.141), channel_id=1, source_target_pairs={{0,1},{1,2},{2,3},{3,4},{4,5},{5,6},{6,7},{8,9},{9,10},{10,11},{11... | collective-permute-start | bytes 1671176 | tf_op jit(solution)/shard_map/ppermute | solution.py:226
  14.0 5.6 %collective-permute-start.3 = (f32[136,8,128]{2,1,0:T(8,128)S(1)}, f32[136,8,128]{2,1,0:T(8,128)S(1)}, u32[]{:S(2)}, u32[]{:S(2)}) collective-permute-start(f32[136,8,128]{2,1,0:T(8,128)S(1)} %get-tuple-element.142), channel_id=1, source_target_pairs={{1,0},{2,1},{3,2},{4,3},{5,4},{6,5},{7,6},{9,8},{10,9},{11,10},{12... | collective-permute-start | bytes 1671176 | tf_op jit(solution)/shard_map/ppermute | solution.py:226
  22.3 2.6 %collective-permute-done.3.back = f32[136,8,128]{2,1,0:T(8,128)S(1)} collective-permute-done((f32[136,8,128]{2,1,0:T(8,128)S(1)}, f32[136,8,128]{2,1,0:T(8,128)S(1)}, u32[]{:S(2)}, u32[]{:S(2)}) %collective-permute-start.3) | collective-permute-done | bytes 557088 | tf_op jit(solution)/shard_map/ppermute | solution.py:226
  26.2 4.5 %collective-permute-start.4 = (f32[4,8,8,128]{3,2,1,0:T(8,128)S(1)}, f32[4,8,8,128]{3,2,1,0:T(8,128)S(1)}, u32[]{:S(2)}, u32[]{:S(2)}) collective-permute-start(f32[4,8,8,128]{3,2,1,0:T(8,128)S(1)} %pad_maximum_fusion), channel_id=1, source_target_pairs={{0,8},{1,9},{2,10},{3,11},{4,12},{5,13},{6,14},{7,15},{8,16},{9,17... | collective-permute-start | bytes 393224 | tf_op jit(solution)/shard_map/ppermute | solution.py:221
  33.2 4.2 %collective-permute-done.1.high = f32[136,8,128]{2,1,0:T(8,128)S(1)} collective-permute-done((f32[136,8,128]{2,1,0:T(8,128)S(1)}, f32[136,8,128]{2,1,0:T(8,128)S(1)}, u32[]{:S(2)}, u32[]{:S(2)}) %collective-permute-start.1) | collective-permute-done | bytes 557088 | tf_op jit(solution)/shard_map/ppermute | solution.py:221
  40.0 3.7 %shard_map.38 = (f32[24,24,8,128]{3,2,1,0:T(8,128)S(1)}, f32[16,16,8,128]{3,2,1,0:T(8,128)S(1)}, f32[24,24,128]{2,1,0:T(8,128)S(1)}, f32[128,8,128]{2,1,0:T(8,12...) custom-call(f32[16,16,8,128]{3,2,1,0:T(8,128)S(1)} %bitcast.22, ...), custom_call_target="tpu_custom_call" | custom-call | tf_op jit(solution)/shard_map/pallas_call | solution.py:209
  48.1 3.6 %collective-permute-start.6 = (f32[128,8,128]{2,1,0:T(8,128)S(1)}, f32[128,8,128]{2,1,0:T(8,128)S(1)}, u32[]{:S(2)}, u32[]{:S(2)}) collective-permute-start(f32[128,8,128]{2,1,0:T(8,128)S(1)} %get-tuple-element.146), channel_id=1, source_target_pairs={{0,8},{1,9},{2,10},{3,11},{4,12},{5,13},{6,14},{7,15},{8,16},{9,17... | collective-permute-start | bytes 1572872 | tf_op jit(solution)/shard_map/ppermute | solution.py:221
  53.0 3.9 %collective-permute-done.9.back = f32[128,8,128]{2,1,0:T(8,128)S(1)} collective-permute-done((f32[128,8,128]{2,1,0:T(8,128)S(1)}, f32[128,8,128]{2,1,0:T(8,128)S(1)}, u32[]{:S(2)}, u32[]{:S(2)}) %collective-permute-start.9) | collective-permute-done | bytes 524320 | tf_op jit(solution)/shard_map/ppermute | solution.py:226
  58.3 4.2 %collective-permute-start.10 = (f32[4,8,8,128]{3,2,1,0:T(8,128)S(1)}, f32[4,8,8,128]{3,2,1,0:T(8,128)S(1)}, u32[]{:S(2)}, u32[]{:S(2)}) collective-permute-start(f32[4,8,8,128]{3,2,1,0:T(8,128)S(1)} %pad_maximum_fusion.2), channel_id=1, source_target_pairs={{0,8},{1,9},{2,10},{3,11},{4,12},{5,13},{6,14},{7,15},{8,16},{9,17... | collective-permute-start | bytes 393224 | tf_op jit(solution)/shard_map/ppermute | solution.py:221
  62.5 4.7 %collective-permute-done.7.high = f32[128,8,128]{2,1,0:T(8,128)S(1)} collective-permute-done((f32[128,8,128]{2,1,0:T(8,128)S(1)}, f32[128,8,128]{2,1,0:T(8,128)S(1)}, u32[]{:S(2)}, u32[]{:S(2)}) %collective-permute-start.7) | collective-permute-done | bytes 524320 | tf_op jit(solution)/shard_map/ppermute | solution.py:221
  68.6 5.6 %shard_map.39 = (f32[128,8,128]{2,1,0:T(8,128)S(1)}, f32[128,8,128]{2,1,0:T(8,128)S(1)}) custom-call(f32[16,16,8,128]{3,2,1,0:T(8,128)S(1)} %get-tuple-element.143.field, f32[24,24,8,128]{3,2,1,0:T(8,128)S(1)} %get-tuple-element.144.once, f32[24,24,128]{2,1,0:T(8,128)S(1)} %get-tuple-element.145.potential, f32[128,8,128]{2,1,0:T(8,128)S(1)} %collective-permute-done.6.low, ...), custom_call_target="tpu_custom_call" | custom-call | tf_op jit(solution)/shard_map/pallas_call | solution.py:209
  74.2 12.3 %all_to_all.51.mine = f32[128,8,128]{2,1,0:T(8,128)S(1)} all-to-all(f32[128,8,128]{2,1,0:T(8,128)S(1)} %get-tuple-element.151), channel_id=1, replica_groups={{0,128,256,384},{64,192,320,448},{1,129,257,385},{65,193,321,449},{2,13..., dimensions={0} | all-to-all | bytes 1048576 | tf_op jit(solution)/shard_map/all_to_all | solution.py:269
  86.4 13.2 %collective-permute-start.12 = (f32[128,8,128]{2,1,0:T(8,128)S(1)}, f32[128,8,128]{2,1,0:T(8,128)S(1)}, u32[]{:S(2)}, u32[]{:S(2)}) collective-permute-start(f32[128,8,128]{2,1,0:T(8,128)S(1)} %all_to_all.51.mine), channel_id=1, source_target_pairs={{0,64},{64,0},{128,192},{192,128},{256,320},{320,256},{384,448},{4... | collective-permute-start | bytes 1572872 | tf_op jit(solution)/shard_map/ppermute | solution.py:273
  99.7 12.5 %all_to_all.52.kept = f32[128,8,128]{2,1,0:T(8,128)} all-to-all(f32[128,8,128]{2,1,0:T(8,128)S(1)} %get-tuple-element.150), channel_id=1, replica_groups={{0,128,256,384},{64,192,320,448},{1,129,257,385},{65,193,321,449},{2,13..., dimensions={0} | all-to-all | bytes 1048576 | tf_op jit(solution)/shard_map/all_to_all | solution.py:269
  112.1 10.8 %collective-permute-done.12.taken = f32[128,8,128]{2,1,0:T(8,128)S(1)} collective-permute-done((f32[128,8,128]{2,1,0:T(8,128)S(1)}, f32[128,8,128]{2,1,0:T(8,128)S(1)}, u32[]{:S(2)}, u32[]{:S(2)}) %collective-permute-start.12) | collective-permute-done | bytes 524320 | tf_op jit(solution)/shard_map/ppermute | solution.py:273
  124.7 25.9 %all_to_all.53 = f32[32,1,128]{2,1,0:T(1,128)S(1)} all-to-all(f32[32,1,128]{2,1,0:T(1,128)S(1)} %bitcast.29), channel_id=1, replica_groups={{0,1,2,3,4,5,6,7,128,129,130,131,132,133,134,135,256,257,258,259,260,26..., dimensions={0} | all-to-all | bytes 32768 | tf_op jit(solution)/shard_map/while/body/all_to_all | solution.py:277
  151.2 17.8 %all-to-all-start.5 = ((f32[16,1,128]{2,1,0:T(1,128)}), f32[16,1,128]{2,1,0:T(1,128)S(1)}, u32[]{:S(2)}, u32[]{:S(2)}) async-start(f32[16,1,128]{2,1,0:T(1,128)} %broadcast_in_dim.34), calls=%async_computation.5 | async-start | bytes 16384 | tf_op jit(solution)/shard_map/while/body/all_to_all | solution.py:277
  169.0 13.3 %all-to-all-done.5 = f32[16,1,128]{2,1,0:T(1,128)S(1)} async-done(((f32[16,1,128]{2,1,0:T(1,128)}), f32[16,1,128]{2,1,0:T(1,128)S(1)}, u32[]{:S(2)}, u32[]{:S(2)}) %all-to-all-start.5) | async-done | bytes 8224 | tf_op jit(solution)/shard_map/while/body/all_to_all | solution.py:277
  183.7 33.0 %while.16 = (s32[]{:T(128)}, f32[64,64]{1,0:T(8,128)}, f32[128,8,128]{2,1,0:T(8,128)}, s32[]{:T(128)}, f32[128]{0:T(128)S(1)}, /*index=5*/f32[128,8,128]{2,1,0:T(8,128)}, f32[128,8,128]{2,1,0:T(8,128)S(1)}, s32[]{:T(128)}) while((s32[]{:T(128)}, f32[64,64]{1,0:T(8,128)}, f32[128,8,128]{2,1,0:T(8,128)}, s32[]{:T(128)}, f32[128]{0:T(128)S(1)}, ...), condition=%wide.region_3.4_spmd, body=%wide.region_2.0_spmd.sunk | while | flops 2 | bytes 3785389 | solution.py:380
  183.7 14.3 %all_to_all.55 = f32[32,1,128]{2,1,0:T(1,128)S(1)} all-to-all(f32[32,1,128]{2,1,0:T(1,128)S(1)} %broadcast_in_dim.36), channel_id=1, replica_groups={{0,1,2,3,4,5,6,7,128,129,130,131,132,133,134,135,256,257,258,259,260,26..., dimensions={0} | all-to-all | bytes 32768 | tf_op jit(solution)/shard_map/while/body/all_to_all | solution.py:277
  198.0 2.7 %body.10.inverse = f32[64,64]{1,0:T(8,128)S(1)} custom-call(f32[32,128]{1,0:T(8,128)S(1)} %bitcast.23), custom_call_target="tpu_custom_call" | custom-call | tf_op jit(solution)/shard_map/while/body/pallas_call | solution.py:209
  203.0 3.5 %all-to-all-start.1 = ((f32[128,8,128]{2,1,0:T(8,128)}), f32[128,8,128]{2,1,0:T(8,128)S(1)}, u32[]{:S(2)}, u32[]{:S(2)}) async-start(f32[128,8,128]{2,1,0:T(8,128)} %body.11), calls=%async_computation.1 | async-start | bytes 1048576 | tf_op jit(solution)/shard_map/while/body/all_to_all | solution.py:269
  206.5 9.4 %all-to-all-done.1 = f32[128,8,128]{2,1,0:T(8,128)S(1)} async-done(((f32[128,8,128]{2,1,0:T(8,128)}), f32[128,8,128]{2,1,0:T(8,128)S(1)}, u32[]{:S(2)}, u32[]{:S(2)}) %all-to-all-start.1) | async-done | bytes 524320 | tf_op jit(solution)/shard_map/while/body/all_to_all | solution.py:269
  219.3 12.4 %all_to_all.54.late = f32[128,8,128]{2,1,0:T(8,128)S(1)} all-to-all(f32[128,8,128]{2,1,0:T(8,128)S(1)} %shard_map.40), channel_id=1, replica_groups={{0,128,256,384},{64,192,320,448},{1,129,257,385},{65,193,321,449},{2,13..., dimensions={0} | all-to-all | bytes 1048576 | tf_op jit(solution)/shard_map/all_to_all | solution.py:269
  (53 shorter events, 31.0 us)
Async XLA Ops:
  6.5 210.3 %all-gather.3.cloned.1.call-start = ((), (), s32[]{:S(2)}) async-start(), calls=%async_computation.7 | async-start | bytes 1572864 | tf_op jit(solution)/shard_map/all_gather | solution.py:366
  6.5 33.4 %copy-start.2 = (f32[1,16,16,128]{3,2,1,0:T(8,128)S(1)}, f32[1,16,16,128]{3,2,1,0:T(8,128)}, u32[]{:S(2)}) copy-start(f32[1,16,16,128]{3,2,1,0:T(8,128)} %param.6) | copy-start | bytes 393220
  6.5 33.4 %copy-start.3 = (f32[128,128]{1,0:T(8,128)S(1)}, f32[128,128]{1,0:T(8,128)}, u32[]{:S(2)}) copy-start(f32[128,128]{1,0:T(8,128)} %constant.31.clone.along) | copy-start | bytes 196612
  8.4 0.9 copy-start.1
  9.5 12.8 %collective-permute-start.2 = (f32[136,8,128]{2,1,0:T(8,128)S(1)}, f32[136,8,128]{2,1,0:T(8,128)S(1)}, u32[]{:S(2)}, u32[]{:S(2)}) collective-permute-start(f32[136,8,128]{2,1,0:T(8,128)S(1)} %get-tuple-element.141), channel_id=1, source_target_pairs={{0,1},{1,2},{2,3},{3,4},{4,5},{5,6},{6,7},{8,9},{9,10},{10,11},{11... | collective-permute-start | bytes 1671176 | tf_op jit(solution)/shard_map/ppermute | solution.py:226
  14.0 10.9 %collective-permute-start.3 = (f32[136,8,128]{2,1,0:T(8,128)S(1)}, f32[136,8,128]{2,1,0:T(8,128)S(1)}, u32[]{:S(2)}, u32[]{:S(2)}) collective-permute-start(f32[136,8,128]{2,1,0:T(8,128)S(1)} %get-tuple-element.142), channel_id=1, source_target_pairs={{1,0},{2,1},{3,2},{4,3},{5,4},{6,5},{7,6},{9,8},{10,9},{11,10},{12... | collective-permute-start | bytes 1671176 | tf_op jit(solution)/shard_map/ppermute | solution.py:226
  19.6 13.6 %collective-permute-start = (f32[136,8,128]{2,1,0:T(8,128)S(1)}, f32[136,8,128]{2,1,0:T(8,128)S(1)}, u32[]{:S(2)}, u32[]{:S(2)}) collective-permute-start(f32[136,8,128]{2,1,0:T(8,128)S(1)} %get-tuple-element.139), channel_id=1, source_target_pairs={{0,8},{1,9},{2,10},{3,11},{4,12},{5,13},{6,14},{7,15},{8,16},{9,17... | collective-permute-start | bytes 1671176 | tf_op jit(solution)/shard_map/ppermute | solution.py:221
  20.9 16.5 %collective-permute-start.1 = (f32[136,8,128]{2,1,0:T(8,128)S(1)}, f32[136,8,128]{2,1,0:T(8,128)S(1)}, u32[]{:S(2)}, u32[]{:S(2)}) collective-permute-start(f32[136,8,128]{2,1,0:T(8,128)S(1)} %get-tuple-element.140), channel_id=1, source_target_pairs={{8,0},{9,1},{10,2},{11,3},{12,4},{13,5},{14,6},{15,7},{16,8},{17,9... | collective-permute-start | bytes 1671176 | tf_op jit(solution)/shard_map/ppermute | solution.py:221
  24.9 15.0 %collective-permute-start.5 = (f32[4,8,8,128]{3,2,1,0:T(8,128)S(1)}, f32[4,8,8,128]{3,2,1,0:T(8,128)S(1)}, u32[]{:S(2)}, u32[]{:S(2)}) collective-permute-start(f32[4,8,8,128]{3,2,1,0:T(8,128)S(1)} %pad_maximum_fusion.1), channel_id=1, source_target_pairs={{8,0},{9,1},{10,2},{11,3},{12,4},{13,5},{14,6},{15,7},{16,8},{17,9... | collective-permute-start | bytes 393224 | tf_op jit(solution)/shard_map/ppermute | solution.py:221
  26.2 13.7 %collective-permute-start.4 = (f32[4,8,8,128]{3,2,1,0:T(8,128)S(1)}, f32[4,8,8,128]{3,2,1,0:T(8,128)S(1)}, u32[]{:S(2)}, u32[]{:S(2)}) collective-permute-start(f32[4,8,8,128]{3,2,1,0:T(8,128)S(1)} %pad_maximum_fusion), channel_id=1, source_target_pairs={{0,8},{1,9},{2,10},{3,11},{4,12},{5,13},{6,14},{7,15},{8,16},{9,17... | collective-permute-start | bytes 393224 | tf_op jit(solution)/shard_map/ppermute | solution.py:221
  43.7 9.3 %collective-permute-start.8 = (f32[128,8,128]{2,1,0:T(8,128)S(1)}, f32[128,8,128]{2,1,0:T(8,128)S(1)}, u32[]{:S(2)}, u32[]{:S(2)}) collective-permute-start(f32[128,8,128]{2,1,0:T(8,128)S(1)} %get-tuple-element.148), channel_id=1, source_target_pairs={{0,1},{1,2},{2,3},{3,4},{4,5},{5,6},{6,7},{8,9},{9,10},{10,11},{11... | collective-permute-start | bytes 1572872 | tf_op jit(solution)/shard_map/ppermute | solution.py:226
  46.2 10.8 %collective-permute-start.9 = (f32[128,8,128]{2,1,0:T(8,128)S(1)}, f32[128,8,128]{2,1,0:T(8,128)S(1)}, u32[]{:S(2)}, u32[]{:S(2)}) collective-permute-start(f32[128,8,128]{2,1,0:T(8,128)S(1)} %get-tuple-element.149), channel_id=1, source_target_pairs={{1,0},{2,1},{3,2},{4,3},{5,4},{6,5},{7,6},{9,8},{10,9},{11,10},{12... | collective-permute-start | bytes 1572872 | tf_op jit(solution)/shard_map/ppermute | solution.py:226
  48.1 14.4 %collective-permute-start.6 = (f32[128,8,128]{2,1,0:T(8,128)S(1)}, f32[128,8,128]{2,1,0:T(8,128)S(1)}, u32[]{:S(2)}, u32[]{:S(2)}) collective-permute-start(f32[128,8,128]{2,1,0:T(8,128)S(1)} %get-tuple-element.146), channel_id=1, source_target_pairs={{0,8},{1,9},{2,10},{3,11},{4,12},{5,13},{6,14},{7,15},{8,16},{9,17... | collective-permute-start | bytes 1572872 | tf_op jit(solution)/shard_map/ppermute | solution.py:221
  51.7 15.5 %collective-permute-start.7 = (f32[128,8,128]{2,1,0:T(8,128)S(1)}, f32[128,8,128]{2,1,0:T(8,128)S(1)}, u32[]{:S(2)}, u32[]{:S(2)}) collective-permute-start(f32[128,8,128]{2,1,0:T(8,128)S(1)} %get-tuple-element.147), channel_id=1, source_target_pairs={{8,0},{9,1},{10,2},{11,3},{12,4},{13,5},{14,6},{15,7},{16,8},{17,9... | collective-permute-start | bytes 1572872 | tf_op jit(solution)/shard_map/ppermute | solution.py:221
  57.0 11.6 %collective-permute-start.11 = (f32[4,8,8,128]{3,2,1,0:T(8,128)S(1)}, f32[4,8,8,128]{3,2,1,0:T(8,128)S(1)}, u32[]{:S(2)}, u32[]{:S(2)}) collective-permute-start(f32[4,8,8,128]{3,2,1,0:T(8,128)S(1)} %pad_maximum_fusion.3), channel_id=1, source_target_pairs={{8,0},{9,1},{10,2},{11,3},{12,4},{13,5},{14,6},{15,7},{16,8},{17,9... | collective-permute-start | bytes 393224 | tf_op jit(solution)/shard_map/ppermute | solution.py:221
  58.3 10.3 %collective-permute-start.10 = (f32[4,8,8,128]{3,2,1,0:T(8,128)S(1)}, f32[4,8,8,128]{3,2,1,0:T(8,128)S(1)}, u32[]{:S(2)}, u32[]{:S(2)}) collective-permute-start(f32[4,8,8,128]{3,2,1,0:T(8,128)S(1)} %pad_maximum_fusion.2), channel_id=1, source_target_pairs={{0,8},{1,9},{2,10},{3,11},{4,12},{5,13},{6,14},{7,15},{8,16},{9,17... | collective-permute-start | bytes 393224 | tf_op jit(solution)/shard_map/ppermute | solution.py:221
  86.4 36.5 %collective-permute-start.12 = (f32[128,8,128]{2,1,0:T(8,128)S(1)}, f32[128,8,128]{2,1,0:T(8,128)S(1)}, u32[]{:S(2)}, u32[]{:S(2)}) collective-permute-start(f32[128,8,128]{2,1,0:T(8,128)S(1)} %all_to_all.51.mine), channel_id=1, source_target_pairs={{0,64},{64,0},{128,192},{192,128},{256,320},{320,256},{384,448},{4... | collective-permute-start | bytes 1572872 | tf_op jit(solution)/shard_map/ppermute | solution.py:273
  151.2 31.0 %all-to-all-start.5 = ((f32[16,1,128]{2,1,0:T(1,128)}), f32[16,1,128]{2,1,0:T(1,128)S(1)}, u32[]{:S(2)}, u32[]{:S(2)}) async-start(f32[16,1,128]{2,1,0:T(1,128)} %broadcast_in_dim.34), calls=%async_computation.5 | async-start | bytes 16384 | tf_op jit(solution)/shard_map/while/body/all_to_all | solution.py:277
  200.8 15.2 %copy-start.6 = (f32[64,64]{1,0:T(8,128)}, f32[64,64]{1,0:T(8,128)S(1)}, u32[]{:S(2)}) copy-start(f32[64,64]{1,0:T(8,128)S(1)} %body.10.inverse) | copy-start | bytes 49156 | tf_op jit(solution)/shard_map/while
  203.0 12.9 %all-to-all-start.1 = ((f32[128,8,128]{2,1,0:T(8,128)}), f32[128,8,128]{2,1,0:T(8,128)S(1)}, u32[]{:S(2)}, u32[]{:S(2)}) async-start(f32[128,8,128]{2,1,0:T(8,128)} %body.11), calls=%async_computation.1 | async-start | bytes 1048576 | tf_op jit(solution)/shard_map/while/body/all_to_all | solution.py:269
  216.0 0.8 copy-start.4
  216.8 1.2 copy-start
  218.1 13.6 %copy-start.5 = (f32[128,8,128]{2,1,0:T(8,128)S(1)}, f32[128,8,128]{2,1,0:T(8,128)}, u32[]{:S(2)}) copy-start(f32[128,8,128]{2,1,0:T(8,128)} %get-tuple-element.155.early) | copy-start | bytes 1572868
Sparse Core Ops, SparseCore 0:
  123.1 93.6 all-gather.2
